TPU v7x, 32 devices: a whole 2x2x4 slice. The times are simulated.
32 devices in a mesh: gx: 4 (over y, x), gy: 4 (over z), gz: 2 (over core).
Axes of the slice: x: 2, y: 2, z: 4, core: 2. Of those that a mesh axis runs over, the one named last changes fastest.
Arguments:
- solution: float32 [3, 32, 32, 512], P(None, 'gx', 'gy', 'gz'), may hold values from -6 to 6
- residual: float32 [3, 32, 32, 512], P(None, 'gx', 'gy', 'gz'), may hold values from -6 to 6
- prev_direction: float32 [3, 32, 32, 512], P(None, 'gx', 'gy', 'gz'), may hold values from -6 to 6
- prev_image: float32 [3, 32, 32, 512], P(None, 'gx', 'gy', 'gz'), may hold values from -6 to 6
- prev_rz: float32 [], replicated, may hold values from 524288 to 2097152
- density_index: int32 [32, 32, 512], P('gx', 'gy', 'gz'), may hold values from 0 to 15
- stiffness_table: float32 [16], replicated, may hold values from 0.2 to 2
- coarse_inverse: float32 [4, 4, 48, 48], P('gx', 'gy'), may hold values from -0.05 to 5, as said below
Outputs:
- new_solution: float32 [3, 32, 32, 512], P(None, 'gx', 'gy', 'gz')
- new_residual: float32 [3, 32, 32, 512], P(None, 'gx', 'gy', 'gz')
- direction: float32 [3, 32, 32, 512], P(None, 'gx', 'gy', 'gz')
- image: float32 [3, 32, 32, 512], P(None, 'gx', 'gy', 'gz')
Inputs may be any that keep to these rules, and one draw needn't show every extreme that they name: `coarse_inverse`: each group's matrix is symmetric positive definite.
All inputs are finite; a program needn't handle non-finite values.
Results may differ from a plain program's by a relative error of at most 0.00016.
Values sent between devices are 32-bit elements; how exact they have to be, the bound alone decides.
No kernel may reach another device: no remote copies, remote signals or barrier semaphores. Data moves between devices by JAX's collectives and lax.ppermute only.
A program may use at most 128 MiB of HBM per device.

v0:
```python
import math

import jax
import jax.numpy as jnp
from jax import lax
from jax.sharding import PartitionSpec as P

COUPLING = ((1.0, 0.3, 0.3), (0.3, 1.0, 0.3), (0.3, 0.3, 1.0))
DAMPING = 0.6
MASS_SHIFT = 0.1
WEIGHT_BY_KIND = (0.0, 0.1, 0.05, 0.025)


def extended(shard, sides, width):
    for axis, dim in sides:
        count, length = (lax.axis_size(axis), shard.shape[dim])
        up = [(i, (i + 1) % count) for i in range(count - 1)]
        down = [(j, i) for i, j in up]
        last = lax.slice_in_dim(shard, length - width, length, axis=dim)
        leading = lax.slice_in_dim(shard, 0, width, axis=dim)
        before = lax.ppermute(last, axis, up)
        after = lax.ppermute(leading, axis, down)
        shard = jnp.concatenate([before, shard, after], axis=dim)
    return shard


def neighbour_list():
    listing = []
    for step_x in (-1, 0, 1):
        for step_y in (-1, 0, 1):
            for step_z in (-1, 0, 1):
                kind = abs(step_x) + abs(step_y) + abs(step_z)
                if kind > 0:
                    listing.append((step_x, step_y, step_z, 0.5 * WEIGHT_BY_KIND[kind]))
    return listing


def stencil(padded, coeff):
    size_x = padded.shape[1] - 2
    size_y = padded.shape[2] - 2
    size_z = padded.shape[3] - 2
    centre = padded[:, 1:-1, 1:-1, 1:-1]
    coeff_centre = coeff[1:-1, 1:-1, 1:-1]
    total = MASS_SHIFT * coeff_centre * centre
    for step_x, step_y, step_z, weight in neighbour_list():
        other = padded[
            :,
            1 + step_x : 1 + step_x + size_x,
            1 + step_y : 1 + step_y + size_y,
            1 + step_z : 1 + step_z + size_z,
        ]
        other_coeff = coeff[
            1 + step_x : 1 + step_x + size_x,
            1 + step_y : 1 + step_y + size_y,
            1 + step_z : 1 + step_z + size_z,
        ]
        total = total + weight * (coeff_centre + other_coeff) * (centre - other)
    return jnp.stack(
        [
            COUPLING[line][0] * total[0]
            + COUPLING[line][1] * total[1]
            + COUPLING[line][2] * total[2]
            for line in range(3)
        ]
    )


def diagonal_of(coeff):
    size_x = coeff.shape[0] - 2
    size_y = coeff.shape[1] - 2
    size_z = coeff.shape[2] - 2
    coeff_centre = coeff[1:-1, 1:-1, 1:-1]
    total = MASS_SHIFT * coeff_centre
    for step_x, step_y, step_z, weight in neighbour_list():
        other_coeff = coeff[
            1 + step_x : 1 + step_x + size_x,
            1 + step_y : 1 + step_y + size_y,
            1 + step_z : 1 + step_z + size_z,
        ]
        total = total + weight * (coeff_centre + other_coeff)
    return total


def boxed_sum(field, box_x, box_y, box_z):
    shaped = field.reshape(
        3,
        field.shape[1] // box_x,
        box_x,
        field.shape[2] // box_y,
        box_y,
        field.shape[3] // box_z,
        box_z,
    )
    return jnp.sum(shaped, axis=(2, 4, 6))


def coarsen_cells(cells):
    shaped = cells.reshape(cells.shape[0] // 2, 2, cells.shape[1] // 2, 2, cells.shape[2] // 2, 2)
    return jnp.sum(shaped, axis=(1, 3, 5)) * 0.125


def spread_up(field, box_x, box_y, box_z):
    comps, size_x, size_y, size_z = field.shape
    wide = jnp.broadcast_to(
        field[:, :, None, :, None, :, None], (comps, size_x, box_x, size_y, box_y, size_z, box_z)
    )
    return wide.reshape(comps, size_x * box_x, size_y * box_y, size_z * box_z)


def on_device(
    solution,
    residual,
    prev_direction,
    prev_image,
    prev_rz,
    density_index,
    stiffness_table,
    coarse_inverse,
):
    young = jnp.zeros(density_index.shape, jnp.float32)
    for level in range(stiffness_table.shape[0]):
        young = young + jnp.where(density_index == level, stiffness_table[level], 0.0)
    coeff_wide = extended(young, (("gx", 0), ("gy", 1), ("gz", 2)), 2)
    coeff_fine = coeff_wide[1:-1, 1:-1, 1:-1]
    diag_fine = diagonal_of(coeff_fine)
    smooth = DAMPING * residual / diag_fine
    padded = extended(smooth, (("gx", 1), ("gy", 2), ("gz", 3)), 1)
    smooth = smooth + DAMPING * (residual - stencil(padded, coeff_fine)) / diag_fine
    padded = extended(smooth, (("gx", 1), ("gy", 2), ("gz", 3)), 1)
    rest = residual - stencil(padded, coeff_fine)
    coarse_rhs = 0.5 * boxed_sum(rest, 2, 2, 2)
    coeff_mid = extended(coarsen_cells(young), (("gx", 0), ("gy", 1), ("gz", 2)), 1)
    diag_mid = diagonal_of(coeff_mid)
    middle = DAMPING * coarse_rhs / diag_mid
    mid_padded = extended(middle, (("gx", 1), ("gy", 2), ("gz", 3)), 1)
    mid_rest = coarse_rhs - stencil(mid_padded, coeff_mid)
    box_x = middle.shape[1] // 2
    box_y = middle.shape[2] // 2
    box_z = middle.shape[3] // 2
    lowest = boxed_sum(mid_rest, box_x, box_y, box_z) * (1.0 / math.sqrt(box_x * box_y * box_z))
    flat_rhs = lowest.reshape(-1)
    own_rows = flat_rhs.shape[0]
    matrix = coarse_inverse[0, 0]
    offset = lax.axis_index("gz") * own_rows
    whole_rhs = lax.all_gather(flat_rhs, "gz", axis=0, tiled=True)
    own_block = lax.dynamic_slice_in_dim(matrix, offset, own_rows, 0)
    correction = jnp.dot(own_block, whole_rhs, precision=lax.Precision.HIGHEST)
    middle = middle + spread_up(correction.reshape(3, 2, 2, 2), box_x, box_y, box_z)
    mid_padded = extended(middle, (("gx", 1), ("gy", 2), ("gz", 3)), 1)
    middle = middle + DAMPING * (coarse_rhs - stencil(mid_padded, coeff_mid)) / diag_mid
    smooth = smooth + spread_up(middle, 2, 2, 2)
    padded = extended(smooth, (("gx", 1), ("gy", 2), ("gz", 3)), 1)
    smooth = smooth + DAMPING * (residual - stencil(padded, coeff_fine)) / diag_fine
    padded = extended(smooth, (("gx", 1), ("gy", 2), ("gz", 3)), 1)
    precond = smooth + DAMPING * (residual - stencil(padded, coeff_fine)) / diag_fine
    precond_padded = extended(precond, (("gx", 1), ("gy", 2), ("gz", 3)), 1)
    operated = stencil(precond_padded, coeff_fine)
    inner_rz = lax.psum(jnp.sum(residual * precond), ("gx", "gy", "gz"))
    beta = inner_rz / prev_rz
    direction = precond + beta * prev_direction
    image = operated + beta * prev_image
    inner_pq = lax.psum(jnp.sum(direction * image), ("gx", "gy", "gz"))
    alpha = inner_rz / inner_pq
    new_solution = solution + alpha * direction
    new_residual = residual - alpha * image
    return (new_solution, new_residual, direction, image)


def solution(mesh):
    placed = (
        P(None, "gx", "gy", "gz"),
        P(None, "gx", "gy", "gz"),
        P(None, "gx", "gy", "gz"),
        P(None, "gx", "gy", "gz"),
        P(),
        P("gx", "gy", "gz"),
        P(),
        P("gx", "gy", None, None),
    )
    return jax.shard_map(
        on_device,
        mesh=mesh,
        in_specs=placed,
        out_specs=(
            P(None, "gx", "gy", "gz"),
            P(None, "gx", "gy", "gz"),
            P(None, "gx", "gy", "gz"),
            P(None, "gx", "gy", "gz"),
        ),
        check_vma=False,
    )
```

profile of v0, /device:TPU:0, one launch (start us, length us, event | category | flops | bytes accessed | tf_op | source)
XLA Modules:
  0.0 340.3 jit_solution(1543599121722692803)
XLA Ops:
  2.6 11.0 %broadcast_multiply_fusion = (f32[8,8,256]{2,1,0:T(8,128)S(1)}, f32[8,8,256]{2,1,0:T(8,128)S(1)}) fusion(f32[]{:T(128)} %bitcast.15, s32[8,8,256]{2,1,0:T(8,128)} %param.13, f32[]{:T(128)} %bitcast.14, f32[]{:T(128)} %bitcast.13, f32[]{:T(128)} %bitcast.12, f32[]{:T(128)} %bitcast.11, f32[]{:T(128)} %bitcast.10, f32[]{:T(128)} %bitcast.9, f32[]{:T(128)} %bitcast.8, ...), kind=kLoop, calls=%fused_computation.550 | loop fusion | flops 786432 | bytes 196672 | tf_op jit(solution)/shard_map/mul | solution.py:73
  15.0 5.5 %collective-permute-start = (f32[2,8,256]{2,1,0:T(8,128)S(1)}, f32[2,8,256]{2,1,0:T(8,128)S(1)}, u32[]{:S(2)}, u32[]{:S(2)}) collective-permute-start(f32[2,8,256]{2,1,0:T(8,128)S(1)} %get-tuple-element.118), channel_id=1, source_target_pairs={{0,8},{8,16},{16,24},{1,9},{9,17},{17,25},{2,10},{10,18},{18,26},{... | collective-permute-start | bytes 49160 | tf_op jit(solution)/shard_map/ppermute | solution.py:21
  20.5 5.6 %reshape.137 = f32[4,2,4,2,128,2]{5,4,3,2,1,0:T(8,128)} reshape(f32[8,8,256]{2,1,0:T(8,128)S(1)} %get-tuple-element.13) | data formatting | bytes 131072 | tf_op jit(solution)/shard_map/reshape | solution.py:98
  26.0 2.5 reduce_sum.46
  29.9 5.4 %collective-permute-start.18 = (f32[1,4,128]{2,1,0:T(4,128)S(1)}, f32[1,4,128]{2,1,0:T(4,128)S(1)}, u32[]{:S(2)}, u32[]{:S(2)}) collective-permute-start(f32[1,4,128]{2,1,0:T(4,128)S(1)} %get-tuple-element.183), channel_id=1, source_target_pairs={{0,8},{8,16},{16,24},{1,9},{9,17},{17,25},{2,10},{10,18},{18,26},{... | collective-permute-start | bytes 6152 | tf_op jit(solution)/shard_map/ppermute | solution.py:21
  38.6 4.5 %collective-permute-start.20 = (f32[6,1,128]{2,1,0:T(1,128)S(1)}, f32[6,1,128]{2,1,0:T(1,128)S(1)}, u32[]{:S(2)}, u32[]{:S(2)}) collective-permute-start(f32[6,1,128]{2,1,0:T(1,128)S(1)} %get-tuple-element.174), channel_id=1, source_target_pairs={{0,2},{2,4},{4,6},{1,3},{3,5},{5,7},{8,10},{10,12},{12,14},{9,11},... | collective-permute-start | bytes 9224 | tf_op jit(solution)/shard_map/ppermute | solution.py:21
  44.5 4.5 %collective-permute-start.2 = (f32[12,2,256]{2,1,0:T(2,128)S(1)}, f32[12,2,256]{2,1,0:T(2,128)S(1)}, u32[]{:S(2)}, u32[]{:S(2)}) collective-permute-start(f32[12,2,256]{2,1,0:T(2,128)S(1)} %get-tuple-element.112), channel_id=1, source_target_pairs={{0,2},{2,4},{4,6},{1,3},{3,5},{5,7},{8,10},{10,12},{12,14},{9,11},... | collective-permute-start | bytes 73736 | tf_op jit(solution)/shard_map/ppermute | solution.py:21
  52.0 3.0 collective-permute-start.4
  58.0 5.5 %collective-permute-start.6 = (f32[3,1,8,256]{3,2,1,0:T(8,128)S(1)}, f32[3,1,8,256]{3,2,1,0:T(8,128)S(1)}, u32[]{:S(2)}, u32[]{:S(2)}) collective-permute-start(f32[3,1,8,256]{3,2,1,0:T(8,128)S(1)} %get-tuple-element.104), channel_id=1, source_target_pairs={{0,8},{8,16},{16,24},{1,9},{9,17},{17,25},{2,10},{10,18},{18,26},{... | collective-permute-start | bytes 73736 | tf_op jit(solution)/shard_map/ppermute | solution.py:21
  64.8 3.0 collective-permute-start.22
  69.2 4.8 %collective-permute-start.8 = (f32[3,10,1,256]{3,2,1,0:T(1,128)S(1)}, f32[3,10,1,256]{3,2,1,0:T(1,128)S(1)}, u32[]{:S(2)}, u32[]{:S(2)}) collective-permute-start(f32[3,10,1,256]{3,2,1,0:T(1,128)S(1)} %get-tuple-element.79), channel_id=1, source_target_pairs={{0,2},{2,4},{4,6},{1,3},{3,5},{5,7},{8,10},{10,12},{12,14},{9,11},... | collective-permute-start | bytes 92168 | tf_op jit(solution)/shard_map/ppermute | solution.py:21
  78.6 2.0 collective-permute-done.11
  83.4 5.4 %collective-permute-start.12 = (f32[3,1,8,256]{3,2,1,0:T(8,128)S(1)}, f32[3,1,8,256]{3,2,1,0:T(8,128)S(1)}, u32[]{:S(2)}, u32[]{:S(2)}) collective-permute-start(f32[3,1,8,256]{3,2,1,0:T(8,128)S(1)} %get-tuple-element.99), channel_id=1, source_target_pairs={{0,8},{8,16},{16,24},{1,9},{9,17},{17,25},{2,10},{10,18},{18,26},{... | collective-permute-start | bytes 73736 | tf_op jit(solution)/shard_map/ppermute | solution.py:21
  91.7 4.8 %collective-permute-start.14 = (f32[3,10,1,256]{3,2,1,0:T(1,128)S(1)}, f32[3,10,1,256]{3,2,1,0:T(1,128)S(1)}, u32[]{:S(2)}, u32[]{:S(2)}) collective-permute-start(f32[3,10,1,256]{3,2,1,0:T(1,128)S(1)} %get-tuple-element.75), channel_id=1, source_target_pairs={{0,2},{2,4},{4,6},{1,3},{3,5},{5,7},{8,10},{10,12},{12,14},{9,11},... | collective-permute-start | bytes 92168 | tf_op jit(solution)/shard_map/ppermute | solution.py:21
  104.5 14.0 %reshape.136 = f32[3,4,2,4,2,128,2]{6,5,4,3,2,1,0:T(8,128)} reshape(f32[3,8,8,256]{3,2,1,0:T(8,128)S(1)} %maximum_subtract_fusion.1) | data formatting | bytes 393216 | tf_op jit(solution)/shard_map/reshape | solution.py:85
  118.5 5.5 %reduce_sum.45 = f32[3,4,4,128]{3,2,1,0:T(4,128)S(1)} reduce(f32[3,4,2,4,2,128,2]{6,5,4,3,2,1,0:T(8,128)} %reshape.136, f32[]{:T(128)} %constant.31.clone.1), dimensions={2,4,6}, to_apply=%region_0.1 | reduce | flops 43008 | bytes 221188 | tf_op jit(solution)/shard_map/reduce_sum | solution.py:94
  125.3 5.4 %collective-permute-start.24 = (f32[3,1,4,128]{3,2,1,0:T(4,128)S(1)}, f32[3,1,4,128]{3,2,1,0:T(4,128)S(1)}, u32[]{:S(2)}, u32[]{:S(2)}) collective-permute-start(f32[3,1,4,128]{3,2,1,0:T(4,128)S(1)} %get-tuple-element.164), channel_id=1, source_target_pairs={{0,8},{8,16},{16,24},{1,9},{9,17},{17,25},{2,10},{10,18},{18,26},{... | collective-permute-start | bytes 18440 | tf_op jit(solution)/shard_map/ppermute | solution.py:21
  133.4 4.8 %collective-permute-start.26 = (f32[3,6,1,128]{3,2,1,0:T(1,128)S(1)}, f32[3,6,1,128]{3,2,1,0:T(1,128)S(1)}, u32[]{:S(2)}, u32[]{:S(2)}) collective-permute-start(f32[3,6,1,128]{3,2,1,0:T(1,128)S(1)} %get-tuple-element.148), channel_id=1, source_target_pairs={{0,2},{2,4},{4,6},{1,3},{3,5},{5,7},{8,10},{10,12},{12,14},{9,11},... | collective-permute-start | bytes 27656 | tf_op jit(solution)/shard_map/ppermute | solution.py:21
  145.4 2.4 all-reduce
  150.1 5.7 %collective-permute-start.30 = (f32[3,1,4,128]{3,2,1,0:T(4,128)S(1)}, f32[3,1,4,128]{3,2,1,0:T(4,128)S(1)}, u32[]{:S(2)}, u32[]{:S(2)}) collective-permute-start(f32[3,1,4,128]{3,2,1,0:T(4,128)S(1)} %get-tuple-element.159), channel_id=1, source_target_pairs={{0,8},{8,16},{16,24},{1,9},{9,17},{17,25},{2,10},{10,18},{18,26},{... | collective-permute-start | bytes 18440 | tf_op jit(solution)/shard_map/ppermute | solution.py:21
  158.5 4.8 %collective-permute-start.32 = (f32[3,6,1,128]{3,2,1,0:T(1,128)S(1)}, f32[3,6,1,128]{3,2,1,0:T(1,128)S(1)}, u32[]{:S(2)}, u32[]{:S(2)}) collective-permute-start(f32[3,6,1,128]{3,2,1,0:T(1,128)S(1)} %get-tuple-element.144), channel_id=1, source_target_pairs={{0,2},{2,4},{4,6},{1,3},{3,5},{5,7},{8,10},{10,12},{12,14},{9,11},... | collective-permute-start | bytes 27656 | tf_op jit(solution)/shard_map/ppermute | solution.py:21
  169.8 5.3 %broadcast_in_dim.90 = f32[3,4,2,4,2,128,2]{6,5,4,3,2,1,0:T(8,128)} broadcast(f32[3,4,4,128]{3,2,1,0:T(4,128)S(1)} %divide_add_fusion), dimensions={0,1,3,5} | broadcast | bytes 221184 | tf_op jit(solution)/shard_map/broadcast_in_dim | solution.py:104
  175.0 9.8 %reshape.140 = f32[3,8,8,256]{3,2,1,0:T(8,128)S(1)} reshape(f32[3,4,2,4,2,128,2]{6,5,4,3,2,1,0:T(8,128)} %broadcast_in_dim.90) | data formatting | bytes 393216 | tf_op jit(solution)/shard_map/reshape | solution.py:107
  186.2 5.7 %collective-permute-start.36 = (f32[3,1,8,256]{3,2,1,0:T(8,128)S(1)}, f32[3,1,8,256]{3,2,1,0:T(8,128)S(1)}, u32[]{:S(2)}, u32[]{:S(2)}) collective-permute-start(f32[3,1,8,256]{3,2,1,0:T(8,128)S(1)} %get-tuple-element.94), channel_id=1, source_target_pairs={{0,8},{8,16},{16,24},{1,9},{9,17},{17,25},{2,10},{10,18},{18,26},{... | collective-permute-start | bytes 73736 | tf_op jit(solution)/shard_map/ppermute | solution.py:21
  194.8 4.8 %collective-permute-start.38 = (f32[3,10,1,256]{3,2,1,0:T(1,128)S(1)}, f32[3,10,1,256]{3,2,1,0:T(1,128)S(1)}, u32[]{:S(2)}, u32[]{:S(2)}) collective-permute-start(f32[3,10,1,256]{3,2,1,0:T(1,128)S(1)} %get-tuple-element.71), channel_id=1, source_target_pairs={{0,2},{2,4},{4,6},{1,3},{3,5},{5,7},{8,10},{10,12},{12,14},{9,11},... | collective-permute-start | bytes 92168 | tf_op jit(solution)/shard_map/ppermute | solution.py:21
  208.9 5.7 %collective-permute-start.42 = (f32[3,1,8,256]{3,2,1,0:T(8,128)S(1)}, f32[3,1,8,256]{3,2,1,0:T(8,128)S(1)}, u32[]{:S(2)}, u32[]{:S(2)}) collective-permute-start(f32[3,1,8,256]{3,2,1,0:T(8,128)S(1)} %get-tuple-element.89), channel_id=1, source_target_pairs={{0,8},{8,16},{16,24},{1,9},{9,17},{17,25},{2,10},{10,18},{18,26},{... | collective-permute-start | bytes 73736 | tf_op jit(solution)/shard_map/ppermute | solution.py:21
  217.5 4.8 %collective-permute-start.44 = (f32[3,10,1,256]{3,2,1,0:T(1,128)S(1)}, f32[3,10,1,256]{3,2,1,0:T(1,128)S(1)}, u32[]{:S(2)}, u32[]{:S(2)}) collective-permute-start(f32[3,10,1,256]{3,2,1,0:T(1,128)S(1)} %get-tuple-element.67), channel_id=1, source_target_pairs={{0,2},{2,4},{4,6},{1,3},{3,5},{5,7},{8,10},{10,12},{12,14},{9,11},... | collective-permute-start | bytes 92168 | tf_op jit(solution)/shard_map/ppermute | solution.py:21
  232.4 5.7 %collective-permute-start.48 = (f32[3,1,8,256]{3,2,1,0:T(8,128)S(1)}, f32[3,1,8,256]{3,2,1,0:T(8,128)S(1)}, u32[]{:S(2)}, u32[]{:S(2)}) collective-permute-start(f32[3,1,8,256]{3,2,1,0:T(8,128)S(1)} %get-tuple-element.84), channel_id=1, source_target_pairs={{0,8},{8,16},{16,24},{1,9},{9,17},{17,25},{2,10},{10,18},{18,26},{... | collective-permute-start | bytes 73736 | tf_op jit(solution)/shard_map/ppermute | solution.py:21
  241.0 4.8 %collective-permute-start.50 = (f32[3,10,1,256]{3,2,1,0:T(1,128)S(1)}, f32[3,10,1,256]{3,2,1,0:T(1,128)S(1)}, u32[]{:S(2)}, u32[]{:S(2)}) collective-permute-start(f32[3,10,1,256]{3,2,1,0:T(1,128)S(1)} %get-tuple-element.63), channel_id=1, source_target_pairs={{0,2},{2,4},{4,6},{1,3},{3,5},{5,7},{8,10},{10,12},{12,14},{9,11},... | collective-permute-start | bytes 92168 | tf_op jit(solution)/shard_map/ppermute | solution.py:21
  246.5 44.7 %psum.14 = f32[]{:T(128)} all-reduce(f32[]{:T(128)} %get-tuple-element.7), channel_id=1, replica_groups=mesh['gx'=4,'gy'=4,'gz'=2] {'gx','gy','gz'}, use_global_device_ids=true, to_apply=%region_4.5 | all-reduce | flops 1 | bytes 8 | tf_op jit(solution)/shard_map/psum | solution.py:158
  294.8 2.0 collective-permute-done.53
  298.9 39.2 %psum.15 = f32[]{:T(128)} all-reduce(f32[]{:T(128)} %get-tuple-element.4), channel_id=1, replica_groups=mesh['gx'=4,'gy'=4,'gz'=2] {'gx','gy','gz'}, use_global_device_ids=true, to_apply=%region_6.7 | all-reduce | flops 1 | bytes 8 | tf_op jit(solution)/shard_map/psum | solution.py:162
  (199 shorter events, 91.9 us)
Async XLA Ops:
  13.7 29.5 %collective-permute-start.1 = (f32[2,8,256]{2,1,0:T(8,128)S(1)}, f32[2,8,256]{2,1,0:T(8,128)S(1)}, u32[]{:S(2)}, u32[]{:S(2)}) collective-permute-start(f32[2,8,256]{2,1,0:T(8,128)S(1)} %get-tuple-element.119), channel_id=1, source_target_pairs={{8,0},{16,8},{24,16},{9,1},{17,9},{25,17},{10,2},{18,10},{26,18},{... | collective-permute-start | bytes 49160 | tf_op jit(solution)/shard_map/ppermute | solution.py:22
  15.0 28.2 %collective-permute-start = (f32[2,8,256]{2,1,0:T(8,128)S(1)}, f32[2,8,256]{2,1,0:T(8,128)S(1)}, u32[]{:S(2)}, u32[]{:S(2)}) collective-permute-start(f32[2,8,256]{2,1,0:T(8,128)S(1)} %get-tuple-element.118), channel_id=1, source_target_pairs={{0,8},{8,16},{16,24},{1,9},{9,17},{17,25},{2,10},{10,18},{18,26},{... | collective-permute-start | bytes 49160 | tf_op jit(solution)/shard_map/ppermute | solution.py:21
  28.6 8.7 %collective-permute-start.19 = (f32[1,4,128]{2,1,0:T(4,128)S(1)}, f32[1,4,128]{2,1,0:T(4,128)S(1)}, u32[]{:S(2)}, u32[]{:S(2)}) collective-permute-start(f32[1,4,128]{2,1,0:T(4,128)S(1)} %get-tuple-element.184), channel_id=1, source_target_pairs={{8,0},{16,8},{24,16},{9,1},{17,9},{25,17},{10,2},{18,10},{26,18},{... | collective-permute-start | bytes 6152 | tf_op jit(solution)/shard_map/ppermute | solution.py:22
  29.9 7.4 %collective-permute-start.18 = (f32[1,4,128]{2,1,0:T(4,128)S(1)}, f32[1,4,128]{2,1,0:T(4,128)S(1)}, u32[]{:S(2)}, u32[]{:S(2)}) collective-permute-start(f32[1,4,128]{2,1,0:T(4,128)S(1)} %get-tuple-element.183), channel_id=1, source_target_pairs={{0,8},{8,16},{16,24},{1,9},{9,17},{17,25},{2,10},{10,18},{18,26},{... | collective-permute-start | bytes 6152 | tf_op jit(solution)/shard_map/ppermute | solution.py:21
  37.3 11.8 %collective-permute-start.21 = (f32[6,1,128]{2,1,0:T(1,128)S(1)}, f32[6,1,128]{2,1,0:T(1,128)S(1)}, u32[]{:S(2)}, u32[]{:S(2)}) collective-permute-start(f32[6,1,128]{2,1,0:T(1,128)S(1)} %get-tuple-element.175), channel_id=1, source_target_pairs={{2,0},{4,2},{6,4},{3,1},{5,3},{7,5},{10,8},{12,10},{14,12},{11,9},... | collective-permute-start | bytes 9224 | tf_op jit(solution)/shard_map/ppermute | solution.py:22
  38.6 10.5 %collective-permute-start.20 = (f32[6,1,128]{2,1,0:T(1,128)S(1)}, f32[6,1,128]{2,1,0:T(1,128)S(1)}, u32[]{:S(2)}, u32[]{:S(2)}) collective-permute-start(f32[6,1,128]{2,1,0:T(1,128)S(1)} %get-tuple-element.174), channel_id=1, source_target_pairs={{0,2},{2,4},{4,6},{1,3},{3,5},{5,7},{8,10},{10,12},{12,14},{9,11},... | collective-permute-start | bytes 9224 | tf_op jit(solution)/shard_map/ppermute | solution.py:21
  56.7 11.2 %collective-permute-start.7 = (f32[3,1,8,256]{3,2,1,0:T(8,128)S(1)}, f32[3,1,8,256]{3,2,1,0:T(8,128)S(1)}, u32[]{:S(2)}, u32[]{:S(2)}) collective-permute-start(f32[3,1,8,256]{3,2,1,0:T(8,128)S(1)} %get-tuple-element.105), channel_id=1, source_target_pairs={{8,0},{16,8},{24,16},{9,1},{17,9},{25,17},{10,2},{18,10},{26,18},{... | collective-permute-start | bytes 73736 | tf_op jit(solution)/shard_map/ppermute | solution.py:22
  58.0 9.9 %collective-permute-start.6 = (f32[3,1,8,256]{3,2,1,0:T(8,128)S(1)}, f32[3,1,8,256]{3,2,1,0:T(8,128)S(1)}, u32[]{:S(2)}, u32[]{:S(2)}) collective-permute-start(f32[3,1,8,256]{3,2,1,0:T(8,128)S(1)} %get-tuple-element.104), channel_id=1, source_target_pairs={{0,8},{8,16},{16,24},{1,9},{9,17},{17,25},{2,10},{10,18},{18,26},{... | collective-permute-start | bytes 73736 | tf_op jit(solution)/shard_map/ppermute | solution.py:21
  63.5 25.3 %collective-permute-start.23 = (f32[6,6,1]{2,1,0:T(8,128)S(1)}, f32[6,6,1]{2,1,0:T(8,128)S(1)}, u32[]{:S(2)}, u32[]{:S(2)}) collective-permute-start(f32[6,6,1]{2,1,0:T(8,128)S(1)} %get-tuple-element.168), channel_id=1, source_target_pairs={{1,0},{3,2},{5,4},{7,6},{9,8},{11,10},{13,12},{15,14},{17,16},{19,... | collective-permute-start | bytes 440 | tf_op jit(solution)/shard_map/ppermute | solution.py:22
  64.8 24.0 %collective-permute-start.22 = (f32[6,6,1]{2,1,0:T(8,128)S(1)}, f32[6,6,1]{2,1,0:T(8,128)S(1)}, u32[]{:S(2)}, u32[]{:S(2)}) collective-permute-start(f32[6,6,1]{2,1,0:T(8,128)S(1)} %get-tuple-element.169), channel_id=1, source_target_pairs={{0,1},{2,3},{4,5},{6,7},{8,9},{10,11},{12,13},{14,15},{16,17},{18,... | collective-permute-start | bytes 440 | tf_op jit(solution)/shard_map/ppermute | solution.py:21
  69.2 6.4 %collective-permute-start.8 = (f32[3,10,1,256]{3,2,1,0:T(1,128)S(1)}, f32[3,10,1,256]{3,2,1,0:T(1,128)S(1)}, u32[]{:S(2)}, u32[]{:S(2)}) collective-permute-start(f32[3,10,1,256]{3,2,1,0:T(1,128)S(1)} %get-tuple-element.79), channel_id=1, source_target_pairs={{0,2},{2,4},{4,6},{1,3},{3,5},{5,7},{8,10},{10,12},{12,14},{9,11},... | collective-permute-start | bytes 92168 | tf_op jit(solution)/shard_map/ppermute | solution.py:21
  82.1 6.9 %collective-permute-start.13 = (f32[3,1,8,256]{3,2,1,0:T(8,128)S(1)}, f32[3,1,8,256]{3,2,1,0:T(8,128)S(1)}, u32[]{:S(2)}, u32[]{:S(2)}) collective-permute-start(f32[3,1,8,256]{3,2,1,0:T(8,128)S(1)} %get-tuple-element.100), channel_id=1, source_target_pairs={{8,0},{16,8},{24,16},{9,1},{17,9},{25,17},{10,2},{18,10},{26,18},{... | collective-permute-start | bytes 73736 | tf_op jit(solution)/shard_map/ppermute | solution.py:22
  83.4 7.0 %collective-permute-start.12 = (f32[3,1,8,256]{3,2,1,0:T(8,128)S(1)}, f32[3,1,8,256]{3,2,1,0:T(8,128)S(1)}, u32[]{:S(2)}, u32[]{:S(2)}) collective-permute-start(f32[3,1,8,256]{3,2,1,0:T(8,128)S(1)} %get-tuple-element.99), channel_id=1, source_target_pairs={{0,8},{8,16},{16,24},{1,9},{9,17},{17,25},{2,10},{10,18},{18,26},{... | collective-permute-start | bytes 73736 | tf_op jit(solution)/shard_map/ppermute | solution.py:21
  90.4 6.3 %collective-permute-start.15 = (f32[3,10,1,256]{3,2,1,0:T(1,128)S(1)}, f32[3,10,1,256]{3,2,1,0:T(1,128)S(1)}, u32[]{:S(2)}, u32[]{:S(2)}) collective-permute-start(f32[3,10,1,256]{3,2,1,0:T(1,128)S(1)} %get-tuple-element.76), channel_id=1, source_target_pairs={{2,0},{4,2},{6,4},{3,1},{5,3},{7,5},{10,8},{12,10},{14,12},{11,9},... | collective-permute-start | bytes 92168 | tf_op jit(solution)/shard_map/ppermute | solution.py:22
  91.7 6.4 %collective-permute-start.14 = (f32[3,10,1,256]{3,2,1,0:T(1,128)S(1)}, f32[3,10,1,256]{3,2,1,0:T(1,128)S(1)}, u32[]{:S(2)}, u32[]{:S(2)}) collective-permute-start(f32[3,10,1,256]{3,2,1,0:T(1,128)S(1)} %get-tuple-element.75), channel_id=1, source_target_pairs={{0,2},{2,4},{4,6},{1,3},{3,5},{5,7},{8,10},{10,12},{12,14},{9,11},... | collective-permute-start | bytes 92168 | tf_op jit(solution)/shard_map/ppermute | solution.py:21
  124.0 6.8 %collective-permute-start.25 = (f32[3,1,4,128]{3,2,1,0:T(4,128)S(1)}, f32[3,1,4,128]{3,2,1,0:T(4,128)S(1)}, u32[]{:S(2)}, u32[]{:S(2)}) collective-permute-start(f32[3,1,4,128]{3,2,1,0:T(4,128)S(1)} %get-tuple-element.165), channel_id=1, source_target_pairs={{8,0},{16,8},{24,16},{9,1},{17,9},{25,17},{10,2},{18,10},{26,18},{... | collective-permute-start | bytes 18440 | tf_op jit(solution)/shard_map/ppermute | solution.py:22
  125.3 6.8 %collective-permute-start.24 = (f32[3,1,4,128]{3,2,1,0:T(4,128)S(1)}, f32[3,1,4,128]{3,2,1,0:T(4,128)S(1)}, u32[]{:S(2)}, u32[]{:S(2)}) collective-permute-start(f32[3,1,4,128]{3,2,1,0:T(4,128)S(1)} %get-tuple-element.164), channel_id=1, source_target_pairs={{0,8},{8,16},{16,24},{1,9},{9,17},{17,25},{2,10},{10,18},{18,26},{... | collective-permute-start | bytes 18440 | tf_op jit(solution)/shard_map/ppermute | solution.py:21
  132.1 6.4 %collective-permute-start.27 = (f32[3,6,1,128]{3,2,1,0:T(1,128)S(1)}, f32[3,6,1,128]{3,2,1,0:T(1,128)S(1)}, u32[]{:S(2)}, u32[]{:S(2)}) collective-permute-start(f32[3,6,1,128]{3,2,1,0:T(1,128)S(1)} %get-tuple-element.149), channel_id=1, source_target_pairs={{2,0},{4,2},{6,4},{3,1},{5,3},{7,5},{10,8},{12,10},{14,12},{11,9},... | collective-permute-start | bytes 27656 | tf_op jit(solution)/shard_map/ppermute | solution.py:22
  133.4 6.2 %collective-permute-start.26 = (f32[3,6,1,128]{3,2,1,0:T(1,128)S(1)}, f32[3,6,1,128]{3,2,1,0:T(1,128)S(1)}, u32[]{:S(2)}, u32[]{:S(2)}) collective-permute-start(f32[3,6,1,128]{3,2,1,0:T(1,128)S(1)} %get-tuple-element.148), channel_id=1, source_target_pairs={{0,2},{2,4},{4,6},{1,3},{3,5},{5,7},{8,10},{10,12},{12,14},{9,11},... | collective-permute-start | bytes 27656 | tf_op jit(solution)/shard_map/ppermute | solution.py:21
  148.8 7.0 %collective-permute-start.31 = (f32[3,1,4,128]{3,2,1,0:T(4,128)S(1)}, f32[3,1,4,128]{3,2,1,0:T(4,128)S(1)}, u32[]{:S(2)}, u32[]{:S(2)}) collective-permute-start(f32[3,1,4,128]{3,2,1,0:T(4,128)S(1)} %get-tuple-element.160), channel_id=1, source_target_pairs={{8,0},{16,8},{24,16},{9,1},{17,9},{25,17},{10,2},{18,10},{26,18},{... | collective-permute-start | bytes 18440 | tf_op jit(solution)/shard_map/ppermute | solution.py:22
  150.1 7.1 %collective-permute-start.30 = (f32[3,1,4,128]{3,2,1,0:T(4,128)S(1)}, f32[3,1,4,128]{3,2,1,0:T(4,128)S(1)}, u32[]{:S(2)}, u32[]{:S(2)}) collective-permute-start(f32[3,1,4,128]{3,2,1,0:T(4,128)S(1)} %get-tuple-element.159), channel_id=1, source_target_pairs={{0,8},{8,16},{16,24},{1,9},{9,17},{17,25},{2,10},{10,18},{18,26},{... | collective-permute-start | bytes 18440 | tf_op jit(solution)/shard_map/ppermute | solution.py:21
  158.5 6.2 %collective-permute-start.32 = (f32[3,6,1,128]{3,2,1,0:T(1,128)S(1)}, f32[3,6,1,128]{3,2,1,0:T(1,128)S(1)}, u32[]{:S(2)}, u32[]{:S(2)}) collective-permute-start(f32[3,6,1,128]{3,2,1,0:T(1,128)S(1)} %get-tuple-element.144), channel_id=1, source_target_pairs={{0,2},{2,4},{4,6},{1,3},{3,5},{5,7},{8,10},{10,12},{12,14},{9,11},... | collective-permute-start | bytes 27656 | tf_op jit(solution)/shard_map/ppermute | solution.py:21
  184.9 7.0 %collective-permute-start.37 = (f32[3,1,8,256]{3,2,1,0:T(8,128)S(1)}, f32[3,1,8,256]{3,2,1,0:T(8,128)S(1)}, u32[]{:S(2)}, u32[]{:S(2)}) collective-permute-start(f32[3,1,8,256]{3,2,1,0:T(8,128)S(1)} %get-tuple-element.95), channel_id=1, source_target_pairs={{8,0},{16,8},{24,16},{9,1},{17,9},{25,17},{10,2},{18,10},{26,18},{... | collective-permute-start | bytes 73736 | tf_op jit(solution)/shard_map/ppermute | solution.py:22
  186.2 7.2 %collective-permute-start.36 = (f32[3,1,8,256]{3,2,1,0:T(8,128)S(1)}, f32[3,1,8,256]{3,2,1,0:T(8,128)S(1)}, u32[]{:S(2)}, u32[]{:S(2)}) collective-permute-start(f32[3,1,8,256]{3,2,1,0:T(8,128)S(1)} %get-tuple-element.94), channel_id=1, source_target_pairs={{0,8},{8,16},{16,24},{1,9},{9,17},{17,25},{2,10},{10,18},{18,26},{... | collective-permute-start | bytes 73736 | tf_op jit(solution)/shard_map/ppermute | solution.py:21
  194.8 6.4 %collective-permute-start.38 = (f32[3,10,1,256]{3,2,1,0:T(1,128)S(1)}, f32[3,10,1,256]{3,2,1,0:T(1,128)S(1)}, u32[]{:S(2)}, u32[]{:S(2)}) collective-permute-start(f32[3,10,1,256]{3,2,1,0:T(1,128)S(1)} %get-tuple-element.71), channel_id=1, source_target_pairs={{0,2},{2,4},{4,6},{1,3},{3,5},{5,7},{8,10},{10,12},{12,14},{9,11},... | collective-permute-start | bytes 92168 | tf_op jit(solution)/shard_map/ppermute | solution.py:21
  207.6 7.0 %collective-permute-start.43 = (f32[3,1,8,256]{3,2,1,0:T(8,128)S(1)}, f32[3,1,8,256]{3,2,1,0:T(8,128)S(1)}, u32[]{:S(2)}, u32[]{:S(2)}) collective-permute-start(f32[3,1,8,256]{3,2,1,0:T(8,128)S(1)} %get-tuple-element.90), channel_id=1, source_target_pairs={{8,0},{16,8},{24,16},{9,1},{17,9},{25,17},{10,2},{18,10},{26,18},{... | collective-permute-start | bytes 73736 | tf_op jit(solution)/shard_map/ppermute | solution.py:22
  208.9 7.2 %collective-permute-start.42 = (f32[3,1,8,256]{3,2,1,0:T(8,128)S(1)}, f32[3,1,8,256]{3,2,1,0:T(8,128)S(1)}, u32[]{:S(2)}, u32[]{:S(2)}) collective-permute-start(f32[3,1,8,256]{3,2,1,0:T(8,128)S(1)} %get-tuple-element.89), channel_id=1, source_target_pairs={{0,8},{8,16},{16,24},{1,9},{9,17},{17,25},{2,10},{10,18},{18,26},{... | collective-permute-start | bytes 73736 | tf_op jit(solution)/shard_map/ppermute | solution.py:21
  217.5 6.4 %collective-permute-start.44 = (f32[3,10,1,256]{3,2,1,0:T(1,128)S(1)}, f32[3,10,1,256]{3,2,1,0:T(1,128)S(1)}, u32[]{:S(2)}, u32[]{:S(2)}) collective-permute-start(f32[3,10,1,256]{3,2,1,0:T(1,128)S(1)} %get-tuple-element.67), channel_id=1, source_target_pairs={{0,2},{2,4},{4,6},{1,3},{3,5},{5,7},{8,10},{10,12},{12,14},{9,11},... | collective-permute-start | bytes 92168 | tf_op jit(solution)/shard_map/ppermute | solution.py:21
  231.1 7.0 %collective-permute-start.49 = (f32[3,1,8,256]{3,2,1,0:T(8,128)S(1)}, f32[3,1,8,256]{3,2,1,0:T(8,128)S(1)}, u32[]{:S(2)}, u32[]{:S(2)}) collective-permute-start(f32[3,1,8,256]{3,2,1,0:T(8,128)S(1)} %get-tuple-element.85), channel_id=1, source_target_pairs={{8,0},{16,8},{24,16},{9,1},{17,9},{25,17},{10,2},{18,10},{26,18},{... | collective-permute-start | bytes 73736 | tf_op jit(solution)/shard_map/ppermute | solution.py:22
  232.4 7.2 %collective-permute-start.48 = (f32[3,1,8,256]{3,2,1,0:T(8,128)S(1)}, f32[3,1,8,256]{3,2,1,0:T(8,128)S(1)}, u32[]{:S(2)}, u32[]{:S(2)}) collective-permute-start(f32[3,1,8,256]{3,2,1,0:T(8,128)S(1)} %get-tuple-element.84), channel_id=1, source_target_pairs={{0,8},{8,16},{16,24},{1,9},{9,17},{17,25},{2,10},{10,18},{18,26},{... | collective-permute-start | bytes 73736 | tf_op jit(solution)/shard_map/ppermute | solution.py:21
  239.7 52.1 %collective-permute-start.51 = (f32[3,10,1,256]{3,2,1,0:T(1,128)S(1)}, f32[3,10,1,256]{3,2,1,0:T(1,128)S(1)}, u32[]{:S(2)}, u32[]{:S(2)}) collective-permute-start(f32[3,10,1,256]{3,2,1,0:T(1,128)S(1)} %get-tuple-element.64), channel_id=1, source_target_pairs={{2,0},{4,2},{6,4},{3,1},{5,3},{7,5},{10,8},{12,10},{14,12},{11,9},... | collective-permute-start | bytes 92168 | tf_op jit(solution)/shard_map/ppermute | solution.py:22
  241.0 50.8 %collective-permute-start.50 = (f32[3,10,1,256]{3,2,1,0:T(1,128)S(1)}, f32[3,10,1,256]{3,2,1,0:T(1,128)S(1)}, u32[]{:S(2)}, u32[]{:S(2)}) collective-permute-start(f32[3,10,1,256]{3,2,1,0:T(1,128)S(1)} %get-tuple-element.63), channel_id=1, source_target_pairs={{0,2},{2,4},{4,6},{1,3},{3,5},{5,7},{8,10},{10,12},{12,14},{9,11},... | collective-permute-start | bytes 92168 | tf_op jit(solution)/shard_map/ppermute | solution.py:21
  (29 other events, 521.6 us)
where the time goes:
time: 342 us; the launch traced here: 340 us
  starting transfers between devices  143 us (42%)
  blocking collectives  86.3 us (25%)
  local copies, waits for them, and re-layouts  39.8 us (12%)
  waiting for transfers between devices  32.6 us (10%)
  other arithmetic  32.1 us (9%)
  between operations  5.2 us (2%)
    ppermute x27, starting transfers between devices, extended(): before = lax.ppermute(last, axis, up)  108 us
    psum x1, blocking collectives, on_device(): inner_rz = lax.psum(jnp.sum(residual * precond), ('gx', 'gy', 'gz'))  44.7 us
    psum x1, blocking collectives, on_device(): inner_pq = lax.psum(jnp.sum(direction * image), ('gx', 'gy', 'gz'))  39.2 us
    ppermute x27, starting transfers between devices, extended(): after = lax.ppermute(leading, axis, down)  35 us
    ppermute x27, waiting for transfers between devices, extended(): before = lax.ppermute(last, axis, up)  19.3 us
    reshape x1, local copies, waits for them, and re-layouts, boxed_sum(): field.reshape(3, field.shape[1] // box_x, box_x, field.shape[2] // box_y,...  14 us
    ppermute x27, waiting for transfers between devices, extended(): after = lax.ppermute(leading, axis, down)  13.3 us
    mul x1, other arithmetic, diagonal_of(): total = MASS_SHIFT * coeff_centre  11 us
  transfers between devices with their start and end apart: 54, of which 21 were waited for; matrix products, arithmetic and copies ran while one was open for 4% of the time, Pallas kernels for 0%

commit v1 on v0

v1 whole, which is shorter than its diff:
```python
import functools
import math

import jax
import jax.numpy as jnp
from jax import lax
from jax.experimental import pallas as pl
from jax.experimental.pallas import tpu as pltpu
from jax.sharding import PartitionSpec as P

X, Y, Z = 8, 8, 256
COMPS = 3
RIM = 4
WIDE = 6
ROWS = Y + 2 * RIM
LANES = Z + 128
MID_LANES = Z // 2 + 128
DAMPING = 0.6
ALL = ("gx", "gy", "gz")
F32 = jnp.float32
VMEM = pl.BlockSpec(memory_space=pltpu.VMEM)
SMEM = pl.BlockSpec(memory_space=pltpu.SMEM)


def shape(*dims):
    return jax.ShapeDtypeStruct(dims, F32)


def call(body, outs, scratch=(), n_in=0, smem=(), mib=16, flops=1000000):
    return pl.pallas_call(
        body,
        out_shape=outs,
        in_specs=[SMEM if i in smem else VMEM for i in range(n_in)],
        out_specs=[VMEM] * len(outs),
        scratch_shapes=list(scratch),
        compiler_params=pltpu.CompilerParams(vmem_limit_bytes=mib * 1024 * 1024),
    )


def pairs(count, odd):
    if odd:
        return [(i, (i + 1) % count if i % 2 else (i - 1) % count) for i in range(count)]
    return [(i, i ^ 1) for i in range(count)]


def swap(axis, even_pack, odd_pack):
    count = lax.axis_size(axis)
    got_even = lax.ppermute(even_pack, axis, pairs(count, False))
    if count == 2:
        return [got_even]
    return [got_even, lax.ppermute(odd_pack, axis, pairs(count, True))]


def is_even(axis):
    return lax.rem(lax.axis_index(axis), 2) == 0


def inner(axis):
    index = lax.axis_index(axis)
    return jnp.logical_and(index > 0, index < lax.axis_size(axis) - 1)


def from_sides(got, axis):
    even = is_even(axis)
    if len(got) == 1:

        def lower(key):
            value = got[0][key]
            return jnp.where(even, 0.0, value)

        def upper(key):
            value = got[0][key]
            return jnp.where(even, value, 0.0)

        return lower, upper
    ok = inner(axis)

    def lower(key):
        return jnp.where(even, jnp.where(ok, got[1][key], 0.0), got[0][key])

    def upper(key):
        return jnp.where(even, got[0][key], jnp.where(ok, got[1][key], 0.0))

    return lower, upper


def tri_yz(a):
    rows, lanes = a.shape
    a = a + pltpu.roll(a, 1, 0)
    a = a + pltpu.roll(a, rows - 1, 0)
    a = a + pltpu.roll(a, 1, 1)
    return a + pltpu.roll(a, lanes - 1, 1)


def tri_x(before, centre, after):
    return before + after + (centre + centre)


def coupled(parts):
    total = 0.3 * (parts[0] + parts[1] + parts[2])
    return [0.7 * part + total for part in parts]


def row_of(shape):
    return lax.broadcasted_iota(jnp.int32, shape, 0)


def lane_of(shape):
    return lax.broadcasted_iota(jnp.int32, shape, 1)


def up(a, shift):
    shift %= a.shape[0]
    return pltpu.roll(a, shift, 0) if shift else a


def pool_matrix(value):
    lane = row_of((LANES, MID_LANES))
    mid = jnp.where(lane < Z + 64, lane // 2, lane // 2 + 64)
    return jnp.where(mid == lane_of((LANES, MID_LANES)), value, 0.0).astype(F32)


def spread_matrix():
    lane = lane_of((MID_LANES, LANES))
    mid = jnp.where(lane < Z + 64, lane // 2, lane // 2 + 64)
    return jnp.where(mid == row_of((MID_LANES, LANES)), 1.0, 0.0).astype(F32)


def put_tiles(ref, at, value):
    for k in range(ref.shape[0]):
        ref[k, at : at + value.shape[0]] = value[:, 128 * k : 128 * k + 128]


def every_other(ref, at, size):
    return jnp.concatenate(
        [ref[k, pl.ds(at, size, stride=2)] for k in range(ref.shape[0])], axis=1
    )


def exact_dot(a, b):
    return jnp.dot(a, b, precision=lax.Precision.HIGHEST, preferred_element_type=F32)


X_PACK = COMPS * RIM + WIDE
R_TILES = COMPS * X
E_PLANES = X + 2 * WIDE
E4_TILES = E_PLANES // 2
E2_TILES = E_PLANES // 4
Y_PACK = R_TILES + E4_TILES + E2_TILES
Z_PACK = COMPS * (X + 2 * RIM) * ROWS + E_PLANES * 24
R_SLAB = COMPS * (X + 2 * RIM) * ROWS


def pack_x_body(table, index, res, young, pack_even, pack_odd):
    levels = index[...]
    value = jnp.zeros(levels.shape, F32)
    for level in range(table.shape[0]):
        value = jnp.where(levels == level, table[level], value)
    young[...] = value
    even = is_even("gx")
    high_first = jnp.where(even, 1, 0)
    for pack, high in ((pack_even, high_first), (pack_odd, 1 - high_first)):
        for c in range(COMPS):
            pack[c * RIM : (c + 1) * RIM] = res[c, pl.ds(high * (X - RIM), RIM)]
        pack[COMPS * RIM :] = young[pl.ds(high * (X - WIDE), WIDE)]


def x_planes(res, young, got_x, lanes=slice(None)):
    lower, upper = from_sides(got_x, "gx")
    whole = slice(None)

    def res_plane(c, i):
        if i < RIM:
            return lower((c * RIM + i, whole, lanes))
        if i < RIM + X:
            return res[c, i - RIM, :, lanes]
        return upper((c * RIM + i - RIM - X, whole, lanes))

    def young_plane(i):
        if i < WIDE:
            return lower((COMPS * RIM + i, whole, lanes))
        if i < WIDE + X:
            return young[i - WIDE, :, lanes]
        return upper((COMPS * RIM + i - WIDE - X, whole, lanes))

    return res_plane, young_plane


def pack_y_body(res, young, got_a, got_b, pack_even, pack_odd):
    res_plane, young_plane = x_planes(res, young, (got_a, got_b))
    row = row_of((Y, Z))
    even = is_even("gy")

    def put(tile, low, high):
        pack_even[tile] = jnp.where(even, high, low)
        pack_odd[tile] = jnp.where(even, low, high)

    def halves(tile, a, b):
        put(
            tile,
            jnp.where(row < 4, a, up(b, 4)),
            jnp.where(row < 4, up(a, 4), b),
        )

    for c in range(COMPS):
        for i in range(X):
            halves(c * X + i, res_plane(c, i), res_plane(c, i + X))
    planes = [young_plane(i) for i in range(E_PLANES)]
    for i in range(E4_TILES):
        halves(R_TILES + i, planes[i], planes[i + E4_TILES])
    for j in range(E2_TILES):
        low = high = None
        for k in range(4):
            plane = planes[4 * j + k]
            a, b = up(plane, 2 * k - 4), up(plane, 2 * k - 2)
            low = a if k == 0 else jnp.where(row < 2 * k, low, a)
            high = b if k == 0 else jnp.where(row < 2 * k, high, b)
        put(R_TILES + E4_TILES + j, low, high)


def xy_planes(res, young, got_x, got_y, lanes, width):
    res_plane, young_plane = x_planes(res, young, got_x, lanes)
    lower, upper = from_sides(got_y, "gy")
    row = row_of((Y, width))
    whole = slice(None)

    def res_tiles(c, i):
        own = up(res_plane(c, i), 4)
        key = (c * X + i % X, whole, lanes)
        low, high = lower(key), upper(key)
        if i < X:
            high = up(high, 4)
        else:
            low = up(low, 4)
        return [jnp.where(row < 4, low, own), jnp.where(row < 4, own, high)]

    def young_tiles(i):
        four = (R_TILES + i % E4_TILES, whole, lanes)
        two = (R_TILES + E4_TILES + i // 4, whole, lanes)
        k = i % 4
        low4, high4 = lower(four), upper(four)
        if i < E4_TILES:
            low4 = up(low4, 4)
        else:
            high4 = up(high4, 4)
        low2, high2 = up(lower(two), 2 - 2 * k), up(upper(two), 4 - 2 * k)
        low = jnp.where(row < 4, jnp.where(row < 2, 0.0, low2), low4)
        high = jnp.where(row < 4, high4, jnp.where(row < 6, high2, 0.0))
        return [low, young_plane(i), high]

    return res_tiles, young_tiles


def pack_z_body(res, young, xa, xb, ya, yb, *packs):
    high_first = jnp.where(is_even("gz"), 1, 0)
    for pack, high in zip(packs, (high_first, 1 - high_first)):
        lanes = pl.ds(pl.multiple_of(high * (Z - 128), 128), 128)
        res_tiles, young_tiles = xy_planes(res, young, (xa, xb), (ya, yb), lanes, 128)
        at = 0
        for c in range(COMPS):
            for i in range(X + 2 * RIM):
                for tile in res_tiles(c, i):
                    pack[at : at + 8] = tile
                    at += 8
        for i in range(E_PLANES):
            for tile in young_tiles(i):
                pack[at : at + 8] = tile
                at += 8


M_PLANES = X // 2 + 4
EM_PLANES = X // 2 + 6
LOW_TILE = COMPS * (X // 2)
MZ_PACK = (LOW_TILE + 1) * 8


def fine_apply(s, es, c1, e, i):
    parts = []
    for c in range(COMPS):
        tv = tri_yz(tri_x(s[c, i - 1], s[c, i], s[c, i + 1]))
        te = tri_yz(tri_x(es[c, i - 1], es[c, i], es[c, i + 1]))
        parts.append(c1[i] * s[c, i] - (e[i] * tv + te))
    return coupled(parts)


def smooth_body(n_z, *refs):
    res, young, xa, xb, ya, yb = refs[:6]
    got_z = refs[6 : 6 + n_z]
    r, s1, e, c1, w, em, c1m, wm, pack = refs[6 + n_z : 15 + n_z]
    wide, s0, es0, es1, rest, pooled, wide_x, wide_p = refs[15 + n_z :]
    lane = lane_of((8, 128))

    res_tiles, young_tiles = xy_planes(res, young, (xa, xb), (ya, yb), slice(None), Z)
    left, right = from_sides(got_z, "gz")

    def side(at):
        key = (slice(at, at + 8), slice(None))
        return jnp.where(lane < 64, right(key), left(key))

    at = 0
    for c in range(COMPS):
        for i in range(X + 2 * RIM):
            for t, tile in enumerate(res_tiles(c, i)):
                r[c, i, 8 * t : 8 * t + 8, :Z] = tile
                r[c, i, 8 * t : 8 * t + 8, Z:] = side(at)
                at += 8
    for i in range(E_PLANES):
        for t, tile in enumerate(young_tiles(i)):
            wide[i, 8 * t : 8 * t + 8, :Z] = tile * 0.0125
            wide[i, 8 * t : 8 * t + 8, Z:] = side(at) * 0.0125
            at += 8

    def prepare(i, _):
        total = tri_yz(tri_x(wide[i + 1], wide[i + 2], wide[i + 3]))[4:20]
        centre = wide[i + 2, 4:20]
        e[i] = centre
        c1[i] = 72.0 * centre + total
        inverse = jnp.where(centre > 0.0, DAMPING / (56.0 * centre + total), 0.0)
        w[i] = inverse
        for c in range(COMPS):
            value = inverse * r[c, i]
            s0[c, i] = value
            es0[c, i] = centre * value
        return _

    lax.fori_loop(0, X + 2 * RIM, prepare, 0)

    def sweep(i, _):
        applied = fine_apply(s0, es0, c1, e, i)
        for c in range(COMPS):
            value = s0[c, i] + w[i] * (r[c, i] - applied[c])
            s1[c, i] = value
            es1[c, i] = e[i] * value
        return _

    lax.fori_loop(1, X + 2 * RIM - 1, sweep, 0)

    def residue(m, _):
        first = fine_apply(s1, es1, c1, e, 2 * m + 2)
        second = fine_apply(s1, es1, c1, e, 2 * m + 3)
        for c in range(COMPS):
            total = (r[c, 2 * m + 2] - first[c]) + (r[c, 2 * m + 3] - second[c])
            rest[pl.ds((c * 6 + m) * ROWS, ROWS)] = total
        return _

    lax.fori_loop(0, 6, residue, 0)

    pool = pool_matrix(0.5)
    put_tiles(pooled, 0, exact_dot(rest[...], pool))
    for m in range(EM_PLANES):
        wide_x[24 * m : 24 * m + 24] = wide[2 * m] + wide[2 * m + 1]
    wide_p[...] = jnp.zeros(wide_p.shape, F32)
    put_tiles(wide_p, 0, exact_dot(wide_x[...], pool))
    for m in range(EM_PLANES):
        a = every_other(wide_p, 24 * m, 16) + every_other(wide_p, 24 * m + 1, 16)
        em[m] = jnp.where(row_of(a.shape) < 12, 0.25 * a, 0.0)
    for m in range(M_PLANES):
        total = tri_yz(tri_x(em[m], em[m + 1], em[m + 2]))[2:10]
        centre = em[m + 1, 2:10]
        c1m[m] = 72.0 * centre + total
        wm[m] = jnp.where(centre > 0.0, DAMPING / (56.0 * centre + total), 0.0)

    rhs, mid, e_mid = {}, {}, {}
    for m in range(6):
        centre = em[m + 2, 2:10]
        for c in range(COMPS):
            at = (c * 6 + m) * ROWS
            a = every_other(pooled, at, 8) + every_other(pooled, at + 1, 8)
            rhs[c, m] = a
            mid[c, m] = wm[m + 1] * a
            e_mid[c, m] = centre * mid[c, m]
    rows = []
    kept = {}
    for m in range(1, 5):
        parts = []
        for c in range(COMPS):
            tv = tri_yz(tri_x(mid[c, m - 1], mid[c, m], mid[c, m + 1]))
            te = tri_yz(tri_x(e_mid[c, m - 1], e_mid[c, m], e_mid[c, m + 1]))
            parts.append(c1m[m + 1] * mid[c, m] - (em[m + 2, 2:10] * tv + te))
        applied = coupled(parts)
        for c in range(COMPS):
            left_over = rhs[c, m] - applied[c]
            kept[c, m - 1] = left_over
            value = mid[c, m] + wm[m + 1] * left_over
            tile = c * 4 + m - 1
            pack[8 * tile : 8 * tile + 8] = value[:, :128]
    for c in range(COMPS):
        for b in range(2):
            rows.append(kept[c, 2 * b] + kept[c, 2 * b + 1])
    stacked = jnp.concatenate(rows, axis=0)
    lane_box = row_of((MID_LANES, 128))
    column = lane_of((MID_LANES, 128))
    boxes = jnp.where(
        jnp.logical_and(lane_box < Z // 2, lane_box // 64 == column % 2), 1.0, 0.0
    ).astype(F32)
    sums = exact_dot(stacked, boxes)
    line = row_of((48, 128))
    entry = lane_of((48, 128))
    inside = line % 8
    match = (line // 8) * 2 + (inside - 2) // 2 == entry // 2
    match = jnp.logical_and(match, jnp.logical_and(inside >= 2, inside < 6))
    scale = 1.0 / math.sqrt((X // 4) * (Y // 4) * (Z // 4))
    low = jnp.sum(jnp.where(match, sums, 0.0), axis=0, keepdims=True) * scale
    pack[8 * LOW_TILE :] = jnp.broadcast_to(low, (8, 128))


def coarse_body(n_z, *refs):
    pack = refs[0]
    got_z = refs[1 : 1 + n_z]
    rhs, matrix = refs[1 + n_z : 3 + n_z]
    planes, column, pack_even, pack_odd, scratch = refs[3 + n_z :]
    place = lax.axis_index("gz")
    count = lax.axis_size("gz")
    left, right = from_sides(got_z, "gz")
    lane = lane_of((8, 128))
    for t in range(LOW_TILE):
        key = (slice(8 * t, 8 * t + 8), slice(None))
        planes[t, :, :128] = pack[key]
        planes[t, :, 128:] = jnp.where(lane < 64, right(key), left(key))

    solved = jnp.sum(matrix[...] * rhs[...], axis=1, keepdims=True)
    size = 24
    scratch[...] = jnp.zeros(scratch.shape, F32)
    scratch[size : size + matrix.shape[0]] = jnp.broadcast_to(solved, (matrix.shape[0], 128))
    base = pl.multiple_of(place * size, 8)
    wide = lane_of((16, MID_LANES))
    before, own_a, own_b, after = [
        jnp.concatenate([scratch[pl.ds(base + at, 16, stride=2)]] * 2, axis=1)
        for at in (1, size, size + 1, 2 * size)
    ]
    value = jnp.where(wide < 64, own_a, own_b)
    value = jnp.where(wide < 128, value, jnp.where(wide < 192, after, before))
    value = jnp.where(row_of((16, MID_LANES)) < 12, value, 0.0)
    column[...] = value

    even = is_even("gx")
    row = row_of((8, MID_LANES))
    for c in range(COMPS):
        tiles = [
            jnp.where(row < 4, up(planes[c * 4 + p], -2), up(planes[c * 4 + p + 1], 2))
            for p in (0, 2)
        ]
        pack_even[8 * c : 8 * c + 8] = jnp.where(even, tiles[1], tiles[0])
        pack_odd[8 * c : 8 * c + 8] = jnp.where(even, tiles[0], tiles[1])
    pack_even[24:] = value
    pack_odd[24:] = value


MX_PACK = 24 + 16
MY_PACK = 48 + 40


def mid_y_body(planes, column, got_a, got_b, wide_planes, columns, pack_even, pack_odd):
    lower, upper = from_sides((got_a, got_b), "gx")
    whole = slice(None)
    row = row_of((8, MID_LANES))
    even = is_even("gy")
    for c in range(COMPS):
        key = (slice(8 * c, 8 * c + 8), whole)
        low, high = lower(key), upper(key)
        tiles = [up(low, 2), up(low, -2)]
        tiles += [planes[c * 4 + p] for p in range(4)]
        tiles += [up(high, 2), up(high, -2)]
        for t in range(8):
            wide_planes[c * 8 + t] = tiles[t]
        for h in range(2):
            below = above = None
            for k in range(4):
                tile = tiles[4 * h + k]
                a, b = up(tile, 2 * k - 2), up(tile, 2 * k - 4)
                below = a if k == 0 else jnp.where(row < 2 * k, below, a)
                above = b if k == 0 else jnp.where(row < 2 * k, above, b)
            at = (c * 2 + h) * 8
            pack_even[at : at + 8] = jnp.where(even, above, below)
            pack_odd[at : at + 8] = jnp.where(even, below, above)
    columns[:12] = lower((slice(24, 36), whole))
    columns[12:24] = column[:12]
    columns[24:36] = upper((slice(24, 36), whole))
    columns[36:] = jnp.zeros((4, MID_LANES), F32)
    pack_even[48:] = columns[...]
    pack_odd[48:] = columns[...]


def finish_body(
    wide_planes, columns, got_a, got_b, r, s1, e, c1, w, em, c1m, wm, prev_d, prev_i,
    precond, operated, sums, cor, mid, big, s2, es2, s3, es3, p, ep,
):
    lower, upper = from_sides((got_a, got_b), "gy")
    whole = slice(None)
    row = row_of((8, MID_LANES))
    line = row_of((16, MID_LANES))

    below = lower((slice(48, 88), whole))
    above = upper((slice(48, 88), whole))
    middle = columns[...]
    for c in range(COMPS):
        for b in range(6):
            at = (b // 2) * 12 + c * 4 + (b % 2) * 2
            bands = [source[at + by : at + by + 1] for source in (below, middle, above) for by in range(2)]
            field = jnp.zeros((16, MID_LANES), F32)
            for t, band in enumerate(bands):
                inside = jnp.logical_and(line >= 2 * t, line < 2 * t + 2)
                field = jnp.where(inside, jnp.broadcast_to(band, (16, MID_LANES)), field)
            cor[c, b] = field

    def box(m):
        return (m + 1) // 2

    for m in range(M_PLANES):
        parts = []
        for c in range(COMPS):
            near = [cor[c, box(m + k)] for k in range(3)]
            tv = tri_yz(tri_x(*near))
            te = tri_yz(tri_x(*[em[m + k] * near[k] for k in range(3)]))
            part = em[m + 1] * tv + te
            parts.append(c1m[m] * near[1][2:10] - part[2:10])
        applied = coupled(parts)
        for c in range(COMPS):
            tile = wide_planes[c * 8 + m]
            at = ((c * 2 + m // 4) * 8, (c * 2 + m // 4) * 8 + 8)
            key = (slice(*at), whole)
            k = m % 4
            tile = jnp.where(row < 2, up(lower(key), -2 * k), tile)
            tile = jnp.where(row < 6, tile, up(upper(key), 6 - 2 * k))
            value = tile + cor[c, box(m + 1), 2:10] - wm[m] * applied[c]
            at = (c * 8 + m) * 8
            mid[at : at + 8] = value
    spread = exact_dot(mid[...], spread_matrix())
    for t in range(COMPS * 8):
        piece = spread[8 * t : 8 * t + 8]
        for k in range(LANES // 128):
            tile = piece[:, 128 * k : 128 * k + 128]
            big[k, pl.ds(16 * t, 8, stride=2)] = tile
            big[k, pl.ds(16 * t + 1, 8, stride=2)] = tile

    def add_up(i, _):
        for c in range(COMPS):
            at = pl.multiple_of((c * 8 + i // 2) * 16, 16)
            more = [big[k, pl.ds(at, 16)] for k in range(LANES // 128)]
            value = s1[c, i] + jnp.concatenate(more, axis=1)
            s2[c, i] = value
            es2[c, i] = e[i] * value
        return _

    lax.fori_loop(1, X + 2 * RIM - 1, add_up, 0)

    def sweep(source, e_source, target, e_target):
        def body(i, _):
            applied = fine_apply(source, e_source, c1, e, i)
            for c in range(COMPS):
                value = source[c, i] + w[i] * (r[c, i] - applied[c])
                target[c, i] = value
                e_target[c, i] = e[i] * value
            return _

        return body

    lax.fori_loop(2, X + 2 * RIM - 2, sweep(s2, es2, s3, es3), 0)
    lax.fori_loop(3, X + 2 * RIM - 3, sweep(s3, es3, p, ep), 0)

    def image(i, carry):
        applied = fine_apply(p, ep, c1, e, i)
        x = i - RIM
        rz, pp, mix, old = carry
        for c in range(COMPS):
            own_p = p[c, i, 4:12, :Z]
            own_a = applied[c][4:12, :Z]
            precond[c, x] = own_p
            operated[c, x] = own_a
            d, q = prev_d[c, x], prev_i[c, x]
            rz += r[c, i, 4:12, :Z] * own_p
            pp += own_p * own_a
            mix += own_p * q + d * own_a
            old += d * q
        return rz, pp, mix, old

    zero = jnp.zeros((Y, Z), F32)
    found = lax.fori_loop(RIM, RIM + X, image, (zero, zero, zero, zero))
    lane = lane_of((1, 128))
    total = jnp.zeros((1, 128), F32)
    for k, value in enumerate(found):
        total = jnp.where(lane == k, jnp.sum(value), total)
    sums[...] = jnp.broadcast_to(total, sums.shape)


def last_body(prev_rz, sums, precond, operated, prev_d, prev_i, sol, res, new_s, new_r, new_d, new_i):
    total = jnp.sum(sums[...], axis=0, keepdims=True)
    lane = lane_of((1, 128))

    def entry(k):
        return jnp.sum(jnp.where(lane == k, total, 0.0), axis=1, keepdims=True)

    rz = entry(0)
    beta = rz / prev_rz[0]
    alpha = rz / (entry(1) + beta * (entry(2) + beta * entry(3)))
    beta = jnp.broadcast_to(beta, (Y, Z))
    alpha = jnp.broadcast_to(alpha, (Y, Z))
    for c in range(COMPS):
        for x in range(X):
            d = precond[c, x] + beta * prev_d[c, x]
            q = operated[c, x] + beta * prev_i[c, x]
            new_d[c, x] = d
            new_i[c, x] = q
            new_s[c, x] = sol[c, x] + alpha * d
            new_r[c, x] = res[c, x] - alpha * q


def on_device(
    solution,
    residual,
    prev_direction,
    prev_image,
    prev_rz,
    density_index,
    stiffness_table,
    coarse_inverse,
):
    if residual.shape != (COMPS, X, Y, Z):
        raise ValueError(residual.shape)
    block = shape(COMPS, X, Y, Z)
    n_z = 1 if lax.axis_size("gz") == 2 else 2
    n_all = lax.axis_size(ALL)

    young, px, qx = call(
        pack_x_body,
        [shape(X, Y, Z), shape(X_PACK, Y, Z), shape(X_PACK, Y, Z)],
        n_in=3,
        smem=(0,),
    )(stiffness_table, density_index, residual)
    got_x = swap("gx", px, qx)
    py, qy = call(pack_y_body, [shape(Y_PACK, Y, Z)] * 2, n_in=4)(residual, young, *got_x)
    got_y = swap("gy", py, qy)
    packs = call(pack_z_body, [shape(Z_PACK, 128)] * n_z, n_in=6)(residual, young, *got_x, *got_y)
    got_z = swap("gz", packs[0], packs[-1])

    planes = X + 2 * RIM
    field = (COMPS, planes, ROWS, LANES)
    r, s1, e, c1, w, em, c1m, wm, pack = call(
        functools.partial(smooth_body, n_z),
        [
            shape(*field),
            shape(*field),
            shape(planes, ROWS, LANES),
            shape(planes, ROWS, LANES),
            shape(planes, ROWS, LANES),
            shape(EM_PLANES, 16, MID_LANES),
            shape(M_PLANES, 8, MID_LANES),
            shape(M_PLANES, 8, MID_LANES),
            shape(MZ_PACK, 128),
        ],
        scratch=[
            pltpu.VMEM((E_PLANES, 24, LANES), F32),
            pltpu.VMEM(field, F32),
            pltpu.VMEM(field, F32),
            pltpu.VMEM(field, F32),
            pltpu.VMEM((18 * ROWS, LANES), F32),
            pltpu.VMEM((MID_LANES // 128, 18 * ROWS, 128), F32),
            pltpu.VMEM((24 * EM_PLANES, LANES), F32),
            pltpu.VMEM((MID_LANES // 128, 24 * EM_PLANES + 16, 128), F32),
        ],
        n_in=6 + n_z,
        mib=30,
    )(residual, young, *got_x, *got_y, *got_z)

    got_z = swap("gz", pack, pack)
    low = pack[8 * LOW_TILE, :24]
    if n_z == 1:
        other = got_z[0][8 * LOW_TILE, :24]
        first = lax.axis_index("gz") == 0
        rhs = jnp.where(first, jnp.concatenate([low, other]), jnp.concatenate([other, low]))
    else:
        rhs = lax.all_gather(low, "gz", axis=0, tiled=True)
    size = rhs.shape[0]
    mid_planes, column, px, qx = call(
        functools.partial(coarse_body, n_z),
        [
            shape(LOW_TILE, 8, MID_LANES),
            shape(16, MID_LANES),
            shape(MX_PACK, MID_LANES),
            shape(MX_PACK, MID_LANES),
        ],
        scratch=[pltpu.VMEM((size + 64, 128), F32)],
        n_in=3 + n_z,
    )(pack, *got_z, rhs.reshape(1, size), coarse_inverse.reshape(size, size))
    got_x = swap("gx", px, qx)
    mid_planes, columns, py, qy = call(
        mid_y_body,
        [
            shape(COMPS * 8, 8, MID_LANES),
            shape(40, MID_LANES),
            shape(MY_PACK, MID_LANES),
            shape(MY_PACK, MID_LANES),
        ],
        n_in=4,
    )(mid_planes, column, *got_x)
    got_y = swap("gy", py, qy)
    precond, operated, sums = call(
        finish_body,
        [block, block, shape(n_all, 128)],
        scratch=[
            pltpu.VMEM((COMPS, 6, 16, MID_LANES), F32),
            pltpu.VMEM((COMPS * 64, MID_LANES), F32),
            pltpu.VMEM((LANES // 128, COMPS * 128, 128), F32),
        ]
        + [pltpu.VMEM(field, F32)] * 6,
        n_in=14,
        mib=30,
    )(mid_planes, columns, *got_y, r, s1, e, c1, w, em, c1m, wm, prev_direction, prev_image)
    sums = lax.all_to_all(sums, ALL, 0, 0, tiled=True)
    return tuple(
        call(last_body, [block] * 4, n_in=8, smem=(0,))(
            prev_rz.reshape(1), sums, precond, operated, prev_direction, prev_image, solution, residual
        )
    )


def solution(mesh):
    field = P(None, "gx", "gy", "gz")
    return jax.shard_map(
        on_device,
        mesh=mesh,
        in_specs=(
            field,
            field,
            field,
            field,
            P(),
            P("gx", "gy", "gz"),
            P(),
            P("gx", "gy", None, None),
        ),
        out_specs=(field, field, field, field),
        check_vma=False,
    )
```

time: 342 us -> 92.1 us (0.27)
  starting transfers between devices: 143 us -> 17.3 us
  blocking collectives: 86.3 us -> 0 us
  other arithmetic: 32.1 us -> 0.08 us
  local copies, waits for them, and re-layouts: 39.8 us -> 14.6 us
  Pallas kernels: 0 us -> 20.6 us
  waiting for transfers between devices: 32.6 us -> 37.6 us
  between operations: 5.2 us -> 1.39 us
    ppermute x54 -> x10, starting transfers between devices: 143 us -> 14.3 us  [the longest x4 7.24 us: swap(): return [got_even, lax.ppermute(odd_pack, axis, pairs(count, True))]]
    psum x2 -> x0, blocking collectives: 83.9 us -> none  [the longest x1 44.7 us: on_device(): inner_rz = lax.psum(jnp.sum(residual * precond), ('gx', 'gy', 'gz'))]
    reshape x4 -> x0, local copies, waits for them, and re-layouts: 29.5 us -> none  [the longest x1 14 us: boxed_sum(): field.reshape(3, field.shape[1] // box_x, box_x, field.shape[2] // box_y,...]
    pallas_call x0 -> x8, Pallas kernels: none -> 20.6 us  [the longest x1 10.1 us: on_device(): call(functools.partial(smooth_body, n_z), [shape(*field), shape(*field),...]
    unnamed x17 -> x46, local copies, waits for them, and re-layouts: 1.53 us -> 14.6 us
    mul x6 -> x0, other arithmetic: 11.2 us -> none  [the longest x1 11 us: diagonal_of(): total = MASS_SHIFT * coeff_centre]
    reduce_sum x5 -> x0, other arithmetic: 9.53 us -> none  [the longest x2 5.64 us: boxed_sum(): return jnp.sum(shaped, axis=(2, 4, 6))]
    all_to_all x0 -> x1, waiting for transfers between devices: none -> 6.42 us  [on_device(): sums = lax.all_to_all(sums, ALL, 0, 0, tiled=True)]
  transfers between devices with their start and end apart: 54 -> 11, of which waited for: 21 -> 11; matrix products, arithmetic and copies ran while one was open for 4% -> 0% of each run, Pallas kernels for 0% -> 0%
where the time goes in v1:
time: 92.1 us; the launch traced here: 91.6 us
  waiting for transfers between devices  37.6 us (41%)
  Pallas kernels  20.6 us (22%)
  starting transfers between devices  17.3 us (19%)
  local copies, waits for them, and re-layouts  14.6 us (16%)
  between operations  1.39 us (2%)
    ppermute x6, waiting for transfers between devices, swap(): got_even = lax.ppermute(even_pack, axis, pairs(count, False))  15.9 us
    ppermute x4, waiting for transfers between devices, swap(): return [got_even, lax.ppermute(odd_pack, axis, pairs(count, True))]  15.3 us
    unnamed x46, local copies, waits for them, and re-layouts  14.6 us
    pallas_call x1, Pallas kernels, on_device(): call(functools.partial(smooth_body, n_z), [shape(*field), shape(*field),...  10.1 us
    pallas_call x1, Pallas kernels, on_device(): call(finish_body, [block, block, shape(n_all, 128)], scratch=[pltpu.VMEM(...  8.62 us
    ppermute x4, starting transfers between devices, swap(): return [got_even, lax.ppermute(odd_pack, axis, pairs(count, True))]  7.24 us
    ppermute x6, starting transfers between devices, swap(): got_even = lax.ppermute(even_pack, axis, pairs(count, False))  7.05 us
    all_to_all x1, waiting for transfers between devices, on_device(): sums = lax.all_to_all(sums, ALL, 0, 0, tiled=True)  6.42 us
  transfers between devices with their start and end apart: 11, of which 11 were waited for; matrix products, arithmetic and copies ran while one was open for 0% of the time, Pallas kernels for 0%

profile of v1, /device:TPU:0, one launch (start us, length us, event | category | flops | bytes accessed | tf_op | source)
XLA Modules:
  0.0 91.6 jit_solution(3037058341505625342)
XLA Ops:
  0.6 0.9 %copy-done = f32[3,8,8,256]{3,2,1,0:T(8,128)S(1)} copy-done((f32[3,8,8,256]{3,2,1,0:T(8,128)S(1)}, f32[3,8,8,256]{3,2,1,0:T(8,128)}, u32[]{:S(2)}) %copy-start) | copy-done | bytes 196632
  1.6 0.8 copy-done.20
  3.7 3.0 %collective-permute-start = (f32[18,8,256]{2,1,0:T(8,128)S(1)}, f32[18,8,256]{2,1,0:T(8,128)S(1)}, u32[]{:S(2)}, u32[]{:S(2)}) collective-permute-start(f32[18,8,256]{2,1,0:T(8,128)S(1)} %get-tuple-element.30), channel_id=1, source_target_pairs={{0,8},{8,0},{16,24},{24,16},{1,9},{9,1},{17,25},{25,17},{2,10},{10... | collective-permute-start | bytes 442376 | tf_op jit(solution)/shard_map/ppermute | solution.py:48
  6.7 1.5 %collective-permute-start.1 = (f32[18,8,256]{2,1,0:T(8,128)S(1)}, f32[18,8,256]{2,1,0:T(8,128)S(1)}, u32[]{:S(2)}, u32[]{:S(2)}) collective-permute-start(f32[18,8,256]{2,1,0:T(8,128)S(1)} %get-tuple-element.31), channel_id=1, source_target_pairs={{0,24},{8,16},{16,8},{24,0},{1,25},{9,17},{17,9},{25,1},{2,26},{10... | collective-permute-start | bytes 442376 | tf_op jit(solution)/shard_map/ppermute | solution.py:51
  8.2 3.0 %collective-permute-done.got_a.xa.refs_2_ = f32[18,8,256]{2,1,0:T(8,128)S(1)} collective-permute-done((f32[18,8,256]{2,1,0:T(8,128)S(1)}, f32[18,8,256]{2,1,0:T(8,128)S(1)}, u32[]{:S(2)}, u32[]{:S(2)}) %collective-permute-start) | collective-permute-done | bytes 147488 | tf_op jit(solution)/shard_map/ppermute | solution.py:48
  11.2 3.7 %collective-permute-done.1.got_b.xb.refs_3_ = f32[18,8,256]{2,1,0:T(8,128)S(1)} collective-permute-done((f32[18,8,256]{2,1,0:T(8,128)S(1)}, f32[18,8,256]{2,1,0:T(8,128)S(1)}, u32[]{:S(2)}, u32[]{:S(2)}) %collective-permute-start.1) | collective-permute-done | bytes 147488 | tf_op jit(solution)/shard_map/ppermute | solution.py:51
  14.9 0.9 %copy-done.1 = f32[3,8,8,256]{3,2,1,0:T(8,128)S(1)} copy-done((f32[3,8,8,256]{3,2,1,0:T(8,128)S(1)}, f32[3,8,8,256]{3,2,1,0:T(8,128)}, u32[]{:S(2)}) %copy-start.1) | copy-done | bytes 196632
  15.9 1.6 %collective-permute-start.2 = (f32[39,8,256]{2,1,0:T(8,128)S(1)}, f32[39,8,256]{2,1,0:T(8,128)S(1)}, u32[]{:S(2)}, u32[]{:S(2)}) collective-permute-start(f32[39,8,256]{2,1,0:T(8,128)S(1)} %get-tuple-element.32), channel_id=1, source_target_pairs={{0,2},{2,0},{4,6},{6,4},{1,3},{3,1},{5,7},{7,5},{8,10},{10,8},{12,... | collective-permute-start | bytes 958472 | tf_op jit(solution)/shard_map/ppermute | solution.py:48
  17.6 2.5 %collective-permute-start.3 = (f32[39,8,256]{2,1,0:T(8,128)S(1)}, f32[39,8,256]{2,1,0:T(8,128)S(1)}, u32[]{:S(2)}, u32[]{:S(2)}) collective-permute-start(f32[39,8,256]{2,1,0:T(8,128)S(1)} %get-tuple-element.33), channel_id=1, source_target_pairs={{0,6},{2,4},{4,2},{6,0},{1,7},{3,5},{5,3},{7,1},{8,14},{10,12},{12... | collective-permute-start | bytes 958472 | tf_op jit(solution)/shard_map/ppermute | solution.py:51
  20.1 5.5 %collective-permute-done.2.ya.refs_4_ = f32[39,8,256]{2,1,0:T(8,128)S(1)} collective-permute-done((f32[39,8,256]{2,1,0:T(8,128)S(1)}, f32[39,8,256]{2,1,0:T(8,128)S(1)}, u32[]{:S(2)}, u32[]{:S(2)}) %collective-permute-start.2) | collective-permute-done | bytes 319520 | tf_op jit(solution)/shard_map/ppermute | solution.py:48
  25.6 7.8 %collective-permute-done.3.yb.refs_5_ = f32[39,8,256]{2,1,0:T(8,128)S(1)} collective-permute-done((f32[39,8,256]{2,1,0:T(8,128)S(1)}, f32[39,8,256]{2,1,0:T(8,128)S(1)}, u32[]{:S(2)}, u32[]{:S(2)}) %collective-permute-start.3) | collective-permute-done | bytes 319520 | tf_op jit(solution)/shard_map/ppermute | solution.py:51
  33.6 2.1 %collective-permute-done.4.refs_6_ = f32[1248,128]{1,0:T(8,128)S(1)} collective-permute-done((f32[1248,128]{1,0:T(8,128)S(1)}, f32[1248,128]{1,0:T(8,128)S(1)}, u32[]{:S(2)}, u32[]{:S(2)}) %collective-permute-start.4) | collective-permute-done | bytes 639008 | tf_op jit(solution)/shard_map/ppermute | solution.py:48
  35.6 10.1 %shard_map.114 = (f32[3,16,16,384]{3,2,1,0:T(8,128)S(1)}, f32[3,16,16,384]{3,2,1,0:T(8,128)S(1)}, f32[16,16,384]{2,1,0:T(8,128)S(1)}, f32[16,16,384]{2,1,0:T(8,1...) custom-call(f32[3,8,8,256]{3,2,1,0:T(8,128)S(1)} %copy-done.2, ...), custom_call_target="tpu_custom_call" | custom-call | tf_op jit(solution)/shard_map/pallas_call | solution.py:638
  46.5 0.8 copy-done.7
  49.3 1.1 %collective-permute-done.5.refs_1_ = f32[104,128]{1,0:T(8,128)S(1)} collective-permute-done((f32[104,128]{1,0:T(8,128)S(1)}, f32[104,128]{1,0:T(8,128)S(1)}, u32[]{:S(2)}, u32[]{:S(2)}) %collective-permute-start.5) | collective-permute-done | bytes 53280 | tf_op jit(solution)/shard_map/ppermute | solution.py:48
  50.6 1.6 %collective-permute-start.6 = (f32[40,256]{1,0:T(8,128)S(1)}, f32[40,256]{1,0:T(8,128)S(1)}, u32[]{:S(2)}, u32[]{:S(2)}) collective-permute-start(f32[40,256]{1,0:T(8,128)S(1)} %get-tuple-element.37), channel_id=1, source_target_pairs={{0,8},{8,0},{16,24},{24,16},{1,9},{9,1},{17,25},{25,17},{2,10},{10... | collective-permute-start | bytes 122888 | tf_op jit(solution)/shard_map/ppermute | solution.py:48
  52.8 2.1 %collective-permute-done.6.got_a = f32[40,256]{1,0:T(8,128)S(1)} collective-permute-done((f32[40,256]{1,0:T(8,128)S(1)}, f32[40,256]{1,0:T(8,128)S(1)}, u32[]{:S(2)}, u32[]{:S(2)}) %collective-permute-start.6) | collective-permute-done | bytes 40992 | tf_op jit(solution)/shard_map/ppermute | solution.py:48
  54.8 2.2 %collective-permute-done.7.got_b = f32[40,256]{1,0:T(8,128)S(1)} collective-permute-done((f32[40,256]{1,0:T(8,128)S(1)}, f32[40,256]{1,0:T(8,128)S(1)}, u32[]{:S(2)}, u32[]{:S(2)}) %collective-permute-start.7) | collective-permute-done | bytes 40992 | tf_op jit(solution)/shard_map/ppermute | solution.py:51
  57.7 2.6 %collective-permute-start.9 = (f32[88,256]{1,0:T(8,128)S(1)}, f32[88,256]{1,0:T(8,128)S(1)}, u32[]{:S(2)}, u32[]{:S(2)}) collective-permute-start(f32[88,256]{1,0:T(8,128)S(1)} %get-tuple-element.42), channel_id=1, source_target_pairs={{0,6},{2,4},{4,2},{6,0},{1,7},{3,5},{5,3},{7,1},{8,14},{10,12},{12... | collective-permute-start | bytes 270344 | tf_op jit(solution)/shard_map/ppermute | solution.py:51
  60.4 2.2 %collective-permute-done.8.got_a = f32[88,256]{1,0:T(8,128)S(1)} collective-permute-done((f32[88,256]{1,0:T(8,128)S(1)}, f32[88,256]{1,0:T(8,128)S(1)}, u32[]{:S(2)}, u32[]{:S(2)}) %collective-permute-start.8) | collective-permute-done | bytes 90144 | tf_op jit(solution)/shard_map/ppermute | solution.py:48
  62.6 1.5 %collective-permute-done.9.got_b = f32[88,256]{1,0:T(8,128)S(1)} collective-permute-done((f32[88,256]{1,0:T(8,128)S(1)}, f32[88,256]{1,0:T(8,128)S(1)}, u32[]{:S(2)}, u32[]{:S(2)}) %collective-permute-start.9) | collective-permute-done | bytes 90144 | tf_op jit(solution)/shard_map/ppermute | solution.py:51
  64.1 1.0 %copy-done.6 = f32[16,16,384]{2,1,0:T(8,128)S(1)} copy-done((f32[16,16,384]{2,1,0:T(8,128)S(1)}, f32[16,16,384]{2,1,0:T(8,128)}, u32[]{:S(2)}) %copy-start.6) | copy-done | bytes 393240
  65.1 1.0 %copy-done.8 = f32[16,16,384]{2,1,0:T(8,128)S(1)} copy-done((f32[16,16,384]{2,1,0:T(8,128)S(1)}, f32[16,16,384]{2,1,0:T(8,128)}, u32[]{:S(2)}) %copy-start.8) | copy-done | bytes 393240
  66.1 0.9 copy-done.15
  67.0 0.8 copy-done.17
  67.9 0.8 copy-done.19
  68.7 8.6 %shard_map.117 = (f32[3,8,8,256]{3,2,1,0:T(8,128)S(1)}, f32[3,8,8,256]{3,2,1,0:T(8,128)S(1)}, f32[32,128]{1,0:T(8,128)}) custom-call(f32[24,8,256]{2,1,0:T(8,128)S(1)} %get-tuple-element.39.wide_planes, f32[40,256]{1,0:T(8,128)S(1)} %get-tuple-element.40.columns, f32[88,256]{1,0:T(8,128)S(1)} %collective-permute-done.8.got_a, ...), custom_call_target="tpu_custom_call" | custom-call | tf_op jit(solution)/shard_map/pallas_call | solution.py:697
  78.7 3.0 %all-to-all-start = ((f32[32,1,128]{2,1,0:T(1,128)}), f32[32,1,128]{2,1,0:T(1,128)S(1)}, u32[]{:S(2)}, u32[]{:S(2)}) async-start(f32[32,1,128]{2,1,0:T(1,128)} %bitcast.3), calls=%async_computation | async-start | bytes 32768 | tf_op jit(solution)/shard_map/all_to_all | solution.py:709
  82.3 6.4 %all-to-all-done = f32[32,1,128]{2,1,0:T(1,128)S(1)} async-done(((f32[32,1,128]{2,1,0:T(1,128)}), f32[32,1,128]{2,1,0:T(1,128)S(1)}, u32[]{:S(2)}, u32[]{:S(2)}) %all-to-all-start) | async-done | bytes 16416 | tf_op jit(solution)/shard_map/all_to_all | solution.py:709
  88.8 0.9 %copy-done.11 = f32[3,8,8,256]{3,2,1,0:T(8,128)S(1)} copy-done((f32[3,8,8,256]{3,2,1,0:T(8,128)S(1)}, f32[3,8,8,256]{3,2,1,0:T(8,128)}, u32[]{:S(2)}) %copy-start.11) | copy-done | bytes 196632
  89.7 0.9 %copy-done.13 = f32[3,8,8,256]{3,2,1,0:T(8,128)S(1)} copy-done((f32[3,8,8,256]{3,2,1,0:T(8,128)S(1)}, f32[3,8,8,256]{3,2,1,0:T(8,128)}, u32[]{:S(2)}) %copy-start.13) | copy-done | bytes 196632
  90.6 1.0 %shard_map.118 = (f32[3,8,8,256]{3,2,1,0:T(8,128)}, f32[3,8,8,256]{3,2,1,0:T(8,128)}, f32[3,8,8,256]{3,2,1,0:T(8,128)}, f32[3,8,8,256]{3,2,1,0:T(8,128)}) custom-call(f32[1]{0:T(128)} %bitcast.6.prev_rz, f32[32,128]{1,0:T(8,128)S(1)} %bitcast.7, f32[3,8,8,256]{3,2,1,0:T(8,128)S(1)} %copy-done.11, f32[3,8,8,256]{3,2,1,0:T(8,128)S(1)} %copy-done.13, ...), custom_call_target="tpu_custom_call" | custom-call | tf_op jit(solution)/shard_map/pallas_call | solution.py:711
  (47 shorter events, 7.2 us)
Async XLA Ops:
  0.6 0.9 %copy-start = (f32[3,8,8,256]{3,2,1,0:T(8,128)S(1)}, f32[3,8,8,256]{3,2,1,0:T(8,128)}, u32[]{:S(2)}) copy-start(f32[3,8,8,256]{3,2,1,0:T(8,128)} %res.7) | copy-start | bytes 589828
  1.6 0.8 copy-start.20
  2.4 0.7 copy-start.22
  3.7 7.5 %collective-permute-start = (f32[18,8,256]{2,1,0:T(8,128)S(1)}, f32[18,8,256]{2,1,0:T(8,128)S(1)}, u32[]{:S(2)}, u32[]{:S(2)}) collective-permute-start(f32[18,8,256]{2,1,0:T(8,128)S(1)} %get-tuple-element.30), channel_id=1, source_target_pairs={{0,8},{8,0},{16,24},{24,16},{1,9},{9,1},{17,25},{25,17},{2,10},{10... | collective-permute-start | bytes 442376 | tf_op jit(solution)/shard_map/ppermute | solution.py:48
  6.7 8.2 %collective-permute-start.1 = (f32[18,8,256]{2,1,0:T(8,128)S(1)}, f32[18,8,256]{2,1,0:T(8,128)S(1)}, u32[]{:S(2)}, u32[]{:S(2)}) collective-permute-start(f32[18,8,256]{2,1,0:T(8,128)S(1)} %get-tuple-element.31), channel_id=1, source_target_pairs={{0,24},{8,16},{16,8},{24,0},{1,25},{9,17},{17,9},{25,1},{2,26},{10... | collective-permute-start | bytes 442376 | tf_op jit(solution)/shard_map/ppermute | solution.py:51
  14.9 0.9 %copy-start.1 = (f32[3,8,8,256]{3,2,1,0:T(8,128)S(1)}, f32[3,8,8,256]{3,2,1,0:T(8,128)}, u32[]{:S(2)}) copy-start(f32[3,8,8,256]{3,2,1,0:T(8,128)} %res.7) | copy-start | bytes 589828
  15.8 19.8 %copy-start.2 = (f32[3,8,8,256]{3,2,1,0:T(8,128)S(1)}, f32[3,8,8,256]{3,2,1,0:T(8,128)}, u32[]{:S(2)}) copy-start(f32[3,8,8,256]{3,2,1,0:T(8,128)} %res.7) | copy-start | bytes 589828
  15.9 9.6 %collective-permute-start.2 = (f32[39,8,256]{2,1,0:T(8,128)S(1)}, f32[39,8,256]{2,1,0:T(8,128)S(1)}, u32[]{:S(2)}, u32[]{:S(2)}) collective-permute-start(f32[39,8,256]{2,1,0:T(8,128)S(1)} %get-tuple-element.32), channel_id=1, source_target_pairs={{0,2},{2,0},{4,6},{6,4},{1,3},{3,1},{5,7},{7,5},{8,10},{10,8},{12,... | collective-permute-start | bytes 958472 | tf_op jit(solution)/shard_map/ppermute | solution.py:48
  17.6 15.8 %collective-permute-start.3 = (f32[39,8,256]{2,1,0:T(8,128)S(1)}, f32[39,8,256]{2,1,0:T(8,128)S(1)}, u32[]{:S(2)}, u32[]{:S(2)}) collective-permute-start(f32[39,8,256]{2,1,0:T(8,128)S(1)} %get-tuple-element.33), channel_id=1, source_target_pairs={{0,6},{2,4},{4,2},{6,0},{1,7},{3,5},{5,3},{7,1},{8,14},{10,12},{12... | collective-permute-start | bytes 958472 | tf_op jit(solution)/shard_map/ppermute | solution.py:51
  33.5 17.0 %copy-start.21 = (f32[1,1,48,48]{3,2,1,0:T(8,128)S(1)}, f32[1,1,48,48]{3,2,1,0:T(8,128)}, u32[]{:S(2)}) copy-start(f32[1,1,48,48]{3,2,1,0:T(8,128)} %param.15) | copy-start | bytes 27652
  33.5 30.6 %copy-start.3 = (f32[3,8,8,256]{3,2,1,0:T(8,128)S(1)}, f32[3,8,8,256]{3,2,1,0:T(8,128)}, u32[]{:S(2)}) copy-start(f32[3,8,8,256]{3,2,1,0:T(8,128)} %prev_d.3) | copy-start | bytes 589828
  33.5 30.6 %copy-start.4 = (f32[3,8,8,256]{3,2,1,0:T(8,128)S(1)}, f32[3,8,8,256]{3,2,1,0:T(8,128)}, u32[]{:S(2)}) copy-start(f32[3,8,8,256]{3,2,1,0:T(8,128)} %prev_i.3) | copy-start | bytes 589828
  33.5 2.1 %collective-permute-start.4 = (f32[1248,128]{1,0:T(8,128)S(1)}, f32[1248,128]{1,0:T(8,128)S(1)}, u32[]{:S(2)}, u32[]{:S(2)}) collective-permute-start(f32[1248,128]{1,0:T(8,128)S(1)} %shard_map.113), channel_id=1, source_target_pairs={{0,1},{1,0},{2,3},{3,2},{4,5},{5,4},{6,7},{7,6},{8,9},{9,8},{10,11... | collective-permute-start | bytes 1916936 | tf_op jit(solution)/shard_map/ppermute | solution.py:48
  45.7 0.8 copy-start.5
  46.5 0.8 copy-start.7
  47.2 0.7 copy-start.14
  49.2 1.2 %collective-permute-start.5 = (f32[104,128]{1,0:T(8,128)S(1)}, f32[104,128]{1,0:T(8,128)S(1)}, u32[]{:S(2)}, u32[]{:S(2)}) collective-permute-start(f32[104,128]{1,0:T(8,128)S(1)} %get-tuple-element.34.refs_0_), channel_id=1, source_target_pairs={{0,1},{1,0},{2,3},{3,2},{4,5},{5,4},{6,7},{7,6},{8,9},{9,8},{10,11... | collective-permute-start | bytes 159752 | tf_op jit(solution)/shard_map/ppermute | solution.py:48
  50.6 4.2 %collective-permute-start.6 = (f32[40,256]{1,0:T(8,128)S(1)}, f32[40,256]{1,0:T(8,128)S(1)}, u32[]{:S(2)}, u32[]{:S(2)}) collective-permute-start(f32[40,256]{1,0:T(8,128)S(1)} %get-tuple-element.37), channel_id=1, source_target_pairs={{0,8},{8,0},{16,24},{24,16},{1,9},{9,1},{17,25},{25,17},{2,10},{10... | collective-permute-start | bytes 122888 | tf_op jit(solution)/shard_map/ppermute | solution.py:48
  52.1 4.9 %collective-permute-start.7 = (f32[40,256]{1,0:T(8,128)S(1)}, f32[40,256]{1,0:T(8,128)S(1)}, u32[]{:S(2)}, u32[]{:S(2)}) collective-permute-start(f32[40,256]{1,0:T(8,128)S(1)} %get-tuple-element.38), channel_id=1, source_target_pairs={{0,24},{8,16},{16,8},{24,0},{1,25},{9,17},{17,9},{25,1},{2,26},{10... | collective-permute-start | bytes 122888 | tf_op jit(solution)/shard_map/ppermute | solution.py:51
  57.1 5.5 %collective-permute-start.8 = (f32[88,256]{1,0:T(8,128)S(1)}, f32[88,256]{1,0:T(8,128)S(1)}, u32[]{:S(2)}, u32[]{:S(2)}) collective-permute-start(f32[88,256]{1,0:T(8,128)S(1)} %get-tuple-element.41), channel_id=1, source_target_pairs={{0,2},{2,0},{4,6},{6,4},{1,3},{3,1},{5,7},{7,5},{8,10},{10,8},{12,... | collective-permute-start | bytes 270344 | tf_op jit(solution)/shard_map/ppermute | solution.py:48
  57.7 6.4 %collective-permute-start.9 = (f32[88,256]{1,0:T(8,128)S(1)}, f32[88,256]{1,0:T(8,128)S(1)}, u32[]{:S(2)}, u32[]{:S(2)}) collective-permute-start(f32[88,256]{1,0:T(8,128)S(1)} %get-tuple-element.42), channel_id=1, source_target_pairs={{0,6},{2,4},{4,2},{6,0},{1,7},{3,5},{5,3},{7,1},{8,14},{10,12},{12... | collective-permute-start | bytes 270344 | tf_op jit(solution)/shard_map/ppermute | solution.py:51
  64.1 1.0 %copy-start.6 = (f32[16,16,384]{2,1,0:T(8,128)S(1)}, f32[16,16,384]{2,1,0:T(8,128)}, u32[]{:S(2)}) copy-start(f32[16,16,384]{2,1,0:T(8,128)} %copy-done.5) | copy-start | bytes 1179652
  65.1 1.0 %copy-start.8 = (f32[16,16,384]{2,1,0:T(8,128)S(1)}, f32[16,16,384]{2,1,0:T(8,128)}, u32[]{:S(2)}) copy-start(f32[16,16,384]{2,1,0:T(8,128)} %copy-done.7) | copy-start | bytes 1179652
  66.1 0.9 copy-start.15
  67.0 0.8 copy-start.17
  67.9 0.8 copy-start.19
  68.7 20.1 %copy-start.9 = (f32[3,8,8,256]{3,2,1,0:T(8,128)S(1)}, f32[3,8,8,256]{3,2,1,0:T(8,128)}, u32[]{:S(2)}) copy-start(f32[3,8,8,256]{3,2,1,0:T(8,128)} %sol.1) | copy-start | bytes 589828
  77.3 0.7 copy-start.10
  78.0 0.7 copy-start.12
  78.7 10.1 %all-to-all-start = ((f32[32,1,128]{2,1,0:T(1,128)}), f32[32,1,128]{2,1,0:T(1,128)S(1)}, u32[]{:S(2)}, u32[]{:S(2)}) async-start(f32[32,1,128]{2,1,0:T(1,128)} %bitcast.3), calls=%async_computation | async-start | bytes 32768 | tf_op jit(solution)/shard_map/all_to_all | solution.py:709
  88.8 0.9 %copy-start.11 = (f32[3,8,8,256]{3,2,1,0:T(8,128)S(1)}, f32[3,8,8,256]{3,2,1,0:T(8,128)}, u32[]{:S(2)}) copy-start(f32[3,8,8,256]{3,2,1,0:T(8,128)} %copy-done.10) | copy-start | bytes 589828
  89.7 0.9 %copy-start.13 = (f32[3,8,8,256]{3,2,1,0:T(8,128)S(1)}, f32[3,8,8,256]{3,2,1,0:T(8,128)}, u32[]{:S(2)}) copy-start(f32[3,8,8,256]{3,2,1,0:T(8,128)} %copy-done.12) | copy-start | bytes 589828
  (2 other events, 1.3 us)

commit v2 on v1

--- a/solution.py
+++ b/solution.py
@@ -20,35 +20,37 @@
 F32 = jnp.float32
 VMEM = pl.BlockSpec(memory_space=pltpu.VMEM)
 SMEM = pl.BlockSpec(memory_space=pltpu.SMEM)
+HBM = pl.BlockSpec(memory_space=pltpu.HBM)
 
 
 def shape(*dims):
     return jax.ShapeDtypeStruct(dims, F32)
 
 
-def call(body, outs, scratch=(), n_in=0, smem=(), mib=16, flops=1000000):
+def call(body, outs, scratch=(), n_in=0, smem=(), hbm=(), hbm_out=(), mib=16):
     return pl.pallas_call(
         body,
         out_shape=outs,
-        in_specs=[SMEM if i in smem else VMEM for i in range(n_in)],
-        out_specs=[VMEM] * len(outs),
+        in_specs=[SMEM if i in smem else HBM if i in hbm else VMEM for i in range(n_in)],
+        out_specs=[HBM if i in hbm_out else VMEM for i in range(len(outs))],
         scratch_shapes=list(scratch),
         compiler_params=pltpu.CompilerParams(vmem_limit_bytes=mib * 1024 * 1024),
     )
 
 
-def pairs(count, odd):
-    if odd:
-        return [(i, (i + 1) % count if i % 2 else (i - 1) % count) for i in range(count)]
-    return [(i, i ^ 1) for i in range(count)]
-
-
-def swap(axis, even_pack, odd_pack):
+def pairs(count, odd, closed):
+    if not odd:
+        return [(i, i ^ 1) for i in range(count)]
+    made = [(i, (i + 1) % count if i % 2 else (i - 1) % count) for i in range(count)]
+    return made if closed else made[1:-1]
+
+
+def swap(axis, even_pack, odd_pack, closed=True):
     count = lax.axis_size(axis)
-    got_even = lax.ppermute(even_pack, axis, pairs(count, False))
+    got_even = lax.ppermute(even_pack, axis, pairs(count, False, closed))
     if count == 2:
         return [got_even]
-    return [got_even, lax.ppermute(odd_pack, axis, pairs(count, True))]
+    return [got_even, lax.ppermute(odd_pack, axis, pairs(count, True, closed))]
 
 
 def is_even(axis):
@@ -84,12 +86,15 @@
     return lower, upper
 
 
+def tri_y(a):
+    a = a + pltpu.roll(a, 1, 0)
+    return a + pltpu.roll(a, a.shape[0] - 1, 0)
+
+
 def tri_yz(a):
-    rows, lanes = a.shape
-    a = a + pltpu.roll(a, 1, 0)
-    a = a + pltpu.roll(a, rows - 1, 0)
+    a = tri_y(a)
     a = a + pltpu.roll(a, 1, 1)
-    return a + pltpu.roll(a, lanes - 1, 1)
+    return a + pltpu.roll(a, a.shape[1] - 1, 1)
 
 
 def tri_x(before, centre, after):
@@ -147,16 +152,22 @@
 E4_TILES = E_PLANES // 2
 E2_TILES = E_PLANES // 4
 Y_PACK = R_TILES + E4_TILES + E2_TILES
-Z_PACK = COMPS * (X + 2 * RIM) * ROWS + E_PLANES * 24
-R_SLAB = COMPS * (X + 2 * RIM) * ROWS
-
-
-def pack_x_body(table, index, res, young, pack_even, pack_odd):
+Z_TILES = COMPS * (X + 2 * RIM) * (ROWS // 8) + E_PLANES * 3
+Z_PACK = -(-Z_TILES // 16) * 8
+
+
+def pack_x_body(table, index_in, res_in, res, young, pack_even, pack_odd, index, sems):
+    get_index = pltpu.make_async_copy(index_in, index, sems.at[0])
+    get_res = pltpu.make_async_copy(res_in, res, sems.at[1])
+    get_index.start()
+    get_res.start()
+    get_index.wait()
     levels = index[...]
     value = jnp.zeros(levels.shape, F32)
     for level in range(table.shape[0]):
         value = jnp.where(levels == level, table[level], value)
     young[...] = value
+    get_res.wait()
     even = is_even("gx")
     high_first = jnp.where(even, 1, 0)
     for pack, high in ((pack_even, high_first), (pack_odd, 1 - high_first)):
@@ -253,19 +264,39 @@
 
 def pack_z_body(res, young, xa, xb, ya, yb, *packs):
     high_first = jnp.where(is_even("gz"), 1, 0)
+    lane = lane_of((8, 128))
     for pack, high in zip(packs, (high_first, 1 - high_first)):
         lanes = pl.ds(pl.multiple_of(high * (Z - 128), 128), 128)
         res_tiles, young_tiles = xy_planes(res, young, (xa, xb), (ya, yb), lanes, 128)
-        at = 0
-        for c in range(COMPS):
-            for i in range(X + 2 * RIM):
-                for tile in res_tiles(c, i):
-                    pack[at : at + 8] = tile
-                    at += 8
-        for i in range(E_PLANES):
-            for tile in young_tiles(i):
-                pack[at : at + 8] = tile
-                at += 8
+        tiles = [t for c in range(COMPS) for i in range(X + 2 * RIM) for t in res_tiles(c, i)]
+        tiles += [t for i in range(E_PLANES) for t in young_tiles(i)]
+        for first in range(0, len(tiles), 16):
+            packed = None
+            for j, tile in enumerate(tiles[first : first + 16]):
+                moved = pltpu.roll(tile, lax.rem(8 * j + 8 * high, 128), 1)
+                packed = moved if j == 0 else jnp.where(lane < 8 * j, packed, moved)
+            pack[first // 2 : first // 2 + 8] = packed
+
+
+def z_rims(got_z):
+    lane = lane_of((8, 128))
+    even = is_even("gz")
+
+    def piece(got, t, right):
+        start = jnp.where(right, 0, 120)
+        tile = got[8 * (t // 16) : 8 * (t // 16) + 8, :]
+        moved = pltpu.roll(tile, lax.rem(start + 128 - 8 * (t % 16), 128), 1)
+        inside = jnp.logical_and(lane >= start, lane < start + 8)
+        return jnp.where(inside, moved, 0.0)
+
+    def rim(t):
+        first = piece(got_z[0], t, even)
+        if len(got_z) == 1:
+            return first
+        second = piece(got_z[1], t, jnp.logical_not(even))
+        return first + jnp.where(inner("gz"), second, 0.0)
+
+    return rim
 
 
 M_PLANES = X // 2 + 4
@@ -277,9 +308,11 @@
 def fine_apply(s, es, c1, e, i):
     parts = []
     for c in range(COMPS):
-        tv = tri_yz(tri_x(s[c, i - 1], s[c, i], s[c, i + 1]))
-        te = tri_yz(tri_x(es[c, i - 1], es[c, i], es[c, i + 1]))
-        parts.append(c1[i] * s[c, i] - (e[i] * tv + te))
+        v = tri_y(tri_x(s[c, i - 1], s[c, i], s[c, i + 1]))
+        ev = tri_y(tri_x(es[c, i - 1], es[c, i], es[c, i + 1]))
+        total = pltpu.roll(e[1, i] * v + ev, 1, 1) + pltpu.roll(e[2, i] * v + ev, LANES - 1, 1)
+        both = e[0, i] * v + ev
+        parts.append(c1[i] * s[c, i] - (total + (both + both)))
     return coupled(parts)
 
 
@@ -288,32 +321,28 @@
     got_z = refs[6 : 6 + n_z]
     r, s1, e, c1, w, em, c1m, wm, pack = refs[6 + n_z : 15 + n_z]
     wide, s0, es0, es1, rest, pooled, wide_x, wide_p = refs[15 + n_z :]
-    lane = lane_of((8, 128))
 
     res_tiles, young_tiles = xy_planes(res, young, (xa, xb), (ya, yb), slice(None), Z)
-    left, right = from_sides(got_z, "gz")
-
-    def side(at):
-        key = (slice(at, at + 8), slice(None))
-        return jnp.where(lane < 64, right(key), left(key))
-
+    rim = z_rims(got_z)
     at = 0
     for c in range(COMPS):
         for i in range(X + 2 * RIM):
             for t, tile in enumerate(res_tiles(c, i)):
                 r[c, i, 8 * t : 8 * t + 8, :Z] = tile
-                r[c, i, 8 * t : 8 * t + 8, Z:] = side(at)
-                at += 8
+                r[c, i, 8 * t : 8 * t + 8, Z:] = rim(at)
+                at += 1
     for i in range(E_PLANES):
         for t, tile in enumerate(young_tiles(i)):
             wide[i, 8 * t : 8 * t + 8, :Z] = tile * 0.0125
-            wide[i, 8 * t : 8 * t + 8, Z:] = side(at) * 0.0125
-            at += 8
+            wide[i, 8 * t : 8 * t + 8, Z:] = rim(at) * 0.0125
+            at += 1
 
     def prepare(i, _):
         total = tri_yz(tri_x(wide[i + 1], wide[i + 2], wide[i + 3]))[4:20]
         centre = wide[i + 2, 4:20]
-        e[i] = centre
+        e[0, i] = centre
+        e[1, i] = pltpu.roll(centre, LANES - 1, 1)
+        e[2, i] = pltpu.roll(centre, 1, 1)
         c1[i] = 72.0 * centre + total
         inverse = jnp.where(centre > 0.0, DAMPING / (56.0 * centre + total), 0.0)
         w[i] = inverse
@@ -330,10 +359,10 @@
         for c in range(COMPS):
             value = s0[c, i] + w[i] * (r[c, i] - applied[c])
             s1[c, i] = value
-            es1[c, i] = e[i] * value
+            es1[c, i] = e[0, i] * value
         return _
 
-    lax.fori_loop(1, X + 2 * RIM - 1, sweep, 0)
+    lax.fori_loop(1, X + 2 * RIM - 1, sweep, 0, unroll=2)
 
     def residue(m, _):
         first = fine_apply(s1, es1, c1, e, 2 * m + 2)
@@ -407,8 +436,9 @@
 def coarse_body(n_z, *refs):
     pack = refs[0]
     got_z = refs[1 : 1 + n_z]
-    rhs, matrix = refs[1 + n_z : 3 + n_z]
-    planes, column, pack_even, pack_odd, scratch = refs[3 + n_z :]
+    matrix = refs[1 + n_z]
+    gathered = refs[2 + n_z : -5]
+    planes, column, pack_even, pack_odd, scratch = refs[-5:]
     place = lax.axis_index("gz")
     count = lax.axis_size("gz")
     left, right = from_sides(got_z, "gz")
@@ -418,10 +448,18 @@
         planes[t, :, :128] = pack[key]
         planes[t, :, 128:] = jnp.where(lane < 64, right(key), left(key))
 
-    solved = jnp.sum(matrix[...] * rhs[...], axis=1, keepdims=True)
     size = 24
+    if gathered:
+        rhs = gathered[0][...]
+    else:
+        mine = pack[8 * LOW_TILE : 8 * LOW_TILE + 8]
+        other = got_z[0][8 * LOW_TILE : 8 * LOW_TILE + 8]
+        first = jnp.where(place == 0, mine, other)
+        second = jnp.where(place == 0, other, mine)
+        rhs = jnp.where(lane < size, first, pltpu.roll(second, size, 1))[:1, : 2 * size]
+    solved = jnp.sum(matrix[0, 0] * rhs, axis=1, keepdims=True)
     scratch[...] = jnp.zeros(scratch.shape, F32)
-    scratch[size : size + matrix.shape[0]] = jnp.broadcast_to(solved, (matrix.shape[0], 128))
+    scratch[size : size + solved.shape[0]] = jnp.broadcast_to(solved, (solved.shape[0], 128))
     base = pl.multiple_of(place * size, 8)
     wide = lane_of((16, MID_LANES))
     before, own_a, own_b, after = [
@@ -483,7 +521,7 @@
 
 def finish_body(
     wide_planes, columns, got_a, got_b, r, s1, e, c1, w, em, c1m, wm, prev_d, prev_i,
-    precond, operated, sums, cor, mid, big, s2, es2, s3, es3, p, ep,
+    precond_out, operated_out, sums, cor, mid, big, s2, es2, s3, es3, p, ep, precond, operated, sems,
 ):
     lower, upper = from_sides((got_a, got_b), "gy")
     whole = slice(None)
@@ -539,7 +577,7 @@
             more = [big[k, pl.ds(at, 16)] for k in range(LANES // 128)]
             value = s1[c, i] + jnp.concatenate(more, axis=1)
             s2[c, i] = value
-            es2[c, i] = e[i] * value
+            es2[c, i] = e[0, i] * value
         return _
 
     lax.fori_loop(1, X + 2 * RIM - 1, add_up, 0)
@@ -550,13 +588,17 @@
             for c in range(COMPS):
                 value = source[c, i] + w[i] * (r[c, i] - applied[c])
                 target[c, i] = value
-                e_target[c, i] = e[i] * value
+                e_target[c, i] = e[0, i] * value
             return _
 
         return body
 
-    lax.fori_loop(2, X + 2 * RIM - 2, sweep(s2, es2, s3, es3), 0)
-    lax.fori_loop(3, X + 2 * RIM - 3, sweep(s3, es3, p, ep), 0)
+    lax.fori_loop(2, X + 2 * RIM - 2, sweep(s2, es2, s3, es3), 0, unroll=2)
+    lax.fori_loop(3, X + 2 * RIM - 3, sweep(s3, es3, p, ep), 0, unroll=2)
+    leaving = (
+        (precond, precond_out, sems.at[0]),
+        (operated, operated_out, sems.at[1]),
+    )
 
     def image(i, carry):
         applied = fine_apply(p, ep, c1, e, i)
@@ -565,13 +607,15 @@
         for c in range(COMPS):
             own_p = p[c, i, 4:12, :Z]
             own_a = applied[c][4:12, :Z]
-            precond[c, x] = own_p
-            operated[c, x] = own_a
+            precond[x, c] = own_p
+            operated[x, c] = own_a
             d, q = prev_d[c, x], prev_i[c, x]
             rz += r[c, i, 4:12, :Z] * own_p
             pp += own_p * own_a
             mix += own_p * q + d * own_a
             old += d * q
+        for source, target, sem in leaving:
+            pltpu.make_async_copy(source.at[x], target.at[x], sem).start()
         return rz, pp, mix, old
 
     zero = jnp.zeros((Y, Z), F32)
@@ -581,9 +625,22 @@
     for k, value in enumerate(found):
         total = jnp.where(lane == k, jnp.sum(value), total)
     sums[...] = jnp.broadcast_to(total, sums.shape)
-
-
-def last_body(prev_rz, sums, precond, operated, prev_d, prev_i, sol, res, new_s, new_r, new_d, new_i):
+    for source, target, sem in leaving:
+        pltpu.make_async_copy(source, target, sem).wait()
+
+
+def last_body(
+    prev_rz, sums, precond_in, operated_in, prev_d_in, prev_i_in, sol_in, res_in,
+    new_s_out, new_r_out, new_d_out, new_i_out, precond, operated, fields, news, sems,
+):
+    arriving = [
+        pltpu.make_async_copy(precond_in, precond, sems.at[0]),
+        pltpu.make_async_copy(operated_in, operated, sems.at[1]),
+    ]
+    for k, source in enumerate((prev_d_in, prev_i_in, sol_in, res_in)):
+        arriving.append(pltpu.make_async_copy(source, fields.at[k], sems.at[2 + k]))
+    for copy in arriving:
+        copy.start()
     total = jnp.sum(sums[...], axis=0, keepdims=True)
     lane = lane_of((1, 128))
 
@@ -595,14 +652,23 @@
     alpha = rz / (entry(1) + beta * (entry(2) + beta * entry(3)))
     beta = jnp.broadcast_to(beta, (Y, Z))
     alpha = jnp.broadcast_to(alpha, (Y, Z))
+    for copy in arriving:
+        copy.wait()
+    leaving = []
     for c in range(COMPS):
         for x in range(X):
-            d = precond[c, x] + beta * prev_d[c, x]
-            q = operated[c, x] + beta * prev_i[c, x]
-            new_d[c, x] = d
-            new_i[c, x] = q
-            new_s[c, x] = sol[c, x] + alpha * d
-            new_r[c, x] = res[c, x] - alpha * q
+            d = precond[x, c] + beta * fields[0, c, x]
+            q = operated[x, c] + beta * fields[1, c, x]
+            news[2, c, x] = d
+            news[3, c, x] = q
+            news[0, c, x] = fields[2, c, x] + alpha * d
+            news[1, c, x] = fields[3, c, x] - alpha * q
+        for k, target in enumerate((new_s_out, new_r_out, new_d_out, new_i_out)):
+            copy = pltpu.make_async_copy(news.at[k, c], target.at[c], sems.at[6 + 3 * k + c])
+            copy.start()
+            leaving.append(copy)
+    for copy in leaving:
+        copy.wait()
 
 
 def on_device(
@@ -621,16 +687,18 @@
     n_z = 1 if lax.axis_size("gz") == 2 else 2
     n_all = lax.axis_size(ALL)
 
-    young, px, qx = call(
+    res, young, px, qx = call(
         pack_x_body,
-        [shape(X, Y, Z), shape(X_PACK, Y, Z), shape(X_PACK, Y, Z)],
+        [block, shape(X, Y, Z), shape(X_PACK, Y, Z), shape(X_PACK, Y, Z)],
+        scratch=[pltpu.VMEM((X, Y, Z), jnp.int32), pltpu.SemaphoreType.DMA((2,))],
         n_in=3,
         smem=(0,),
+        hbm=(1, 2),
     )(stiffness_table, density_index, residual)
     got_x = swap("gx", px, qx)
-    py, qy = call(pack_y_body, [shape(Y_PACK, Y, Z)] * 2, n_in=4)(residual, young, *got_x)
-    got_y = swap("gy", py, qy)
-    packs = call(pack_z_body, [shape(Z_PACK, 128)] * n_z, n_in=6)(residual, young, *got_x, *got_y)
+    py, qy = call(pack_y_body, [shape(Y_PACK, Y, Z)] * 2, n_in=4)(res, young, *got_x)
+    got_y = swap("gy", py, qy, closed=False)
+    packs = call(pack_z_body, [shape(Z_PACK, 128)] * n_z, n_in=6)(res, young, *got_x, *got_y)
     got_z = swap("gz", packs[0], packs[-1])
 
     planes = X + 2 * RIM
@@ -640,7 +708,7 @@
         [
             shape(*field),
             shape(*field),
-            shape(planes, ROWS, LANES),
+            shape(3, planes, ROWS, LANES),
             shape(planes, ROWS, LANES),
             shape(planes, ROWS, LANES),
             shape(EM_PLANES, 16, MID_LANES),
@@ -660,17 +728,13 @@
         ],
         n_in=6 + n_z,
         mib=30,
-    )(residual, young, *got_x, *got_y, *got_z)
+    )(res, young, *got_x, *got_y, *got_z)
 
     got_z = swap("gz", pack, pack)
-    low = pack[8 * LOW_TILE, :24]
-    if n_z == 1:
-        other = got_z[0][8 * LOW_TILE, :24]
-        first = lax.axis_index("gz") == 0
-        rhs = jnp.where(first, jnp.concatenate([low, other]), jnp.concatenate([other, low]))
-    else:
-        rhs = lax.all_gather(low, "gz", axis=0, tiled=True)
-    size = rhs.shape[0]
+    gathered = []
+    if n_z > 1:
+        gathered = [lax.all_gather(pack[8 * LOW_TILE, :24], "gz", axis=0, tiled=True)[None]]
+    size = coarse_inverse.shape[-1]
     mid_planes, column, px, qx = call(
         functools.partial(coarse_body, n_z),
         [
@@ -680,8 +744,8 @@
             shape(MX_PACK, MID_LANES),
         ],
         scratch=[pltpu.VMEM((size + 64, 128), F32)],
-        n_in=3 + n_z,
-    )(pack, *got_z, rhs.reshape(1, size), coarse_inverse.reshape(size, size))
+        n_in=2 + n_z + len(gathered),
+    )(pack, *got_z, coarse_inverse, *gathered)
     got_x = swap("gx", px, qx)
     mid_planes, columns, py, qy = call(
         mid_y_body,
@@ -696,19 +760,32 @@
     got_y = swap("gy", py, qy)
     precond, operated, sums = call(
         finish_body,
-        [block, block, shape(n_all, 128)],
+        [shape(X, COMPS, Y, Z), shape(X, COMPS, Y, Z), shape(n_all, 128)],
         scratch=[
             pltpu.VMEM((COMPS, 6, 16, MID_LANES), F32),
             pltpu.VMEM((COMPS * 64, MID_LANES), F32),
             pltpu.VMEM((LANES // 128, COMPS * 128, 128), F32),
         ]
-        + [pltpu.VMEM(field, F32)] * 6,
+        + [pltpu.VMEM(field, F32)] * 6
+        + [pltpu.VMEM((X, COMPS, Y, Z), F32)] * 2
+        + [pltpu.SemaphoreType.DMA((2,))],
         n_in=14,
+        hbm_out=(0, 1),
         mib=30,
     )(mid_planes, columns, *got_y, r, s1, e, c1, w, em, c1m, wm, prev_direction, prev_image)
     sums = lax.all_to_all(sums, ALL, 0, 0, tiled=True)
     return tuple(
-        call(last_body, [block] * 4, n_in=8, smem=(0,))(
+        call(
+            last_body,
+            [block] * 4,
+            scratch=[pltpu.VMEM((X, COMPS, Y, Z), F32)] * 2
+            + [pltpu.VMEM((4, COMPS, X, Y, Z), F32)] * 2
+            + [pltpu.SemaphoreType.DMA((18,))],
+            n_in=8,
+            smem=(0,),
+            hbm=(2, 3, 4, 5, 6, 7),
+            hbm_out=(0, 1, 2, 3),
+        )(
             prev_rz.reshape(1), sums, precond, operated, prev_direction, prev_image, solution, residual
         )
     )

time: 92.1 us -> 72.3 us (0.79)
  local copies, waits for them, and re-layouts: 14.6 us -> 2.43 us
  waiting for transfers between devices: 37.6 us -> 29.3 us
  starting transfers between devices: 17.3 us -> 20 us
  Pallas kernels: 20.6 us -> 19 us
    unnamed x46 -> x16, local copies, waits for them, and re-layouts: 14.6 us -> 2.43 us
    ppermute x10, waiting for transfers between devices: 31.2 us -> 22.9 us  [the longest x6 13.6 us: swap(): got_even = lax.ppermute(even_pack, axis, pairs(count, False, closed))]
    ppermute x10, starting transfers between devices: 14.3 us -> 16.9 us  [the longest x6 11.3 us: swap(): got_even = lax.ppermute(even_pack, axis, pairs(count, False, closed))]
    pallas_call x1, Pallas kernels: 10.1 us -> 8.25 us  [on_device(): call(functools.partial(smooth_body, n_z), [shape(*field), shape(*field),...]
  transfers between devices with their start and end apart: 11 -> 11, of which waited for: 11 -> 10; matrix products, arithmetic and copies ran while one was open for 0% -> 0% of each run, Pallas kernels for 0% -> 0%
where the time goes in v2:
time: 72.3 us; the launch traced here: 72.1 us
  waiting for transfers between devices  29.3 us (41%)
  starting transfers between devices  20 us (28%)
  Pallas kernels  19 us (26%)
  local copies, waits for them, and re-layouts  2.43 us (3%)
  between operations  1.37 us (2%)
    ppermute x6, waiting for transfers between devices, swap(): got_even = lax.ppermute(even_pack, axis, pairs(count, False, closed))  13.6 us
    ppermute x6, starting transfers between devices, swap(): got_even = lax.ppermute(even_pack, axis, pairs(count, False, closed))  11.3 us
    ppermute x4, waiting for transfers between devices, swap(): return [got_even, lax.ppermute(odd_pack, axis, pairs(count, True, closed))]  9.33 us
    pallas_call x1, Pallas kernels, on_device(): call(functools.partial(smooth_body, n_z), [shape(*field), shape(*field),...  8.25 us
    pallas_call x1, Pallas kernels, on_device(): call(finish_body, [shape(X, COMPS, Y, Z), shape(X, COMPS, Y, Z), shape(n_...  6.48 us
    all_to_all x1, waiting for transfers between devices, on_device(): sums = lax.all_to_all(sums, ALL, 0, 0, tiled=True)  6.42 us
    ppermute x4, starting transfers between devices, swap(): return [got_even, lax.ppermute(odd_pack, axis, pairs(count, True, closed))]  5.62 us
    all_to_all x1, starting transfers between devices, on_device(): sums = lax.all_to_all(sums, ALL, 0, 0, tiled=True)  3.07 us
  transfers between devices with their start and end apart: 11, of which 10 were waited for; matrix products, arithmetic and copies ran while one was open for 0% of the time, Pallas kernels for 0%

profile of v2, /device:TPU:0, one launch (start us, length us, event | category | flops | bytes accessed | tf_op | source)
XLA Modules:
  0.0 72.1 jit_solution(8916501854755585106)
XLA Ops:
  0.6 0.9 %copy-done = f32[3,8,8,256]{3,2,1,0:T(8,128)S(1)} copy-done((f32[3,8,8,256]{3,2,1,0:T(8,128)S(1)}, f32[3,8,8,256]{3,2,1,0:T(8,128)}, u32[]{:S(2)}) %copy-start) | copy-done | bytes 196632
  1.6 0.8 %copy-done.5 = s32[8,8,256]{2,1,0:T(8,128)S(1)} copy-done((s32[8,8,256]{2,1,0:T(8,128)S(1)}, s32[8,8,256]{2,1,0:T(8,128)}, u32[]{:S(2)}) %copy-start.5) | copy-done | bytes 65560
  2.4 0.7 copy-done.7
  3.1 1.0 %shard_map.111 = (f32[3,8,8,256]{3,2,1,0:T(8,128)S(1)}, f32[8,8,256]{2,1,0:T(8,128)S(1)}, f32[18,8,256]{2,1,0:T(8,128)S(1)}, f32[18,8,256]{2,1,0:T(8,128)S(1)}) custom-call(f32[16]{0:T(128)S(1)} %copy-done.7, s32[8,8,256]{2,1,0:T(8,128)S(1)} %copy-done.5, f32[3,8,8,256]{3,2,1,0:T(8,128)S(1)} %copy-done), custom_call_target="tpu_custom_call" | custom-call | tf_op jit(solution)/shard_map/pallas_call | solution.py:690
  4.1 3.0 %collective-permute-start = (f32[18,8,256]{2,1,0:T(8,128)S(1)}, f32[18,8,256]{2,1,0:T(8,128)S(1)}, u32[]{:S(2)}, u32[]{:S(2)}) collective-permute-start(f32[18,8,256]{2,1,0:T(8,128)S(1)} %get-tuple-element.32), channel_id=1, source_target_pairs={{0,8},{8,0},{16,24},{24,16},{1,9},{9,1},{17,25},{25,17},{2,10},{10... | collective-permute-start | bytes 442376 | tf_op jit(solution)/shard_map/ppermute | solution.py:50
  7.1 1.5 %collective-permute-start.1 = (f32[18,8,256]{2,1,0:T(8,128)S(1)}, f32[18,8,256]{2,1,0:T(8,128)S(1)}, u32[]{:S(2)}, u32[]{:S(2)}) collective-permute-start(f32[18,8,256]{2,1,0:T(8,128)S(1)} %get-tuple-element.33), channel_id=1, source_target_pairs={{0,24},{8,16},{16,8},{24,0},{1,25},{9,17},{17,9},{25,1},{2,26},{10... | collective-permute-start | bytes 442376 | tf_op jit(solution)/shard_map/ppermute | solution.py:53
  8.6 3.0 %collective-permute-done.got_a.xa.refs_2_ = f32[18,8,256]{2,1,0:T(8,128)S(1)} collective-permute-done((f32[18,8,256]{2,1,0:T(8,128)S(1)}, f32[18,8,256]{2,1,0:T(8,128)S(1)}, u32[]{:S(2)}, u32[]{:S(2)}) %collective-permute-start) | collective-permute-done | bytes 147488 | tf_op jit(solution)/shard_map/ppermute | solution.py:50
  11.6 3.7 %collective-permute-done.1.got_b.xb.refs_3_ = f32[18,8,256]{2,1,0:T(8,128)S(1)} collective-permute-done((f32[18,8,256]{2,1,0:T(8,128)S(1)}, f32[18,8,256]{2,1,0:T(8,128)S(1)}, u32[]{:S(2)}, u32[]{:S(2)}) %collective-permute-start.1) | collective-permute-done | bytes 147488 | tf_op jit(solution)/shard_map/ppermute | solution.py:53
  15.3 0.1 shard_map.112
  15.4 1.6 %collective-permute-start.2 = (f32[39,8,256]{2,1,0:T(8,128)S(1)}, f32[39,8,256]{2,1,0:T(8,128)S(1)}, u32[]{:S(2)}, u32[]{:S(2)}) collective-permute-start(f32[39,8,256]{2,1,0:T(8,128)S(1)} %get-tuple-element.34), channel_id=1, source_target_pairs={{0,2},{2,0},{4,6},{6,4},{1,3},{3,1},{5,7},{7,5},{8,10},{10,8},{12,... | collective-permute-start | bytes 958472 | tf_op jit(solution)/shard_map/ppermute | solution.py:50
  17.0 0.8 %collective-permute-start.3 = (f32[39,8,256]{2,1,0:T(8,128)S(1)}, f32[39,8,256]{2,1,0:T(8,128)S(1)}, u32[]{:S(2)}, u32[]{:S(2)}) collective-permute-start(f32[39,8,256]{2,1,0:T(8,128)S(1)} %get-tuple-element.35), channel_id=1, source_target_pairs={{2,4},{4,2},{3,5},{5,3},{10,12},{12,10},{11,13},{13,11},{18,20},{2... | collective-permute-start | bytes 958472 | tf_op jit(solution)/shard_map/ppermute | solution.py:53
  17.8 6.0 %collective-permute-done.2.ya.refs_4_ = f32[39,8,256]{2,1,0:T(8,128)S(1)} collective-permute-done((f32[39,8,256]{2,1,0:T(8,128)S(1)}, f32[39,8,256]{2,1,0:T(8,128)S(1)}, u32[]{:S(2)}, u32[]{:S(2)}) %collective-permute-start.2) | collective-permute-done | bytes 319520 | tf_op jit(solution)/shard_map/ppermute | solution.py:50
  23.9 0.2 shard_map.113
  24.1 0.1 collective-permute-start.4
  24.2 1.2 %collective-permute-done.4.refs_6_ = f32[80,128]{1,0:T(8,128)S(1)} collective-permute-done((f32[80,128]{1,0:T(8,128)S(1)}, f32[80,128]{1,0:T(8,128)S(1)}, u32[]{:S(2)}, u32[]{:S(2)}) %collective-permute-start.4) | collective-permute-done | bytes 40992 | tf_op jit(solution)/shard_map/ppermute | solution.py:50
  25.4 8.3 %shard_map.114 = (f32[3,16,16,384]{3,2,1,0:T(8,128)S(1)}, f32[3,16,16,384]{3,2,1,0:T(8,128)S(1)}, f32[3,16,16,384]{3,2,1,0:T(8,128)S(1)}, f32[16,16,384]{2,1,0:T...) custom-call(f32[3,8,8,256]{3,2,1,0:T(8,128)S(1)} %get-tuple-element., ...), custom_call_target="tpu_custom_call" | custom-call | tf_op jit(solution)/shard_map/pallas_call | solution.py:706
  33.7 0.2 collective-permute-start.5
  33.9 1.1 %collective-permute-done.5.refs_1_ = f32[104,128]{1,0:T(8,128)S(1)} collective-permute-done((f32[104,128]{1,0:T(8,128)S(1)}, f32[104,128]{1,0:T(8,128)S(1)}, u32[]{:S(2)}, u32[]{:S(2)}) %collective-permute-start.5) | collective-permute-done | bytes 53280 | tf_op jit(solution)/shard_map/ppermute | solution.py:50
  35.0 0.2 shard_map.115
  35.1 1.6 %collective-permute-start.6 = (f32[40,256]{1,0:T(8,128)S(1)}, f32[40,256]{1,0:T(8,128)S(1)}, u32[]{:S(2)}, u32[]{:S(2)}) collective-permute-start(f32[40,256]{1,0:T(8,128)S(1)} %get-tuple-element.39), channel_id=1, source_target_pairs={{0,8},{8,0},{16,24},{24,16},{1,9},{9,1},{17,25},{25,17},{2,10},{10... | collective-permute-start | bytes 122888 | tf_op jit(solution)/shard_map/ppermute | solution.py:50
  36.7 0.7 collective-permute-start.7
  37.4 2.0 %collective-permute-done.6.got_a = f32[40,256]{1,0:T(8,128)S(1)} collective-permute-done((f32[40,256]{1,0:T(8,128)S(1)}, f32[40,256]{1,0:T(8,128)S(1)}, u32[]{:S(2)}, u32[]{:S(2)}) %collective-permute-start.6) | collective-permute-done | bytes 40992 | tf_op jit(solution)/shard_map/ppermute | solution.py:50
  39.4 2.2 %collective-permute-done.7.got_b = f32[40,256]{1,0:T(8,128)S(1)} collective-permute-done((f32[40,256]{1,0:T(8,128)S(1)}, f32[40,256]{1,0:T(8,128)S(1)}, u32[]{:S(2)}, u32[]{:S(2)}) %collective-permute-start.7) | collective-permute-done | bytes 40992 | tf_op jit(solution)/shard_map/ppermute | solution.py:53
  41.6 0.1 shard_map.116
  41.6 4.8 %collective-permute-start.8 = (f32[88,256]{1,0:T(8,128)S(1)}, f32[88,256]{1,0:T(8,128)S(1)}, u32[]{:S(2)}, u32[]{:S(2)}) collective-permute-start(f32[88,256]{1,0:T(8,128)S(1)} %get-tuple-element.43), channel_id=1, source_target_pairs={{0,2},{2,0},{4,6},{6,4},{1,3},{3,1},{5,7},{7,5},{8,10},{10,8},{12,... | collective-permute-start | bytes 270344 | tf_op jit(solution)/shard_map/ppermute | solution.py:50
  46.4 2.6 %collective-permute-start.9 = (f32[88,256]{1,0:T(8,128)S(1)}, f32[88,256]{1,0:T(8,128)S(1)}, u32[]{:S(2)}, u32[]{:S(2)}) collective-permute-start(f32[88,256]{1,0:T(8,128)S(1)} %get-tuple-element.44), channel_id=1, source_target_pairs={{0,6},{2,4},{4,2},{6,0},{1,7},{3,5},{5,3},{7,1},{8,14},{10,12},{12... | collective-permute-start | bytes 270344 | tf_op jit(solution)/shard_map/ppermute | solution.py:53
  49.1 0.3 collective-permute-done.8.got_a
  49.3 3.4 %collective-permute-done.9.got_b = f32[88,256]{1,0:T(8,128)S(1)} collective-permute-done((f32[88,256]{1,0:T(8,128)S(1)}, f32[88,256]{1,0:T(8,128)S(1)}, u32[]{:S(2)}, u32[]{:S(2)}) %collective-permute-start.9) | collective-permute-done | bytes 90144 | tf_op jit(solution)/shard_map/ppermute | solution.py:53
  52.8 6.5 %shard_map.117 = (f32[8,3,8,256]{3,2,1,0:T(8,128)S(1)}, f32[8,3,8,256]{3,2,1,0:T(8,128)S(1)}, f32[32,128]{1,0:T(8,128)}) custom-call(f32[24,8,256]{2,1,0:T(8,128)S(1)} %get-tuple-element.41.wide_planes, f32[40,256]{1,0:T(8,128)S(1)} %get-tuple-element.42.columns, f32[88,256]{1,0:T(8,128)S(1)} %collective-permute-done.8.got_a, ...), custom_call_target="tpu_custom_call" | custom-call | tf_op jit(solution)/shard_map/pallas_call | solution.py:761
  59.3 3.1 %all-to-all-start = ((f32[32,1,128]{2,1,0:T(1,128)}), f32[32,1,128]{2,1,0:T(1,128)S(1)}, u32[]{:S(2)}, u32[]{:S(2)}) async-start(f32[32,1,128]{2,1,0:T(1,128)} %bitcast.2), calls=%async_computation | async-start | bytes 32768 | tf_op jit(solution)/shard_map/all_to_all | solution.py:776
  63.0 6.4 %all-to-all-done = f32[32,1,128]{2,1,0:T(1,128)S(1)} async-done(((f32[32,1,128]{2,1,0:T(1,128)}), f32[32,1,128]{2,1,0:T(1,128)S(1)}, u32[]{:S(2)}, u32[]{:S(2)}) %all-to-all-start) | async-done | bytes 16416 | tf_op jit(solution)/shard_map/all_to_all | solution.py:776
  69.4 2.7 %shard_map.118 = (f32[3,8,8,256]{3,2,1,0:T(8,128)}, f32[3,8,8,256]{3,2,1,0:T(8,128)}, f32[3,8,8,256]{3,2,1,0:T(8,128)}, f32[3,8,8,256]{3,2,1,0:T(8,128)}) custom-call(f32[1]{0:T(128)} %bitcast.5.prev_rz, f32[32,128]{1,0:T(8,128)S(1)} %bitcast.6, f32[8,3,8,256]{3,2,1,0:T(8,128)S(1)} %get-tuple-element.54.precond_in, ...), custom_call_target="tpu_custom_call" | custom-call | tf_op jit(solution)/shard_map/pallas_call | solution.py:778
  (14 shorter events, 0.0 us)
Async XLA Ops:
  0.6 0.9 %copy-start = (f32[3,8,8,256]{3,2,1,0:T(8,128)S(1)}, f32[3,8,8,256]{3,2,1,0:T(8,128)}, u32[]{:S(2)}) copy-start(f32[3,8,8,256]{3,2,1,0:T(8,128)} %res_in.3) | copy-start | bytes 589828
  1.6 0.8 %copy-start.5 = (s32[8,8,256]{2,1,0:T(8,128)S(1)}, s32[8,8,256]{2,1,0:T(8,128)}, u32[]{:S(2)}) copy-start(s32[8,8,256]{2,1,0:T(8,128)} %index_in.1) | copy-start | bytes 196612
  2.4 0.7 copy-start.7
  4.1 7.5 %collective-permute-start = (f32[18,8,256]{2,1,0:T(8,128)S(1)}, f32[18,8,256]{2,1,0:T(8,128)S(1)}, u32[]{:S(2)}, u32[]{:S(2)}) collective-permute-start(f32[18,8,256]{2,1,0:T(8,128)S(1)} %get-tuple-element.32), channel_id=1, source_target_pairs={{0,8},{8,0},{16,24},{24,16},{1,9},{9,1},{17,25},{25,17},{2,10},{10... | collective-permute-start | bytes 442376 | tf_op jit(solution)/shard_map/ppermute | solution.py:50
  7.1 8.2 %collective-permute-start.1 = (f32[18,8,256]{2,1,0:T(8,128)S(1)}, f32[18,8,256]{2,1,0:T(8,128)S(1)}, u32[]{:S(2)}, u32[]{:S(2)}) collective-permute-start(f32[18,8,256]{2,1,0:T(8,128)S(1)} %get-tuple-element.33), channel_id=1, source_target_pairs={{0,24},{8,16},{16,8},{24,0},{1,25},{9,17},{17,9},{25,1},{2,26},{10... | collective-permute-start | bytes 442376 | tf_op jit(solution)/shard_map/ppermute | solution.py:53
  15.4 8.5 %collective-permute-start.2 = (f32[39,8,256]{2,1,0:T(8,128)S(1)}, f32[39,8,256]{2,1,0:T(8,128)S(1)}, u32[]{:S(2)}, u32[]{:S(2)}) collective-permute-start(f32[39,8,256]{2,1,0:T(8,128)S(1)} %get-tuple-element.34), channel_id=1, source_target_pairs={{0,2},{2,0},{4,6},{6,4},{1,3},{3,1},{5,7},{7,5},{8,10},{10,8},{12,... | collective-permute-start | bytes 958472 | tf_op jit(solution)/shard_map/ppermute | solution.py:50
  17.0 17.9 %copy-start.6 = (f32[1,1,48,48]{3,2,1,0:T(8,128)S(1)}, f32[1,1,48,48]{3,2,1,0:T(8,128)}, u32[]{:S(2)}) copy-start(f32[1,1,48,48]{3,2,1,0:T(8,128)} %refs_2_.1) | copy-start | bytes 27652
  17.0 35.7 %copy-start.2 = (f32[3,8,8,256]{3,2,1,0:T(8,128)S(1)}, f32[3,8,8,256]{3,2,1,0:T(8,128)}, u32[]{:S(2)}) copy-start(f32[3,8,8,256]{3,2,1,0:T(8,128)} %prev_d_in.1) | copy-start | bytes 589828
  17.0 35.7 %copy-start.3 = (f32[3,8,8,256]{3,2,1,0:T(8,128)S(1)}, f32[3,8,8,256]{3,2,1,0:T(8,128)}, u32[]{:S(2)}) copy-start(f32[3,8,8,256]{3,2,1,0:T(8,128)} %prev_i_in.1) | copy-start | bytes 589828
  17.0 6.8 %collective-permute-start.3 = (f32[39,8,256]{2,1,0:T(8,128)S(1)}, f32[39,8,256]{2,1,0:T(8,128)S(1)}, u32[]{:S(2)}, u32[]{:S(2)}) collective-permute-start(f32[39,8,256]{2,1,0:T(8,128)S(1)} %get-tuple-element.35), channel_id=1, source_target_pairs={{2,4},{4,2},{3,5},{5,3},{10,12},{12,10},{11,13},{13,11},{18,20},{2... | collective-permute-start | bytes 958472 | tf_op jit(solution)/shard_map/ppermute | solution.py:53
  24.1 1.3 %collective-permute-start.4 = (f32[80,128]{1,0:T(8,128)S(1)}, f32[80,128]{1,0:T(8,128)S(1)}, u32[]{:S(2)}, u32[]{:S(2)}) collective-permute-start(f32[80,128]{1,0:T(8,128)S(1)} %shard_map.113), channel_id=1, source_target_pairs={{0,1},{1,0},{2,3},{3,2},{4,5},{5,4},{6,7},{7,6},{8,9},{9,8},{10,11... | collective-permute-start | bytes 122888 | tf_op jit(solution)/shard_map/ppermute | solution.py:50
  33.7 1.3 %collective-permute-start.5 = (f32[104,128]{1,0:T(8,128)S(1)}, f32[104,128]{1,0:T(8,128)S(1)}, u32[]{:S(2)}, u32[]{:S(2)}) collective-permute-start(f32[104,128]{1,0:T(8,128)S(1)} %get-tuple-element.36.refs_0_), channel_id=1, source_target_pairs={{0,1},{1,0},{2,3},{3,2},{4,5},{5,4},{6,7},{7,6},{8,9},{9,8},{10,11... | collective-permute-start | bytes 159752 | tf_op jit(solution)/shard_map/ppermute | solution.py:50
  35.1 4.2 %collective-permute-start.6 = (f32[40,256]{1,0:T(8,128)S(1)}, f32[40,256]{1,0:T(8,128)S(1)}, u32[]{:S(2)}, u32[]{:S(2)}) collective-permute-start(f32[40,256]{1,0:T(8,128)S(1)} %get-tuple-element.39), channel_id=1, source_target_pairs={{0,8},{8,0},{16,24},{24,16},{1,9},{9,1},{17,25},{25,17},{2,10},{10... | collective-permute-start | bytes 122888 | tf_op jit(solution)/shard_map/ppermute | solution.py:50
  36.7 4.9 %collective-permute-start.7 = (f32[40,256]{1,0:T(8,128)S(1)}, f32[40,256]{1,0:T(8,128)S(1)}, u32[]{:S(2)}, u32[]{:S(2)}) collective-permute-start(f32[40,256]{1,0:T(8,128)S(1)} %get-tuple-element.40), channel_id=1, source_target_pairs={{0,24},{8,16},{16,8},{24,0},{1,25},{9,17},{17,9},{25,1},{2,26},{10... | collective-permute-start | bytes 122888 | tf_op jit(solution)/shard_map/ppermute | solution.py:53
  41.6 7.7 %collective-permute-start.8 = (f32[88,256]{1,0:T(8,128)S(1)}, f32[88,256]{1,0:T(8,128)S(1)}, u32[]{:S(2)}, u32[]{:S(2)}) collective-permute-start(f32[88,256]{1,0:T(8,128)S(1)} %get-tuple-element.43), channel_id=1, source_target_pairs={{0,2},{2,0},{4,6},{6,4},{1,3},{3,1},{5,7},{7,5},{8,10},{10,8},{12,... | collective-permute-start | bytes 270344 | tf_op jit(solution)/shard_map/ppermute | solution.py:50
  46.4 6.3 %collective-permute-start.9 = (f32[88,256]{1,0:T(8,128)S(1)}, f32[88,256]{1,0:T(8,128)S(1)}, u32[]{:S(2)}, u32[]{:S(2)}) collective-permute-start(f32[88,256]{1,0:T(8,128)S(1)} %get-tuple-element.44), channel_id=1, source_target_pairs={{0,6},{2,4},{4,2},{6,0},{1,7},{3,5},{5,3},{7,1},{8,14},{10,12},{12... | collective-permute-start | bytes 270344 | tf_op jit(solution)/shard_map/ppermute | solution.py:53
  52.8 16.6 %copy-start.1 = (f32[3,8,8,256]{3,2,1,0:T(8,128)S(1)}, f32[3,8,8,256]{3,2,1,0:T(8,128)}, u32[]{:S(2)}) copy-start(f32[3,8,8,256]{3,2,1,0:T(8,128)} %res_in.3) | copy-start | bytes 589828
  52.8 16.6 %copy-start.4 = (f32[3,8,8,256]{3,2,1,0:T(8,128)S(1)}, f32[3,8,8,256]{3,2,1,0:T(8,128)}, u32[]{:S(2)}) copy-start(f32[3,8,8,256]{3,2,1,0:T(8,128)} %sol_in.1) | copy-start | bytes 589828
  59.3 10.1 %all-to-all-start = ((f32[32,1,128]{2,1,0:T(1,128)}), f32[32,1,128]{2,1,0:T(1,128)S(1)}, u32[]{:S(2)}, u32[]{:S(2)}) async-start(f32[32,1,128]{2,1,0:T(1,128)} %bitcast.2), calls=%async_computation | async-start | bytes 32768 | tf_op jit(solution)/shard_map/all_to_all | solution.py:776

commit v3 on v2

v3 whole, which is shorter than its diff:
```python
import functools
import math

import jax
import jax.numpy as jnp
from jax import lax
from jax.experimental import pallas as pl
from jax.experimental.pallas import tpu as pltpu
from jax.sharding import PartitionSpec as P

X, Y, Z = 8, 8, 256
COMPS = 3
RIM = 4
WIDE = 6
ROWS = Y + 2 * RIM
LANES = Z + 128
MID_LANES = Z // 2 + 128
DAMPING = 0.6
ALL = ("gx", "gy", "gz")
F32 = jnp.float32
VMEM = pl.BlockSpec(memory_space=pltpu.VMEM)
SMEM = pl.BlockSpec(memory_space=pltpu.SMEM)
HBM = pl.BlockSpec(memory_space=pltpu.HBM)


def shape(*dims):
    return jax.ShapeDtypeStruct(dims, F32)


def call(body, outs, scratch=(), n_in=0, smem=(), hbm=(), hbm_out=(), vmem=16 << 20):
    return pl.pallas_call(
        body,
        out_shape=outs,
        in_specs=[SMEM if i in smem else HBM if i in hbm else VMEM for i in range(n_in)],
        out_specs=[HBM if i in hbm_out else VMEM for i in range(len(outs))],
        scratch_shapes=list(scratch),
        compiler_params=pltpu.CompilerParams(vmem_limit_bytes=vmem),
    )


def pairs(count, odd, closed):
    if not odd:
        return [(i, i ^ 1) for i in range(count)]
    made = [(i, (i + 1) % count if i % 2 else (i - 1) % count) for i in range(count)]
    return made if closed else made[1:-1]


def swap(axis, even_pack, odd_pack, closed=True):
    count = lax.axis_size(axis)
    got_even = lax.ppermute(even_pack, axis, pairs(count, False, closed))
    if count == 2:
        return [got_even]
    return [got_even, lax.ppermute(odd_pack, axis, pairs(count, True, closed))]


def is_even(axis):
    return lax.rem(lax.axis_index(axis), 2) == 0


def inner(axis):
    index = lax.axis_index(axis)
    return jnp.logical_and(index > 0, index < lax.axis_size(axis) - 1)


def from_sides(got, axis):
    even = is_even(axis)
    if len(got) == 1:

        def lower(key):
            value = got[0][key]
            return jnp.where(even, 0.0, value)

        def upper(key):
            value = got[0][key]
            return jnp.where(even, value, 0.0)

        return lower, upper
    ok = inner(axis)

    def lower(key):
        return jnp.where(even, jnp.where(ok, got[1][key], 0.0), got[0][key])

    def upper(key):
        return jnp.where(even, got[0][key], jnp.where(ok, got[1][key], 0.0))

    return lower, upper


def tri_y(a):
    a = a + pltpu.roll(a, 1, 0)
    return a + pltpu.roll(a, a.shape[0] - 1, 0)


def tri_y_with(a, below, above, last):
    rows = a.shape[0]
    row = row_of(a.shape)
    former = jnp.where(row == last + 1, below, pltpu.roll(a, 1, 0))
    after = jnp.where(row == last, above, pltpu.roll(a, rows - 1, 0))
    return former + after + (a + a)


def mixed_z(e, e_next, e_last, v, ev):
    both = e * v + ev
    moved = pltpu.roll(e_next * v + ev, 1, 1) + pltpu.roll(e_last * v + ev, v.shape[1] - 1, 1)
    return moved + (both + both)


def tri_x(before, centre, after):
    return before + after + (centre + centre)


def coupled(parts):
    total = 0.3 * (parts[0] + parts[1] + parts[2])
    return [0.7 * part + total for part in parts]


def row_of(shape):
    return lax.broadcasted_iota(jnp.int32, shape, 0)


def lane_of(shape):
    return lax.broadcasted_iota(jnp.int32, shape, 1)


def up(a, shift):
    shift %= a.shape[0]
    return pltpu.roll(a, shift, 0) if shift else a


def pool_matrix(value):
    lane = row_of((LANES, MID_LANES))
    mid = jnp.where(lane < Z + 64, lane // 2, lane // 2 + 64)
    return jnp.where(mid == lane_of((LANES, MID_LANES)), value, 0.0).astype(F32)


def spread_matrix():
    lane = lane_of((MID_LANES, LANES))
    mid = jnp.where(lane < Z + 64, lane // 2, lane // 2 + 64)
    return jnp.where(mid == row_of((MID_LANES, LANES)), 1.0, 0.0).astype(F32)


def every_other(ref, at, size):
    return jnp.concatenate(
        [ref[k, pl.ds(at, size, stride=2)] for k in range(ref.shape[0])], axis=1
    )


def dot_exact_weights(a, b):
    b = b.astype(jnp.bfloat16)
    total = None
    for k in range(3):
        part = a.astype(jnp.bfloat16)
        found = jnp.dot(part, b, preferred_element_type=F32)
        total = found if total is None else total + found
        if k < 2:
            a = a - part.astype(F32)
    return total


X_PACK = COMPS * RIM + WIDE
R_TILES = COMPS * X
E_PLANES = X + 2 * WIDE
E4_TILES = E_PLANES // 2
E2_TILES = E_PLANES // 4
Y_PACK = R_TILES + E4_TILES + E2_TILES
Z_TILES = COMPS * (X + 2 * RIM) * (ROWS // 8) + E_PLANES * 3
Z_PACK = -(-Z_TILES // 16) * 8


def pack_x_body(table, index, res_in, res, young, pack_even, pack_odd):
    res[...] = res_in[...]
    levels = index[...]
    value = jnp.zeros(levels.shape, F32)
    for level in range(table.shape[0]):
        value = jnp.where(levels == level, table[level], value)
    young[...] = value
    high_first = jnp.where(is_even("gx"), 1, 0)
    for pack, high in ((pack_even, high_first), (pack_odd, 1 - high_first)):
        for c in range(COMPS):
            pack[c * RIM : (c + 1) * RIM] = res[c, pl.ds(high * (X - RIM), RIM)]
        pack[COMPS * RIM :] = young[pl.ds(high * (X - WIDE), WIDE)]


def x_planes(res, young, got_x, lanes=slice(None)):
    lower, upper = from_sides(got_x, "gx")
    whole = slice(None)

    def res_plane(c, i):
        if i < RIM:
            return lower((c * RIM + i, whole, lanes))
        if i < RIM + X:
            return res[c, i - RIM, :, lanes]
        return upper((c * RIM + i - RIM - X, whole, lanes))

    def young_plane(i):
        if i < WIDE:
            return lower((COMPS * RIM + i, whole, lanes))
        if i < WIDE + X:
            return young[i - WIDE, :, lanes]
        return upper((COMPS * RIM + i - WIDE - X, whole, lanes))

    return res_plane, young_plane


def pack_y_body(res, young, got_a, got_b, pack_even, pack_odd):
    res_plane, young_plane = x_planes(res, young, (got_a, got_b))
    row = row_of((Y, Z))
    even = is_even("gy")

    def put(tile, low, high):
        pack_even[tile] = jnp.where(even, high, low)
        pack_odd[tile] = jnp.where(even, low, high)

    def halves(tile, a, b):
        put(
            tile,
            jnp.where(row < 4, a, up(b, 4)),
            jnp.where(row < 4, up(a, 4), b),
        )

    for c in range(COMPS):
        for i in range(X):
            halves(c * X + i, res_plane(c, i), res_plane(c, i + X))
    planes = [young_plane(i) for i in range(E_PLANES)]
    for i in range(E4_TILES):
        halves(R_TILES + i, planes[i], planes[i + E4_TILES])
    for j in range(E2_TILES):
        low = high = None
        for k in range(4):
            plane = planes[4 * j + k]
            a, b = up(plane, 2 * k - 4), up(plane, 2 * k - 2)
            low = a if k == 0 else jnp.where(row < 2 * k, low, a)
            high = b if k == 0 else jnp.where(row < 2 * k, high, b)
        put(R_TILES + E4_TILES + j, low, high)


def xy_planes(res, young, got_x, got_y, lanes, width):
    res_plane, young_plane = x_planes(res, young, got_x, lanes)
    lower, upper = from_sides(got_y, "gy")
    row = row_of((Y, width))
    whole = slice(None)

    def rim_tile(tile, second):
        key = (tile, whole, lanes)
        low, high = lower(key), upper(key)
        if second:
            high = up(high, 4)
        else:
            low = up(low, 4)
        return jnp.where(row < 4, high, low)

    def res_tiles(c, i):
        return [res_plane(c, i), rim_tile(c * X + i % X, i >= X)]

    def young_tiles(i):
        two = (R_TILES + E4_TILES + i // 4, whole, lanes)
        k = i % 4
        low2, high2 = up(lower(two), -2 * k), up(upper(two), 2 - 2 * k)
        side = jnp.where(row < 2, low2, jnp.where(row < 4, high2, 0.0))
        return [young_plane(i), rim_tile(R_TILES + i % E4_TILES, i >= E4_TILES), side]

    return res_tiles, young_tiles


def pack_z_body(res, young, xa, xb, ya, yb, *packs):
    high_first = jnp.where(is_even("gz"), 1, 0)
    lane = lane_of((8, 128))
    for pack, high in zip(packs, (high_first, 1 - high_first)):
        lanes = pl.ds(pl.multiple_of(high * (Z - 128), 128), 128)
        res_tiles, young_tiles = xy_planes(res, young, (xa, xb), (ya, yb), lanes, 128)
        tiles = [t for c in range(COMPS) for i in range(X + 2 * RIM) for t in res_tiles(c, i)]
        tiles += [t for i in range(E_PLANES) for t in young_tiles(i)]
        for first in range(0, len(tiles), 16):
            packed = None
            for j, tile in enumerate(tiles[first : first + 16]):
                moved = pltpu.roll(tile, lax.rem(8 * j + 8 * high, 128), 1)
                packed = moved if j == 0 else jnp.where(lane < 8 * j, packed, moved)
            pack[first // 2 : first // 2 + 8] = packed


def z_rims(got_z):
    lane = lane_of((8, 128))
    even = is_even("gz")

    def piece(got, t, right):
        start = jnp.where(right, 0, 120)
        tile = got[8 * (t // 16) : 8 * (t // 16) + 8, :]
        moved = pltpu.roll(tile, lax.rem(start + 128 - 8 * (t % 16), 128), 1)
        inside = jnp.logical_and(lane >= start, lane < start + 8)
        return jnp.where(inside, moved, 0.0)

    def rim(t):
        first = piece(got_z[0], t, even)
        if len(got_z) == 1:
            return first
        second = piece(got_z[1], t, jnp.logical_not(even))
        return first + jnp.where(inner("gz"), second, 0.0)

    return rim


M_PLANES = X // 2 + 4
EM_PLANES = X // 2 + 6
LOW_TILE = COMPS * (X // 2)
MZ_PACK = (LOW_TILE + 1) * 8


def fine_apply(s, es, c1, e, i):
    parts = []
    for c in range(COMPS):
        v = tri_y(tri_x(s[c, i - 1], s[c, i], s[c, i + 1]))
        ev = tri_y(tri_x(es[c, i - 1], es[c, i], es[c, i + 1]))
        parts.append(c1[i] * s[c, i] - mixed_z(e[0, i], e[1, i], e[2, i], v, ev))
    return coupled(parts)


def sweep(source, e_source, target, e_target, r, c1, e, w, first, last):
    def body(k, carry):
        for i in (first + 2 * k, first + 2 * k + 1):
            applied = fine_apply(source, e_source, c1, e, i)
            for c in range(COMPS):
                value = source[c, i] + w[i] * (r[c, i] - applied[c])
                target[c, i] = value
                e_target[c, i] = e[0, i] * value
        return carry

    lax.fori_loop(0, (last - first) // 2, body, 0)


def smooth_body(n_z, *refs):
    res, young, xa, xb, ya, yb = refs[:6]
    got_z = refs[6 : 6 + n_z]
    r, s1, e, c1, w, em, em_side, c1m, wm, pack = refs[6 + n_z : 16 + n_z]
    wide, wide_z, s0, es0, es1, rest, wide_x = refs[16 + n_z :]

    res_tiles, young_tiles = xy_planes(res, young, (xa, xb), (ya, yb), slice(None), Z)
    rim = z_rims(got_z)
    at = 0
    for c in range(COMPS):
        for i in range(PLANES):
            for t, tile in enumerate(res_tiles(c, i)):
                r[c, i, 8 * t : 8 * t + 8, :Z] = tile
                r[c, i, 8 * t : 8 * t + 8, Z:] = rim(at)
                at += 1
    for i in range(E_PLANES):
        for t, tile in enumerate(young_tiles(i)):
            wide[i, 8 * t : 8 * t + 8, :Z] = tile * 0.0125
            wide[i, 8 * t : 8 * t + 8, Z:] = rim(at) * 0.0125
            at += 1

    def shift(k, carry):
        for i in (2 * k, 2 * k + 1):
            centre = wide[i]
            after, before = pltpu.roll(centre, LANES - 1, 1), pltpu.roll(centre, 1, 1)
            wide_z[i] = after + before + (centre + centre)
            e[0, i] = centre[:ROWS]
            e[1, i] = after[:ROWS]
            e[2, i] = before[:ROWS]
        total = wide[2 * k] + wide[2 * k + 1]
        for t in range(LANES // 128):
            wide_x[t, pl.ds(24 * k, 24)] = total[:, 128 * t : 128 * t + 128]
        return carry

    lax.fori_loop(0, E_PLANES // 2, shift, 0, unroll=5)

    def prepare(k, carry):
        for i in (2 * k, 2 * k + 1):
            total = tri_x(wide_z[i + 1], wide_z[i + 2], wide_z[i + 3])
            side = total[ROWS:]
            below = jnp.concatenate([side, up(side, 3)], axis=0)
            above = jnp.concatenate([side, up(side, 1)], axis=0)
            total = tri_y_with(total[:ROWS], below, above, 11)
            centre = e[0, i + 2]
            c1[i] = 72.0 * centre + total
            inverse = jnp.where(centre > 0.0, DAMPING / (56.0 * centre + total), 0.0)
            w[i] = inverse
            for c in range(COMPS):
                value = inverse * r[c, i]
                s0[c, i] = value
                es0[c, i] = centre * value
        return carry

    lax.fori_loop(0, PLANES // 2, prepare, 0)
    e = e.at[:, 2 : 2 + PLANES]
    sweep(s0, es0, s1, es1, r, c1, e, w, 1, PLANES - 1)

    def residue(m, carry):
        first = fine_apply(s1, es1, c1, e, 2 * m + 2)
        second = fine_apply(s1, es1, c1, e, 2 * m + 3)
        for c in range(COMPS):
            total = (r[c, 2 * m + 2] - first[c]) + (r[c, 2 * m + 3] - second[c])
            for t in range(LANES // 128):
                rest[t, pl.ds((c * 6 + m) * ROWS, ROWS)] = total[:, 128 * t : 128 * t + 128]
        return carry

    lax.fori_loop(0, 6, residue, 0)

    wide_x[:, 24 * EM_PLANES :] = jnp.zeros((LANES // 128, 8, 128), F32)
    pieces = []
    for t in range(COMPS * 6):
        pieces.append(every_other(rest, 16 * t, 8) + every_other(rest, 16 * t + 1, 8))
    for m in range(EM_PLANES):
        for at in (24 * m, 24 * m + 16):
            pieces.append(every_other(wide_x, at, 8) + every_other(wide_x, at + 1, 8))
    pooled = dot_exact_weights(jnp.concatenate(pieces, axis=0), pool_matrix(0.5))
    pooled = [pooled[8 * t : 8 * t + 8] for t in range(len(pieces))]
    for m in range(EM_PLANES):
        centre = 0.25 * pooled[COMPS * 6 + 2 * m]
        em[0, m] = centre
        em[1, m] = pltpu.roll(centre, MID_LANES - 1, 1)
        em[2, m] = pltpu.roll(centre, 1, 1)
        em_side[m] = 0.25 * pooled[COMPS * 6 + 2 * m + 1]
    for m in range(M_PLANES):
        total = tri_x(*[em[0, m + k] for k in range(3)])
        side = tri_x(*[em_side[m + k] for k in range(3)])
        total = tri_y_with(total, up(side, 6), up(side, 4), 5)
        total = total + total + pltpu.roll(total, 1, 1) + pltpu.roll(total, MID_LANES - 1, 1)
        centre = em[0, m + 1]
        c1m[m] = 72.0 * centre + total
        wm[m] = jnp.where(centre > 0.0, DAMPING / (56.0 * centre + total), 0.0)

    rhs, mid, e_mid = {}, {}, {}
    for m in range(6):
        for c in range(COMPS):
            rhs[c, m] = pooled[c * 6 + m]
            mid[c, m] = wm[m + 1] * rhs[c, m]
            e_mid[c, m] = em[0, m + 2] * mid[c, m]
    rows = []
    kept = {}
    for m in range(1, 5):
        parts = []
        for c in range(COMPS):
            v = tri_y(tri_x(mid[c, m - 1], mid[c, m], mid[c, m + 1]))
            ev = tri_y(tri_x(e_mid[c, m - 1], e_mid[c, m], e_mid[c, m + 1]))
            mixed = mixed_z(em[0, m + 2], em[1, m + 2], em[2, m + 2], v, ev)
            parts.append(c1m[m + 1] * mid[c, m] - mixed)
        applied = coupled(parts)
        for c in range(COMPS):
            left_over = rhs[c, m] - applied[c]
            kept[c, m - 1] = left_over
            value = mid[c, m] + wm[m + 1] * left_over
            tile = c * 4 + m - 1
            pack[8 * tile : 8 * tile + 8] = value[:, :128]
    for c in range(COMPS):
        for b in range(2):
            rows.append(kept[c, 2 * b] + kept[c, 2 * b + 1])
    stacked = jnp.concatenate(rows, axis=0)
    lane_box = row_of((MID_LANES, 128))
    column = lane_of((MID_LANES, 128))
    boxes = jnp.where(
        jnp.logical_and(lane_box < Z // 2, lane_box // 64 == column % 2), 1.0, 0.0
    ).astype(F32)
    sums = dot_exact_weights(stacked, boxes)
    line = row_of((48, 128))
    entry = lane_of((48, 128))
    inside = line % 8
    match = jnp.logical_and((line // 8) * 2 + inside // 2 == entry // 2, inside < 4)
    scale = 1.0 / math.sqrt((X // 4) * (Y // 4) * (Z // 4))
    low = jnp.sum(jnp.where(match, sums, 0.0), axis=0, keepdims=True) * scale
    pack[8 * LOW_TILE :] = jnp.broadcast_to(low, (8, 128))


def pack_mid(pack, tiles):
    lane = lane_of((8, 128))
    rims = None
    for n, tile in enumerate(tiles):
        pack[8 * n : 8 * n + 8] = tile[:, :128]
        moved = pltpu.roll(tile[:, 128:], 4 + 8 * n, 1)
        rims = moved if n == 0 else jnp.where(lane < 8 * n, rims, moved)
    pack[8 * len(tiles) :] = rims


def unpack_mid(side, count):
    lane = lane_of((8, 128))
    near = jnp.logical_or(lane < 4, lane >= 124)
    rims = side((slice(8 * count, 8 * count + 8), slice(None)))
    tiles = []
    for n in range(count):
        main = side((slice(8 * n, 8 * n + 8), slice(None)))
        rim = jnp.where(near, pltpu.roll(rims, 124 - 8 * n, 1), 0.0)
        tiles.append(jnp.concatenate([main, rim], axis=1))
    return tiles


def coarse_body(n_z, *refs):
    pack = refs[0]
    got_z = refs[1 : 1 + n_z]
    matrix = refs[1 + n_z]
    gathered = refs[2 + n_z : -5]
    planes, column, pack_even, pack_odd, scratch = refs[-5:]
    place = lax.axis_index("gz")
    left, right = from_sides(got_z, "gz")
    lane = lane_of((8, 128))
    for t in range(LOW_TILE):
        key = (slice(8 * t, 8 * t + 8), slice(None))
        planes[t, :, :128] = pack[key]
        planes[t, :, 128:] = jnp.where(lane < 64, right(key), left(key))

    size = 24
    if gathered:
        rhs = gathered[0][...]
    else:
        mine = pack[8 * LOW_TILE : 8 * LOW_TILE + 8]
        other = got_z[0][8 * LOW_TILE : 8 * LOW_TILE + 8]
        first = jnp.where(place == 0, mine, other)
        second = jnp.where(place == 0, other, mine)
        rhs = jnp.where(lane < size, first, pltpu.roll(second, size, 1))[:1, : 2 * size]
    solved = jnp.sum(matrix[0, 0] * rhs, axis=1, keepdims=True)
    scratch[...] = jnp.zeros(scratch.shape, F32)
    scratch[size : size + solved.shape[0]] = jnp.broadcast_to(solved, (solved.shape[0], 128))
    base = pl.multiple_of(place * size, 8)
    wide = lane_of((16, MID_LANES))
    before, own_a, own_b, after = [
        jnp.concatenate([scratch[pl.ds(base + at, 16, stride=2)]] * 2, axis=1)
        for at in (1, size, size + 1, 2 * size)
    ]
    value = jnp.where(wide < 64, own_a, own_b)
    value = jnp.where(wide < 128, value, jnp.where(wide < 192, after, before))
    value = jnp.where(row_of((16, MID_LANES)) < 12, value, 0.0)
    column[...] = value

    even = is_even("gx")
    row = row_of((8, MID_LANES))
    low, high = [
        [jnp.where(row < 4, planes[c * 4 + p], up(planes[c * 4 + p + 1], 4)) for c in range(COMPS)]
        for p in (0, 2)
    ]
    rest = [value[:8], value[8:]]
    pack_mid(pack_even, [jnp.where(even, b, a) for a, b in zip(low, high)] + rest)
    pack_mid(pack_odd, [jnp.where(even, a, b) for a, b in zip(low, high)] + rest)


MX_TILES = COMPS + 2
MY_TILES = 2 * COMPS + 5
MX_PACK = (MX_TILES + 1) * 8
MY_PACK = (MY_TILES + 1) * 8


def mid_y_body(planes, column, got_a, got_b, wide_planes, columns, pack_even, pack_odd):
    lower, upper = from_sides((got_a, got_b), "gx")
    low_tiles, high_tiles = unpack_mid(lower, MX_TILES), unpack_mid(upper, MX_TILES)
    row = row_of((8, MID_LANES))
    even = is_even("gy")
    below_packs, above_packs = [], []
    for c in range(COMPS):
        tiles = [low_tiles[c], up(low_tiles[c], 4)]
        tiles += [planes[c * 4 + p] for p in range(4)]
        tiles += [high_tiles[c], up(high_tiles[c], 4)]
        for t in range(8):
            wide_planes[c * 8 + t] = tiles[t]
        for h in range(2):
            below = above = None
            for k in range(4):
                tile = tiles[4 * h + k]
                a, b = up(tile, 2 * k), up(tile, 2 * k - 2)
                below = a if k == 0 else jnp.where(row < 2 * k, below, a)
                above = b if k == 0 else jnp.where(row < 2 * k, above, b)
            below_packs.append(below)
            above_packs.append(above)
    columns[:8] = low_tiles[COMPS]
    columns[8:12] = low_tiles[COMPS + 1][:4]
    columns[12:24] = column[:12]
    columns[24:32] = high_tiles[COMPS]
    columns[32:36] = high_tiles[COMPS + 1][:4]
    columns[36:] = jnp.zeros((4, MID_LANES), F32)
    rest = [columns[8 * t : 8 * t + 8] for t in range(5)]
    pairs_of = list(zip(below_packs, above_packs))
    pack_mid(pack_even, [jnp.where(even, a, b) for b, a in pairs_of] + rest)
    pack_mid(pack_odd, [jnp.where(even, b, a) for b, a in pairs_of] + rest)


def finish_body(
    wide_planes, columns, got_a, got_b, r, s1, e_all, c1, w, em, em_side, c1m, wm, prev_d, prev_i,
    precond_out, operated_out, sums, cor, cor_side, mid, big, s2, es2, s3, es3, p, ep, precond,
    operated, sems,
):
    e = e_all.at[:, 2 : 2 + PLANES]
    lower, upper = from_sides((got_a, got_b), "gy")
    row = row_of((8, MID_LANES))

    low_tiles, high_tiles = unpack_mid(lower, MY_TILES), unpack_mid(upper, MY_TILES)
    below = jnp.concatenate(low_tiles[2 * COMPS :], axis=0)
    above = jnp.concatenate(high_tiles[2 * COMPS :], axis=0)
    middle = columns[...]
    for c in range(COMPS):
        for b in range(6):
            at = (b // 2) * 12 + c * 4 + (b % 2) * 2

            def band(source, by):
                return jnp.broadcast_to(source[at + by : at + by + 1], (8, MID_LANES))

            field = jnp.where(row < 6, band(above, 0), band(below, 1))
            field = jnp.where(row < 4, band(middle, 1), field)
            cor[c, b] = jnp.where(row < 2, band(middle, 0), field)
            cor_side[c, b] = jnp.where(row == 0, band(below, 0), band(above, 1))

    def box(m):
        return (m + 1) // 2

    for m in range(M_PLANES):
        parts = []
        for c in range(COMPS):
            near = [cor[c, box(m + k)] for k in range(3)]
            near_side = [cor_side[c, box(m + k)] for k in range(3)]
            e_near = [em[0, m + k] * near[k] for k in range(3)]
            e_side = [em_side[m + k] * near_side[k] for k in range(3)]
            side = tri_x(*near_side)
            v = tri_y_with(tri_x(*near), up(side, 6), up(side, 4), 5)
            side = tri_x(*e_side)
            ev = tri_y_with(tri_x(*e_near), up(side, 6), up(side, 4), 5)
            mixed = mixed_z(em[0, m + 1], em[1, m + 1], em[2, m + 1], v, ev)
            parts.append(c1m[m] * near[1] - mixed)
        applied = coupled(parts)
        for c in range(COMPS):
            tile = wide_planes[c * 8 + m]
            n, k = c * 2 + m // 4, m % 4
            outer = jnp.where(row < 6, up(high_tiles[n], 4 - 2 * k), up(low_tiles[n], 6 - 2 * k))
            tile = jnp.where(row < 4, tile, outer)
            at = (c * 8 + m) * 8
            mid[at : at + 8] = tile + cor[c, box(m + 1)] - wm[m] * applied[c]
    spread = dot_exact_weights(mid[...], spread_matrix())
    for t in range(COMPS * 8):
        piece = spread[8 * t : 8 * t + 8]
        for k in range(LANES // 128):
            tile = piece[:, 128 * k : 128 * k + 128]
            big[k, pl.ds(16 * t, 8, stride=2)] = tile
            big[k, pl.ds(16 * t + 1, 8, stride=2)] = tile

    def add_up(i, carry):
        for c in range(COMPS):
            at = pl.multiple_of((c * 8 + i // 2) * 16, 16)
            more = [big[k, pl.ds(at, 16)] for k in range(LANES // 128)]
            value = s1[c, i] + jnp.concatenate(more, axis=1)
            s2[c, i] = value
            es2[c, i] = e[0, i] * value
        return carry

    lax.fori_loop(1, PLANES - 1, add_up, 0)
    sweep(s2, es2, s3, es3, r, c1, e, w, 2, PLANES - 2)
    sweep(s3, es3, p, ep, r, c1, e, w, 3, PLANES - 3)

    leaving = (
        (precond, precond_out, sems.at[0]),
        (operated, operated_out, sems.at[1]),
    )

    def own(a):
        return a[:Y]

    def image_of(x):
        i = x + RIM
        near = [e[k, i, :Y] for k in range(3)]
        centre = c1[i, :Y]
        owned, parts = [], []
        for c in range(COMPS):
            owned.append(p[c, i, :Y])
            v = own(tri_y(tri_x(p[c, i - 1], p[c, i], p[c, i + 1])))
            ev = own(tri_y(tri_x(ep[c, i - 1], ep[c, i], ep[c, i + 1])))
            parts.append(centre * owned[c] - mixed_z(*near, v, ev))
        return owned, coupled(parts)

    def image(k, carry):
        rz, pp, mix, old = carry
        steps = [2 * k, 2 * k + 1]
        found = [image_of(x) for x in steps]
        for x, (owned, applied) in zip(steps, found):
            for c in range(COMPS):
                own_p, own_a = owned[c][:, :Z], applied[c][:, :Z]
                own_r = r[c, x + RIM, :Y, :Z]
                d, q = prev_d[c, x], prev_i[c, x]
                rz += own_r * own_p
                pp += own_p * own_a
                mix += own_p * q + d * own_a
                old += d * q
                precond[x, c] = own_p
                operated[x, c] = own_a
        part = pl.ds(2 * k, 2)
        for source, target, sem in leaving:
            pltpu.make_async_copy(source.at[part], target.at[part], sem).start()
        return rz, pp, mix, old

    zero = jnp.zeros((Y, Z), F32)
    found = lax.fori_loop(0, X // 2, image, (zero, zero, zero, zero))
    row = row_of((8, 128))
    total = jnp.zeros((8, 128), F32)
    for k, value in enumerate(found):
        line = jnp.sum(value[:, :128] + value[:, 128:], axis=0, keepdims=True)
        total = jnp.where(row == k, jnp.broadcast_to(line, (8, 128)), total)
    total = total + pltpu.roll(total, 64, 1)
    total = total + pltpu.roll(total, 32, 1)
    total = jnp.where(row == lane_of((8, 128)) // 32, total, 0.0)
    sums[...] = jnp.broadcast_to(jnp.sum(total, axis=0, keepdims=True), sums.shape)
    for source, target, sem in leaving:
        pltpu.make_async_copy(source, target, sem).wait()


STEP = 2


def last_body(
    prev_rz, sums, precond_in, operated_in, prev_d, prev_i, sol, res,
    new_s_out, new_r_out, new_d_out, new_i_out, precond, operated, news, in_sems, out_sems,
):
    arriving = []
    for x in range(0, X, STEP):
        part = pl.ds(x, STEP)
        pair = [
            pltpu.make_async_copy(source.at[part], target.at[part], in_sems.at[k, x // STEP])
            for k, (source, target) in enumerate(((precond_in, precond), (operated_in, operated)))
        ]
        for copy in pair:
            copy.start()
        arriving.append(pair)
    total = jnp.sum(sums[...], axis=0, keepdims=True)
    lane = lane_of((1, 128))

    def entry(k):
        return jnp.sum(jnp.where(lane // 32 == k, total, 0.0), axis=1, keepdims=True)

    rz = entry(0)
    beta = rz / prev_rz[0]
    alpha = rz / (entry(1) + beta * (entry(2) + beta * entry(3)))
    beta = jnp.broadcast_to(beta, (Y, Z))
    alpha = jnp.broadcast_to(alpha, (Y, Z))
    leaving = []
    for step, pair in enumerate(arriving):
        for copy in pair:
            copy.wait()
        for x in range(step * STEP, step * STEP + STEP):
            for c in range(COMPS):
                d = precond[x, c] + beta * prev_d[c, x]
                q = operated[x, c] + beta * prev_i[c, x]
                news[2, c, x] = d
                news[3, c, x] = q
                news[0, c, x] = sol[c, x] + alpha * d
                news[1, c, x] = res[c, x] - alpha * q
        part = pl.ds(step * STEP, STEP)
        for k, target in enumerate((new_s_out, new_r_out, new_d_out, new_i_out)):
            copy = pltpu.make_async_copy(
                news.at[k, :, part], target.at[:, part], out_sems.at[k, step]
            )
            copy.start()
            leaving.append(copy)
    for copy in leaving:
        copy.wait()


PLANES = X + 2 * RIM
FIELD = (COMPS, PLANES, ROWS, LANES)
COLS_SHAPE = (40, MID_LANES)


def smooth_outs():
    return [
        shape(*FIELD),
        shape(*FIELD),
        shape(3, E_PLANES, ROWS, LANES),
        shape(PLANES, ROWS, LANES),
        shape(PLANES, ROWS, LANES),
        shape(3, EM_PLANES, 8, MID_LANES),
        shape(EM_PLANES, 8, MID_LANES),
        shape(M_PLANES, 8, MID_LANES),
        shape(M_PLANES, 8, MID_LANES),
        shape(MZ_PACK, 128),
    ]


def smooth_call(n_z):
    return call(
        functools.partial(smooth_body, n_z),
        smooth_outs(),
        scratch=[
            pltpu.VMEM((E_PLANES, 24, LANES), F32),
            pltpu.VMEM((E_PLANES, 24, LANES), F32),
            pltpu.VMEM(FIELD, F32),
            pltpu.VMEM(FIELD, F32),
            pltpu.VMEM(FIELD, F32),
            pltpu.VMEM((LANES // 128, 18 * ROWS, 128), F32),
            pltpu.VMEM((LANES // 128, 24 * EM_PLANES + 8, 128), F32),
        ],
        n_in=6 + n_z,
        vmem=30 << 20,
    )


def finish_call(n_all):
    return call(
        finish_body,
        [shape(X, COMPS, Y, Z), shape(X, COMPS, Y, Z), shape(n_all, 128)],
        scratch=[
            pltpu.VMEM((COMPS, 6, 8, MID_LANES), F32),
            pltpu.VMEM((COMPS, 6, 8, MID_LANES), F32),
            pltpu.VMEM((COMPS * 64, MID_LANES), F32),
            pltpu.VMEM((LANES // 128, COMPS * 128, 128), F32),
        ]
        + [pltpu.VMEM(FIELD, F32)] * 6
        + [pltpu.VMEM((X, COMPS, Y, Z), F32)] * 2
        + [pltpu.SemaphoreType.DMA((2,))],
        n_in=15,
        hbm_out=(0, 1),
        vmem=30 << 20,
    )


def on_device(
    solution,
    residual,
    prev_direction,
    prev_image,
    prev_rz,
    density_index,
    stiffness_table,
    coarse_inverse,
):
    if residual.shape != (COMPS, X, Y, Z):
        raise ValueError(residual.shape)
    block = shape(COMPS, X, Y, Z)
    n_z = 1 if lax.axis_size("gz") == 2 else 2
    n_all = lax.axis_size(ALL)

    res, young, px, qx = call(
        pack_x_body,
        [block, shape(X, Y, Z), shape(X_PACK, Y, Z), shape(X_PACK, Y, Z)],
        n_in=3,
        smem=(0,),
    )(stiffness_table, density_index, residual)
    got_x = swap("gx", px, qx)
    py, qy = call(pack_y_body, [shape(Y_PACK, Y, Z)] * 2, n_in=4)(res, young, *got_x)
    got_y = swap("gy", py, qy, closed=False)
    packs = call(pack_z_body, [shape(Z_PACK, 128)] * n_z, n_in=6)(res, young, *got_x, *got_y)
    got_z = swap("gz", packs[0], packs[-1])

    r, s1, e, c1, w, em, em_side, c1m, wm, pack = smooth_call(n_z)(res, young, *got_x, *got_y, *got_z)

    got_z = swap("gz", pack, pack)
    gathered = []
    if n_z > 1:
        gathered = [lax.all_gather(pack[8 * LOW_TILE, :24], "gz", axis=0, tiled=True)[None]]
    size = coarse_inverse.shape[-1]
    mid_planes, column, px, qx = call(
        functools.partial(coarse_body, n_z),
        [
            shape(LOW_TILE, 8, MID_LANES),
            shape(16, MID_LANES),
            shape(MX_PACK, 128),
            shape(MX_PACK, 128),
        ],
        scratch=[pltpu.VMEM((size + 64, 128), F32)],
        n_in=2 + n_z + len(gathered),
    )(pack, *got_z, coarse_inverse, *gathered)
    got_x = swap("gx", px, qx)
    mid_planes, columns, py, qy = call(
        mid_y_body,
        [
            shape(COMPS * 8, 8, MID_LANES),
            shape(40, MID_LANES),
            shape(MY_PACK, 128),
            shape(MY_PACK, 128),
        ],
        n_in=4,
    )(mid_planes, column, *got_x)
    got_y = swap("gy", py, qy)
    precond, operated, sums = finish_call(n_all)(
        mid_planes, columns, *got_y, r, s1, e, c1, w, em, em_side, c1m, wm, prev_direction, prev_image
    )
    sums = lax.all_to_all(sums, ALL, 0, 0, tiled=True)
    return tuple(
        call(
            last_body,
            [block] * 4,
            scratch=[pltpu.VMEM((X, COMPS, Y, Z), F32)] * 2
            + [pltpu.VMEM((4, COMPS, X, Y, Z), F32)]
            + [pltpu.SemaphoreType.DMA((2, X // STEP)), pltpu.SemaphoreType.DMA((4, X // STEP))],
            n_in=8,
            smem=(0,),
            hbm=(2, 3),
            hbm_out=(0, 1, 2, 3),
        )(
            prev_rz.reshape(1), sums, precond, operated, prev_direction, prev_image, solution, residual
        )
    )


def solution(mesh):
    field = P(None, "gx", "gy", "gz")
    return jax.shard_map(
        on_device,
        mesh=mesh,
        in_specs=(
            field,
            field,
            field,
            field,
            P(),
            P("gx", "gy", "gz"),
            P(),
            P("gx", "gy", None, None),
        ),
        out_specs=(field, field, field, field),
        check_vma=False,
    )
```

time: 72.3 us -> 66.2 us (0.916)
  Pallas kernels: 19 us -> 13.5 us
    pallas_call x2, Pallas kernels: 14.7 us -> 10.5 us  [the longest x1 5.52 us: on_device(): finish_call(n_all)]
    pallas_call x1, Pallas kernels: 2.66 us -> 1.69 us  [on_device(): call(last_body, [block] * 4, scratch=[pltpu.VMEM((X, COMPS, Y, Z), F32)]...]
  transfers between devices with their start and end apart: 11 -> 11, of which waited for: 10 -> 9; matrix products, arithmetic and copies ran while one was open for 0% -> 0% of each run, Pallas kernels for 0% -> 0%
where the time goes in v3:
time: 66.2 us; the launch traced here: 66 us
  waiting for transfers between devices  28.7 us (43%)
  starting transfers between devices  19.9 us (30%)
  Pallas kernels  13.5 us (20%)
  local copies, waits for them, and re-layouts  2.43 us (4%)
  between operations  1.37 us (2%)
    ppermute x6, waiting for transfers between devices, swap(): got_even = lax.ppermute(even_pack, axis, pairs(count, False, closed))  13 us
    ppermute x6, starting transfers between devices, swap(): got_even = lax.ppermute(even_pack, axis, pairs(count, False, closed))  11.3 us
    ppermute x4, waiting for transfers between devices, swap(): return [got_even, lax.ppermute(odd_pack, axis, pairs(count, True, closed))]  9.33 us
    all_to_all x1, waiting for transfers between devices, on_device(): sums = lax.all_to_all(sums, ALL, 0, 0, tiled=True)  6.42 us
    ppermute x4, starting transfers between devices, swap(): return [got_even, lax.ppermute(odd_pack, axis, pairs(count, True, closed))]  5.62 us
    pallas_call x1, Pallas kernels, on_device(): finish_call(n_all)  5.52 us
    pallas_call x1, Pallas kernels, on_device(): smooth_call(n_z)(res, young, *got_x, *got_y, *got_z)  4.95 us
    all_to_all x1, starting transfers between devices, on_device(): sums = lax.all_to_all(sums, ALL, 0, 0, tiled=True)  3.07 us
  transfers between devices with their start and end apart: 11, of which 9 were waited for; matrix products, arithmetic and copies ran while one was open for 0% of the time, Pallas kernels for 0%

profile of v3, /device:TPU:0, one launch (start us, length us, event | category | flops | bytes accessed | tf_op | source)
XLA Modules:
  0.0 66.0 jit_solution(13622223368504689057)
XLA Ops:
  0.6 0.0 copy-start.2
  0.6 0.9 %copy-done.2 = f32[3,8,8,256]{3,2,1,0:T(8,128)S(1)} copy-done((f32[3,8,8,256]{3,2,1,0:T(8,128)S(1)}, f32[3,8,8,256]{3,2,1,0:T(8,128)}, u32[]{:S(2)}) %copy-start.2) | copy-done | bytes 196632
  1.6 0.8 %copy-done.5 = s32[8,8,256]{2,1,0:T(8,128)S(1)} copy-done((s32[8,8,256]{2,1,0:T(8,128)S(1)}, s32[8,8,256]{2,1,0:T(8,128)}, u32[]{:S(2)}) %copy-start.5) | copy-done | bytes 65560
  2.4 0.7 copy-done.7
  3.1 0.6 shard_map.111
  3.7 3.0 %collective-permute-start = (f32[18,8,256]{2,1,0:T(8,128)S(1)}, f32[18,8,256]{2,1,0:T(8,128)S(1)}, u32[]{:S(2)}, u32[]{:S(2)}) collective-permute-start(f32[18,8,256]{2,1,0:T(8,128)S(1)} %get-tuple-element.33), channel_id=1, source_target_pairs={{0,8},{8,0},{16,24},{24,16},{1,9},{9,1},{17,25},{25,17},{2,10},{10... | collective-permute-start | bytes 442376 | tf_op jit(solution)/shard_map/ppermute | solution.py:50
  6.7 1.5 %collective-permute-start.1 = (f32[18,8,256]{2,1,0:T(8,128)S(1)}, f32[18,8,256]{2,1,0:T(8,128)S(1)}, u32[]{:S(2)}, u32[]{:S(2)}) collective-permute-start(f32[18,8,256]{2,1,0:T(8,128)S(1)} %get-tuple-element.34), channel_id=1, source_target_pairs={{0,24},{8,16},{16,8},{24,0},{1,25},{9,17},{17,9},{25,1},{2,26},{10... | collective-permute-start | bytes 442376 | tf_op jit(solution)/shard_map/ppermute | solution.py:53
  8.2 3.0 %collective-permute-done.got_a.xa.refs_2_ = f32[18,8,256]{2,1,0:T(8,128)S(1)} collective-permute-done((f32[18,8,256]{2,1,0:T(8,128)S(1)}, f32[18,8,256]{2,1,0:T(8,128)S(1)}, u32[]{:S(2)}, u32[]{:S(2)}) %collective-permute-start) | collective-permute-done | bytes 147488 | tf_op jit(solution)/shard_map/ppermute | solution.py:50
  11.2 3.7 %collective-permute-done.1.got_b.xb.refs_3_ = f32[18,8,256]{2,1,0:T(8,128)S(1)} collective-permute-done((f32[18,8,256]{2,1,0:T(8,128)S(1)}, f32[18,8,256]{2,1,0:T(8,128)S(1)}, u32[]{:S(2)}, u32[]{:S(2)}) %collective-permute-start.1) | collective-permute-done | bytes 147488 | tf_op jit(solution)/shard_map/ppermute | solution.py:53
  14.9 0.1 shard_map.112
  15.0 1.6 %collective-permute-start.2 = (f32[39,8,256]{2,1,0:T(8,128)S(1)}, f32[39,8,256]{2,1,0:T(8,128)S(1)}, u32[]{:S(2)}, u32[]{:S(2)}) collective-permute-start(f32[39,8,256]{2,1,0:T(8,128)S(1)} %get-tuple-element.35), channel_id=1, source_target_pairs={{0,2},{2,0},{4,6},{6,4},{1,3},{3,1},{5,7},{7,5},{8,10},{10,8},{12,... | collective-permute-start | bytes 958472 | tf_op jit(solution)/shard_map/ppermute | solution.py:50
  16.7 0.8 %collective-permute-start.3 = (f32[39,8,256]{2,1,0:T(8,128)S(1)}, f32[39,8,256]{2,1,0:T(8,128)S(1)}, u32[]{:S(2)}, u32[]{:S(2)}) collective-permute-start(f32[39,8,256]{2,1,0:T(8,128)S(1)} %get-tuple-element.36), channel_id=1, source_target_pairs={{2,4},{4,2},{3,5},{5,3},{10,12},{12,10},{11,13},{13,11},{18,20},{2... | collective-permute-start | bytes 958472 | tf_op jit(solution)/shard_map/ppermute | solution.py:53
  17.5 6.0 %collective-permute-done.2.ya.refs_4_ = f32[39,8,256]{2,1,0:T(8,128)S(1)} collective-permute-done((f32[39,8,256]{2,1,0:T(8,128)S(1)}, f32[39,8,256]{2,1,0:T(8,128)S(1)}, u32[]{:S(2)}, u32[]{:S(2)}) %collective-permute-start.2) | collective-permute-done | bytes 319520 | tf_op jit(solution)/shard_map/ppermute | solution.py:50
  23.5 0.2 shard_map.113
  23.7 0.1 collective-permute-start.4
  23.8 1.2 %collective-permute-done.4.refs_6_ = f32[80,128]{1,0:T(8,128)S(1)} collective-permute-done((f32[80,128]{1,0:T(8,128)S(1)}, f32[80,128]{1,0:T(8,128)S(1)}, u32[]{:S(2)}, u32[]{:S(2)}) %collective-permute-start.4) | collective-permute-done | bytes 40992 | tf_op jit(solution)/shard_map/ppermute | solution.py:50
  25.0 4.9 %shard_map.114 = (f32[3,16,16,384]{3,2,1,0:T(8,128)S(1)}, f32[3,16,16,384]{3,2,1,0:T(8,128)S(1)}, f32[3,20,16,384]{3,2,1,0:T(8,128)S(1)}, f32[16,16,384]{2,1,0:T...) custom-call(f32[3,8,8,256]{3,2,1,0:T(8,128)S(1)} %get-tuple-element., ...), custom_call_target="tpu_custom_call" | custom-call | tf_op jit(solution)/shard_map/pallas_call | solution.py:833
  30.0 0.2 collective-permute-start.5
  30.2 1.1 %collective-permute-done.5.refs_1_ = f32[104,128]{1,0:T(8,128)S(1)} collective-permute-done((f32[104,128]{1,0:T(8,128)S(1)}, f32[104,128]{1,0:T(8,128)S(1)}, u32[]{:S(2)}, u32[]{:S(2)}) %collective-permute-start.5) | collective-permute-done | bytes 53280 | tf_op jit(solution)/shard_map/ppermute | solution.py:50
  31.3 0.2 shard_map.115
  31.5 1.5 %collective-permute-start.6 = (f32[48,128]{1,0:T(8,128)S(1)}, f32[48,128]{1,0:T(8,128)S(1)}, u32[]{:S(2)}, u32[]{:S(2)}) collective-permute-start(f32[48,128]{1,0:T(8,128)S(1)} %get-tuple-element.40), channel_id=1, source_target_pairs={{0,8},{8,0},{16,24},{24,16},{1,9},{9,1},{17,25},{25,17},{2,10},{10... | collective-permute-start | bytes 73736 | tf_op jit(solution)/shard_map/ppermute | solution.py:50
  33.0 0.7 %collective-permute-start.7 = (f32[48,128]{1,0:T(8,128)S(1)}, f32[48,128]{1,0:T(8,128)S(1)}, u32[]{:S(2)}, u32[]{:S(2)}) collective-permute-start(f32[48,128]{1,0:T(8,128)S(1)} %get-tuple-element.41), channel_id=1, source_target_pairs={{0,24},{8,16},{16,8},{24,0},{1,25},{9,17},{17,9},{25,1},{2,26},{10... | collective-permute-start | bytes 73736 | tf_op jit(solution)/shard_map/ppermute | solution.py:53
  33.7 1.6 %collective-permute-done.6.got_a = f32[48,128]{1,0:T(8,128)S(1)} collective-permute-done((f32[48,128]{1,0:T(8,128)S(1)}, f32[48,128]{1,0:T(8,128)S(1)}, u32[]{:S(2)}, u32[]{:S(2)}) %collective-permute-start.6) | collective-permute-done | bytes 24608 | tf_op jit(solution)/shard_map/ppermute | solution.py:50
  35.3 2.4 %collective-permute-done.7.got_b = f32[48,128]{1,0:T(8,128)S(1)} collective-permute-done((f32[48,128]{1,0:T(8,128)S(1)}, f32[48,128]{1,0:T(8,128)S(1)}, u32[]{:S(2)}, u32[]{:S(2)}) %collective-permute-start.7) | collective-permute-done | bytes 24608 | tf_op jit(solution)/shard_map/ppermute | solution.py:53
  37.7 0.2 shard_map.116
  37.9 4.8 %collective-permute-start.8 = (f32[96,128]{1,0:T(8,128)S(1)}, f32[96,128]{1,0:T(8,128)S(1)}, u32[]{:S(2)}, u32[]{:S(2)}) collective-permute-start(f32[96,128]{1,0:T(8,128)S(1)} %get-tuple-element.44), channel_id=1, source_target_pairs={{0,2},{2,0},{4,6},{6,4},{1,3},{3,1},{5,7},{7,5},{8,10},{10,8},{12,... | collective-permute-start | bytes 147464 | tf_op jit(solution)/shard_map/ppermute | solution.py:50
  42.7 2.6 %collective-permute-start.9 = (f32[96,128]{1,0:T(8,128)S(1)}, f32[96,128]{1,0:T(8,128)S(1)}, u32[]{:S(2)}, u32[]{:S(2)}) collective-permute-start(f32[96,128]{1,0:T(8,128)S(1)} %get-tuple-element.45), channel_id=1, source_target_pairs={{0,6},{2,4},{4,2},{6,0},{1,7},{3,5},{5,3},{7,1},{8,14},{10,12},{12... | collective-permute-start | bytes 147464 | tf_op jit(solution)/shard_map/ppermute | solution.py:53
  45.4 3.3 %collective-permute-done.9.got_b = f32[96,128]{1,0:T(8,128)S(1)} collective-permute-done((f32[96,128]{1,0:T(8,128)S(1)}, f32[96,128]{1,0:T(8,128)S(1)}, u32[]{:S(2)}, u32[]{:S(2)}) %collective-permute-start.9) | collective-permute-done | bytes 49184 | tf_op jit(solution)/shard_map/ppermute | solution.py:53
  48.6 5.5 %shard_map.117 = (f32[8,3,8,256]{3,2,1,0:T(8,128)S(1)}, f32[8,3,8,256]{3,2,1,0:T(8,128)S(1)}, f32[32,128]{1,0:T(8,128)}) custom-call(f32[24,8,256]{2,1,0:T(8,128)S(1)} %get-tuple-element.42.wide_planes, f32[40,256]{1,0:T(8,128)S(1)} %get-tuple-element.43.columns, f32[96,128]{1,0:T(8,128)S(1)} %collective-permute-done.8.got_a, ...), custom_call_target="tpu_custom_call" | custom-call | tf_op jit(solution)/shard_map/pallas_call | solution.py:863
  54.1 3.1 %all-to-all-start = ((f32[32,1,128]{2,1,0:T(1,128)}), f32[32,1,128]{2,1,0:T(1,128)S(1)}, u32[]{:S(2)}, u32[]{:S(2)}) async-start(f32[32,1,128]{2,1,0:T(1,128)} %bitcast.2), calls=%async_computation | async-start | bytes 32768 | tf_op jit(solution)/shard_map/all_to_all | solution.py:866
  57.9 6.4 %all-to-all-done = f32[32,1,128]{2,1,0:T(1,128)S(1)} async-done(((f32[32,1,128]{2,1,0:T(1,128)}), f32[32,1,128]{2,1,0:T(1,128)S(1)}, u32[]{:S(2)}, u32[]{:S(2)}) %all-to-all-start) | async-done | bytes 16416 | tf_op jit(solution)/shard_map/all_to_all | solution.py:866
  64.3 1.7 %shard_map.118 = (f32[3,8,8,256]{3,2,1,0:T(8,128)}, f32[3,8,8,256]{3,2,1,0:T(8,128)}, f32[3,8,8,256]{3,2,1,0:T(8,128)}, f32[3,8,8,256]{3,2,1,0:T(8,128)}) custom-call(f32[1]{0:T(128)} %bitcast.5.prev_rz, f32[32,128]{1,0:T(8,128)S(1)} %bitcast.6, f32[8,3,8,256]{3,2,1,0:T(8,128)S(1)} %get-tuple-element.56.precond_in, ...), custom_call_target="tpu_custom_call" | custom-call | tf_op jit(solution)/shard_map/pallas_call | solution.py:868
  (14 shorter events, 0.0 us)
Async XLA Ops:
  0.6 0.9 %copy-start.2 = (f32[3,8,8,256]{3,2,1,0:T(8,128)S(1)}, f32[3,8,8,256]{3,2,1,0:T(8,128)}, u32[]{:S(2)}) copy-start(f32[3,8,8,256]{3,2,1,0:T(8,128)} %res.1) | copy-start | bytes 589828
  1.6 0.8 %copy-start.5 = (s32[8,8,256]{2,1,0:T(8,128)S(1)}, s32[8,8,256]{2,1,0:T(8,128)}, u32[]{:S(2)}) copy-start(s32[8,8,256]{2,1,0:T(8,128)} %index.1) | copy-start | bytes 196612
  2.4 0.7 copy-start.7
  3.7 7.5 %collective-permute-start = (f32[18,8,256]{2,1,0:T(8,128)S(1)}, f32[18,8,256]{2,1,0:T(8,128)S(1)}, u32[]{:S(2)}, u32[]{:S(2)}) collective-permute-start(f32[18,8,256]{2,1,0:T(8,128)S(1)} %get-tuple-element.33), channel_id=1, source_target_pairs={{0,8},{8,0},{16,24},{24,16},{1,9},{9,1},{17,25},{25,17},{2,10},{10... | collective-permute-start | bytes 442376 | tf_op jit(solution)/shard_map/ppermute | solution.py:50
  6.7 8.2 %collective-permute-start.1 = (f32[18,8,256]{2,1,0:T(8,128)S(1)}, f32[18,8,256]{2,1,0:T(8,128)S(1)}, u32[]{:S(2)}, u32[]{:S(2)}) collective-permute-start(f32[18,8,256]{2,1,0:T(8,128)S(1)} %get-tuple-element.34), channel_id=1, source_target_pairs={{0,24},{8,16},{16,8},{24,0},{1,25},{9,17},{17,9},{25,1},{2,26},{10... | collective-permute-start | bytes 442376 | tf_op jit(solution)/shard_map/ppermute | solution.py:53
  15.0 8.5 %collective-permute-start.2 = (f32[39,8,256]{2,1,0:T(8,128)S(1)}, f32[39,8,256]{2,1,0:T(8,128)S(1)}, u32[]{:S(2)}, u32[]{:S(2)}) collective-permute-start(f32[39,8,256]{2,1,0:T(8,128)S(1)} %get-tuple-element.35), channel_id=1, source_target_pairs={{0,2},{2,0},{4,6},{6,4},{1,3},{3,1},{5,7},{7,5},{8,10},{10,8},{12,... | collective-permute-start | bytes 958472 | tf_op jit(solution)/shard_map/ppermute | solution.py:50
  16.7 14.6 %copy-start.6 = (f32[1,1,48,48]{3,2,1,0:T(8,128)S(1)}, f32[1,1,48,48]{3,2,1,0:T(8,128)}, u32[]{:S(2)}) copy-start(f32[1,1,48,48]{3,2,1,0:T(8,128)} %refs_2_.1) | copy-start | bytes 27652
  16.7 31.9 %copy-start = (f32[3,8,8,256]{3,2,1,0:T(8,128)S(1)}, f32[3,8,8,256]{3,2,1,0:T(8,128)}, u32[]{:S(2)}) copy-start(f32[3,8,8,256]{3,2,1,0:T(8,128)} %prev_d.3) | copy-start | bytes 589828
  16.7 31.9 %copy-start.1 = (f32[3,8,8,256]{3,2,1,0:T(8,128)S(1)}, f32[3,8,8,256]{3,2,1,0:T(8,128)}, u32[]{:S(2)}) copy-start(f32[3,8,8,256]{3,2,1,0:T(8,128)} %prev_i.3) | copy-start | bytes 589828
  16.7 6.8 %collective-permute-start.3 = (f32[39,8,256]{2,1,0:T(8,128)S(1)}, f32[39,8,256]{2,1,0:T(8,128)S(1)}, u32[]{:S(2)}, u32[]{:S(2)}) collective-permute-start(f32[39,8,256]{2,1,0:T(8,128)S(1)} %get-tuple-element.36), channel_id=1, source_target_pairs={{2,4},{4,2},{3,5},{5,3},{10,12},{12,10},{11,13},{13,11},{18,20},{2... | collective-permute-start | bytes 958472 | tf_op jit(solution)/shard_map/ppermute | solution.py:53
  23.7 1.3 %collective-permute-start.4 = (f32[80,128]{1,0:T(8,128)S(1)}, f32[80,128]{1,0:T(8,128)S(1)}, u32[]{:S(2)}, u32[]{:S(2)}) collective-permute-start(f32[80,128]{1,0:T(8,128)S(1)} %shard_map.113), channel_id=1, source_target_pairs={{0,1},{1,0},{2,3},{3,2},{4,5},{5,4},{6,7},{7,6},{8,9},{9,8},{10,11... | collective-permute-start | bytes 122888 | tf_op jit(solution)/shard_map/ppermute | solution.py:50
  30.0 1.3 %collective-permute-start.5 = (f32[104,128]{1,0:T(8,128)S(1)}, f32[104,128]{1,0:T(8,128)S(1)}, u32[]{:S(2)}, u32[]{:S(2)}) collective-permute-start(f32[104,128]{1,0:T(8,128)S(1)} %get-tuple-element.37.refs_0_), channel_id=1, source_target_pairs={{0,1},{1,0},{2,3},{3,2},{4,5},{5,4},{6,7},{7,6},{8,9},{9,8},{10,11... | collective-permute-start | bytes 159752 | tf_op jit(solution)/shard_map/ppermute | solution.py:50
  31.5 3.8 %collective-permute-start.6 = (f32[48,128]{1,0:T(8,128)S(1)}, f32[48,128]{1,0:T(8,128)S(1)}, u32[]{:S(2)}, u32[]{:S(2)}) collective-permute-start(f32[48,128]{1,0:T(8,128)S(1)} %get-tuple-element.40), channel_id=1, source_target_pairs={{0,8},{8,0},{16,24},{24,16},{1,9},{9,1},{17,25},{25,17},{2,10},{10... | collective-permute-start | bytes 73736 | tf_op jit(solution)/shard_map/ppermute | solution.py:50
  33.0 4.7 %collective-permute-start.7 = (f32[48,128]{1,0:T(8,128)S(1)}, f32[48,128]{1,0:T(8,128)S(1)}, u32[]{:S(2)}, u32[]{:S(2)}) collective-permute-start(f32[48,128]{1,0:T(8,128)S(1)} %get-tuple-element.41), channel_id=1, source_target_pairs={{0,24},{8,16},{16,8},{24,0},{1,25},{9,17},{17,9},{25,1},{2,26},{10... | collective-permute-start | bytes 73736 | tf_op jit(solution)/shard_map/ppermute | solution.py:53
  37.9 7.4 %collective-permute-start.8 = (f32[96,128]{1,0:T(8,128)S(1)}, f32[96,128]{1,0:T(8,128)S(1)}, u32[]{:S(2)}, u32[]{:S(2)}) collective-permute-start(f32[96,128]{1,0:T(8,128)S(1)} %get-tuple-element.44), channel_id=1, source_target_pairs={{0,2},{2,0},{4,6},{6,4},{1,3},{3,1},{5,7},{7,5},{8,10},{10,8},{12,... | collective-permute-start | bytes 147464 | tf_op jit(solution)/shard_map/ppermute | solution.py:50
  42.7 5.9 %collective-permute-start.9 = (f32[96,128]{1,0:T(8,128)S(1)}, f32[96,128]{1,0:T(8,128)S(1)}, u32[]{:S(2)}, u32[]{:S(2)}) collective-permute-start(f32[96,128]{1,0:T(8,128)S(1)} %get-tuple-element.45), channel_id=1, source_target_pairs={{0,6},{2,4},{4,2},{6,0},{1,7},{3,5},{5,3},{7,1},{8,14},{10,12},{12... | collective-permute-start | bytes 147464 | tf_op jit(solution)/shard_map/ppermute | solution.py:53
  48.6 15.7 %copy-start.3 = (f32[3,8,8,256]{3,2,1,0:T(8,128)S(1)}, f32[3,8,8,256]{3,2,1,0:T(8,128)}, u32[]{:S(2)}) copy-start(f32[3,8,8,256]{3,2,1,0:T(8,128)} %res.1) | copy-start | bytes 589828
  48.6 15.7 %copy-start.4 = (f32[3,8,8,256]{3,2,1,0:T(8,128)S(1)}, f32[3,8,8,256]{3,2,1,0:T(8,128)}, u32[]{:S(2)}) copy-start(f32[3,8,8,256]{3,2,1,0:T(8,128)} %sol.1) | copy-start | bytes 589828
  54.1 10.2 %all-to-all-start = ((f32[32,1,128]{2,1,0:T(1,128)}), f32[32,1,128]{2,1,0:T(1,128)S(1)}, u32[]{:S(2)}, u32[]{:S(2)}) async-start(f32[32,1,128]{2,1,0:T(1,128)} %bitcast.2), calls=%async_computation | async-start | bytes 32768 | tf_op jit(solution)/shard_map/all_to_all | solution.py:866

commit v4 on v3

--- a/solution.py
+++ b/solution.py
@@ -38,6 +38,14 @@
     )
 
 
+def in_hbm(a):
+    return pltpu.with_memory_space_constraint(a, pltpu.HBM)
+
+
+def in_vmem(a):
+    return pltpu.with_memory_space_constraint(a, pltpu.VMEM)
+
+
 def pairs(count, odd, closed):
     if not odd:
         return [(i, i ^ 1) for i in range(count)]
@@ -107,6 +115,12 @@
 
 def tri_x(before, centre, after):
     return before + after + (centre + centre)
+
+
+def tree_sum(terms):
+    while len(terms) > 1:
+        terms = [sum(terms[k : k + 2]) for k in range(0, len(terms), 2)]
+    return terms[0]
 
 
 def coupled(parts):
@@ -167,13 +181,21 @@
 Z_PACK = -(-Z_TILES // 16) * 8
 
 
-def pack_x_body(table, index, res_in, res, young, pack_even, pack_odd):
-    res[...] = res_in[...]
+def pack_x_body(table_in, index_in, res_in, res, young, pack_even, pack_odd, table, index, sems):
+    copies = [
+        pltpu.make_async_copy(source, target, sems.at[k])
+        for k, (source, target) in enumerate(((table_in, table), (index_in, index), (res_in, res)))
+    ]
+    for copy in copies:
+        copy.start()
+    copies[0].wait()
+    copies[1].wait()
     levels = index[...]
     value = jnp.zeros(levels.shape, F32)
     for level in range(table.shape[0]):
         value = jnp.where(levels == level, table[level], value)
     young[...] = value
+    copies[2].wait()
     high_first = jnp.where(is_even("gx"), 1, 0)
     for pack, high in ((pack_even, high_first), (pack_odd, 1 - high_first)):
         for c in range(COMPS):
@@ -571,8 +593,7 @@
 
 def finish_body(
     wide_planes, columns, got_a, got_b, r, s1, e_all, c1, w, em, em_side, c1m, wm, prev_d, prev_i,
-    precond_out, operated_out, sums, cor, cor_side, mid, big, s2, es2, s3, es3, p, ep, precond,
-    operated, sems,
+    precond, operated, sums, cor, cor_side, mid, big, s2, es2, s3, es3, p, ep,
 ):
     e = e_all.at[:, 2 : 2 + PLANES]
     lower, upper = from_sides((got_a, got_b), "gy")
@@ -639,10 +660,6 @@
     sweep(s2, es2, s3, es3, r, c1, e, w, 2, PLANES - 2)
     sweep(s3, es3, p, ep, r, c1, e, w, 3, PLANES - 3)
 
-    leaving = (
-        (precond, precond_out, sems.at[0]),
-        (operated, operated_out, sems.at[1]),
-    )
 
     def own(a):
         return a[:Y]
@@ -660,27 +677,24 @@
         return owned, coupled(parts)
 
     def image(k, carry):
-        rz, pp, mix, old = carry
         steps = [2 * k, 2 * k + 1]
         found = [image_of(x) for x in steps]
         for x, (owned, applied) in zip(steps, found):
             for c in range(COMPS):
-                own_p, own_a = owned[c][:, :Z], applied[c][:, :Z]
-                own_r = r[c, x + RIM, :Y, :Z]
-                d, q = prev_d[c, x], prev_i[c, x]
-                rz += own_r * own_p
-                pp += own_p * own_a
-                mix += own_p * q + d * own_a
-                old += d * q
-                precond[x, c] = own_p
-                operated[x, c] = own_a
-        part = pl.ds(2 * k, 2)
-        for source, target, sem in leaving:
-            pltpu.make_async_copy(source.at[part], target.at[part], sem).start()
-        return rz, pp, mix, old
-
-    zero = jnp.zeros((Y, Z), F32)
-    found = lax.fori_loop(0, X // 2, image, (zero, zero, zero, zero))
+                precond[x, c] = owned[c][:, :Z]
+                operated[x, c] = applied[c][:, :Z]
+        return carry
+
+    lax.fori_loop(0, X // 2, image, 0)
+    found = [[], [], [], []]
+    for x in range(X):
+        for c in range(COMPS):
+            own_p, own_a = precond[x, c], operated[x, c]
+            d, q = prev_d[c, x], prev_i[c, x]
+            terms = (r[c, x + RIM, :Y, :Z] * own_p, own_p * own_a, own_p * q + d * own_a, d * q)
+            for kept, term in zip(found, terms):
+                kept.append(term)
+    found = [tree_sum(kept) for kept in found]
     row = row_of((8, 128))
     total = jnp.zeros((8, 128), F32)
     for k, value in enumerate(found):
@@ -690,27 +704,15 @@
     total = total + pltpu.roll(total, 32, 1)
     total = jnp.where(row == lane_of((8, 128)) // 32, total, 0.0)
     sums[...] = jnp.broadcast_to(jnp.sum(total, axis=0, keepdims=True), sums.shape)
-    for source, target, sem in leaving:
-        pltpu.make_async_copy(source, target, sem).wait()
 
 
 STEP = 2
 
 
 def last_body(
-    prev_rz, sums, precond_in, operated_in, prev_d, prev_i, sol, res,
-    new_s_out, new_r_out, new_d_out, new_i_out, precond, operated, news, in_sems, out_sems,
+    prev_rz, sums, precond, operated, prev_d, prev_i, sol, res,
+    new_s_out, new_r_out, new_d_out, new_i_out, news, out_sems,
 ):
-    arriving = []
-    for x in range(0, X, STEP):
-        part = pl.ds(x, STEP)
-        pair = [
-            pltpu.make_async_copy(source.at[part], target.at[part], in_sems.at[k, x // STEP])
-            for k, (source, target) in enumerate(((precond_in, precond), (operated_in, operated)))
-        ]
-        for copy in pair:
-            copy.start()
-        arriving.append(pair)
     total = jnp.sum(sums[...], axis=0, keepdims=True)
     lane = lane_of((1, 128))
 
@@ -723,9 +725,7 @@
     beta = jnp.broadcast_to(beta, (Y, Z))
     alpha = jnp.broadcast_to(alpha, (Y, Z))
     leaving = []
-    for step, pair in enumerate(arriving):
-        for copy in pair:
-            copy.wait()
+    for step in range(X // STEP):
         for x in range(step * STEP, step * STEP + STEP):
             for c in range(COMPS):
                 d = precond[x, c] + beta * prev_d[c, x]
@@ -786,18 +786,15 @@
 def finish_call(n_all):
     return call(
         finish_body,
-        [shape(X, COMPS, Y, Z), shape(X, COMPS, Y, Z), shape(n_all, 128)],
+        [pltpu.VMEM((X, COMPS, Y, Z), F32)] * 2 + [shape(n_all, 128)],
         scratch=[
             pltpu.VMEM((COMPS, 6, 8, MID_LANES), F32),
             pltpu.VMEM((COMPS, 6, 8, MID_LANES), F32),
             pltpu.VMEM((COMPS * 64, MID_LANES), F32),
             pltpu.VMEM((LANES // 128, COMPS * 128, 128), F32),
         ]
-        + [pltpu.VMEM(FIELD, F32)] * 6
-        + [pltpu.VMEM((X, COMPS, Y, Z), F32)] * 2
-        + [pltpu.SemaphoreType.DMA((2,))],
+        + [pltpu.VMEM(FIELD, F32)] * 6,
         n_in=15,
-        hbm_out=(0, 1),
         vmem=30 << 20,
     )
 
@@ -821,9 +818,14 @@
     res, young, px, qx = call(
         pack_x_body,
         [block, shape(X, Y, Z), shape(X_PACK, Y, Z), shape(X_PACK, Y, Z)],
+        scratch=[
+            pltpu.SMEM(stiffness_table.shape, F32),
+            pltpu.VMEM((X, Y, Z), jnp.int32),
+            pltpu.SemaphoreType.DMA((3,)),
+        ],
         n_in=3,
-        smem=(0,),
-    )(stiffness_table, density_index, residual)
+        hbm=(0, 1, 2),
+    )(*[in_hbm(a) for a in (stiffness_table, density_index, residual)])
     got_x = swap("gx", px, qx)
     py, qy = call(pack_y_body, [shape(Y_PACK, Y, Z)] * 2, n_in=4)(res, young, *got_x)
     got_y = swap("gy", py, qy, closed=False)
@@ -859,21 +861,22 @@
         ],
         n_in=4,
     )(mid_planes, column, *got_x)
-    got_y = swap("gy", py, qy)
+    got_y = swap("gy", py, qy, closed=False)
     precond, operated, sums = finish_call(n_all)(
         mid_planes, columns, *got_y, r, s1, e, c1, w, em, em_side, c1m, wm, prev_direction, prev_image
     )
+    precond, operated = in_vmem(precond), in_vmem(operated)
     sums = lax.all_to_all(sums, ALL, 0, 0, tiled=True)
     return tuple(
         call(
             last_body,
             [block] * 4,
-            scratch=[pltpu.VMEM((X, COMPS, Y, Z), F32)] * 2
-            + [pltpu.VMEM((4, COMPS, X, Y, Z), F32)]
-            + [pltpu.SemaphoreType.DMA((2, X // STEP)), pltpu.SemaphoreType.DMA((4, X // STEP))],
+            scratch=[
+                pltpu.VMEM((4, COMPS, X, Y, Z), F32),
+                pltpu.SemaphoreType.DMA((4, X // STEP)),
+            ],
             n_in=8,
             smem=(0,),
-            hbm=(2, 3),
             hbm_out=(0, 1, 2, 3),
         )(
             prev_rz.reshape(1), sums, precond, operated, prev_direction, prev_image, solution, residual

time: 66.2 us -> 61.7 us (0.932)
  local copies, waits for them, and re-layouts: 2.43 us -> 0.02 us
  waiting for transfers between devices: 28.7 us -> 26.9 us
  Pallas kernels: 13.5 us -> 12.8 us
    ppermute x4, waiting for transfers between devices: 9.33 us -> 6.09 us  [swap(): return [got_even, lax.ppermute(odd_pack, axis, pairs(count, True, closed))]]
    all_to_all x1, starting transfers between devices: 3.07 us -> 5.51 us  [on_device(): sums = lax.all_to_all(sums, ALL, 0, 0, tiled=True)]
    unnamed x16 -> x10, local copies, waits for them, and re-layouts: 2.43 us -> 0.02 us
    ppermute x4, starting transfers between devices: 5.62 us -> 3.64 us  [swap(): return [got_even, lax.ppermute(odd_pack, axis, pairs(count, True, closed))]]
    ppermute x6, waiting for transfers between devices: 13 us -> 14.4 us  [swap(): got_even = lax.ppermute(even_pack, axis, pairs(count, False, closed))]
where the time goes in v4:
time: 61.7 us; the launch traced here: 61.5 us
  waiting for transfers between devices  26.9 us (44%)
  starting transfers between devices  20.4 us (33%)
  Pallas kernels  12.8 us (21%)
  between operations  1.37 us (2%)
    ppermute x6, waiting for transfers between devices, swap(): got_even = lax.ppermute(even_pack, axis, pairs(count, False, closed))  14.4 us
    ppermute x6, starting transfers between devices, swap(): got_even = lax.ppermute(even_pack, axis, pairs(count, False, closed))  11.3 us
    all_to_all x1, waiting for transfers between devices, on_device(): sums = lax.all_to_all(sums, ALL, 0, 0, tiled=True)  6.42 us
    ppermute x4, waiting for transfers between devices, swap(): return [got_even, lax.ppermute(odd_pack, axis, pairs(count, True, closed))]  6.09 us
    all_to_all x1, starting transfers between devices, on_device(): sums = lax.all_to_all(sums, ALL, 0, 0, tiled=True)  5.51 us
    pallas_call x1, Pallas kernels, on_device(): finish_call(n_all)  5.04 us
    pallas_call x1, Pallas kernels, on_device(): smooth_call(n_z)(res, young, *got_x, *got_y, *got_z)  4.95 us
    ppermute x4, starting transfers between devices, swap(): return [got_even, lax.ppermute(odd_pack, axis, pairs(count, True, closed))]  3.64 us
  transfers between devices with their start and end apart: 11, of which 9 were waited for; matrix products, arithmetic and copies ran while one was open for 0% of the time, Pallas kernels for 0%

profile of v4, /device:TPU:0, one launch (start us, length us, event | category | flops | bytes accessed | tf_op | source)
XLA Modules:
  0.0 61.5 jit_solution(6343581652656292933)
XLA Ops:
  0.6 1.0 %shard_map.111 = (f32[3,8,8,256]{3,2,1,0:T(8,128)S(1)}, f32[8,8,256]{2,1,0:T(8,128)S(1)}, f32[18,8,256]{2,1,0:T(8,128)S(1)}, f32[18,8,256]{2,1,0:T(8,128)S(1)}) custom-call(f32[16]{0:T(128)} %table_in.1, s32[8,8,256]{2,1,0:T(8,128)} %index_in.1, f32[3,8,8,256]{3,2,1,0:T(8,128)} %res.1), custom_call_target="tpu_custom_call" | custom-call | tf_op jit(solution)/shard_map/pallas_call | solution.py:818
  1.7 3.0 %collective-permute-start = (f32[18,8,256]{2,1,0:T(8,128)S(1)}, f32[18,8,256]{2,1,0:T(8,128)S(1)}, u32[]{:S(2)}, u32[]{:S(2)}) collective-permute-start(f32[18,8,256]{2,1,0:T(8,128)S(1)} %get-tuple-element.33), channel_id=1, source_target_pairs={{0,8},{8,0},{16,24},{24,16},{1,9},{9,1},{17,25},{25,17},{2,10},{10... | collective-permute-start | bytes 442376 | tf_op jit(solution)/shard_map/ppermute | solution.py:58
  4.7 1.5 %collective-permute-start.1 = (f32[18,8,256]{2,1,0:T(8,128)S(1)}, f32[18,8,256]{2,1,0:T(8,128)S(1)}, u32[]{:S(2)}, u32[]{:S(2)}) collective-permute-start(f32[18,8,256]{2,1,0:T(8,128)S(1)} %get-tuple-element.34), channel_id=1, source_target_pairs={{0,24},{8,16},{16,8},{24,0},{1,25},{9,17},{17,9},{25,1},{2,26},{10... | collective-permute-start | bytes 442376 | tf_op jit(solution)/shard_map/ppermute | solution.py:61
  6.1 3.0 %collective-permute-done.got_a.xa.refs_2_ = f32[18,8,256]{2,1,0:T(8,128)S(1)} collective-permute-done((f32[18,8,256]{2,1,0:T(8,128)S(1)}, f32[18,8,256]{2,1,0:T(8,128)S(1)}, u32[]{:S(2)}, u32[]{:S(2)}) %collective-permute-start) | collective-permute-done | bytes 147488 | tf_op jit(solution)/shard_map/ppermute | solution.py:58
  9.2 3.7 %collective-permute-done.1.got_b.xb.refs_3_ = f32[18,8,256]{2,1,0:T(8,128)S(1)} collective-permute-done((f32[18,8,256]{2,1,0:T(8,128)S(1)}, f32[18,8,256]{2,1,0:T(8,128)S(1)}, u32[]{:S(2)}, u32[]{:S(2)}) %collective-permute-start.1) | collective-permute-done | bytes 147488 | tf_op jit(solution)/shard_map/ppermute | solution.py:61
  12.9 0.1 shard_map.112
  13.0 1.6 %collective-permute-start.2 = (f32[39,8,256]{2,1,0:T(8,128)S(1)}, f32[39,8,256]{2,1,0:T(8,128)S(1)}, u32[]{:S(2)}, u32[]{:S(2)}) collective-permute-start(f32[39,8,256]{2,1,0:T(8,128)S(1)} %get-tuple-element.35), channel_id=1, source_target_pairs={{0,2},{2,0},{4,6},{6,4},{1,3},{3,1},{5,7},{7,5},{8,10},{10,8},{12,... | collective-permute-start | bytes 958472 | tf_op jit(solution)/shard_map/ppermute | solution.py:58
  14.6 0.8 %collective-permute-start.3 = (f32[39,8,256]{2,1,0:T(8,128)S(1)}, f32[39,8,256]{2,1,0:T(8,128)S(1)}, u32[]{:S(2)}, u32[]{:S(2)}) collective-permute-start(f32[39,8,256]{2,1,0:T(8,128)S(1)} %get-tuple-element.36), channel_id=1, source_target_pairs={{2,4},{4,2},{3,5},{5,3},{10,12},{12,10},{11,13},{13,11},{18,20},{2... | collective-permute-start | bytes 958472 | tf_op jit(solution)/shard_map/ppermute | solution.py:61
  15.4 6.0 %collective-permute-done.2.ya.refs_4_ = f32[39,8,256]{2,1,0:T(8,128)S(1)} collective-permute-done((f32[39,8,256]{2,1,0:T(8,128)S(1)}, f32[39,8,256]{2,1,0:T(8,128)S(1)}, u32[]{:S(2)}, u32[]{:S(2)}) %collective-permute-start.2) | collective-permute-done | bytes 319520 | tf_op jit(solution)/shard_map/ppermute | solution.py:58
  21.4 0.0 collective-permute-done.3.yb.refs_5_
  21.4 0.2 shard_map.113
  21.7 0.1 collective-permute-start.4
  21.8 1.2 %collective-permute-done.4.refs_6_ = f32[80,128]{1,0:T(8,128)S(1)} collective-permute-done((f32[80,128]{1,0:T(8,128)S(1)}, f32[80,128]{1,0:T(8,128)S(1)}, u32[]{:S(2)}, u32[]{:S(2)}) %collective-permute-start.4) | collective-permute-done | bytes 40992 | tf_op jit(solution)/shard_map/ppermute | solution.py:58
  23.0 4.9 %shard_map.114 = (f32[3,16,16,384]{3,2,1,0:T(8,128)S(1)}, f32[3,16,16,384]{3,2,1,0:T(8,128)S(1)}, f32[3,20,16,384]{3,2,1,0:T(8,128)S(1)}, f32[16,16,384]{2,1,0:T...) custom-call(f32[3,8,8,256]{3,2,1,0:T(8,128)S(1)} %get-tuple-element., ...), custom_call_target="tpu_custom_call" | custom-call | tf_op jit(solution)/shard_map/pallas_call | solution.py:835
  27.9 0.2 collective-permute-start.5
  28.2 1.1 %collective-permute-done.5.refs_1_ = f32[104,128]{1,0:T(8,128)S(1)} collective-permute-done((f32[104,128]{1,0:T(8,128)S(1)}, f32[104,128]{1,0:T(8,128)S(1)}, u32[]{:S(2)}, u32[]{:S(2)}) %collective-permute-start.5) | collective-permute-done | bytes 53280 | tf_op jit(solution)/shard_map/ppermute | solution.py:58
  29.2 0.2 shard_map.115
  29.5 1.5 %collective-permute-start.6 = (f32[48,128]{1,0:T(8,128)S(1)}, f32[48,128]{1,0:T(8,128)S(1)}, u32[]{:S(2)}, u32[]{:S(2)}) collective-permute-start(f32[48,128]{1,0:T(8,128)S(1)} %get-tuple-element.40), channel_id=1, source_target_pairs={{0,8},{8,0},{16,24},{24,16},{1,9},{9,1},{17,25},{25,17},{2,10},{10... | collective-permute-start | bytes 73736 | tf_op jit(solution)/shard_map/ppermute | solution.py:58
  31.0 0.7 %collective-permute-start.7 = (f32[48,128]{1,0:T(8,128)S(1)}, f32[48,128]{1,0:T(8,128)S(1)}, u32[]{:S(2)}, u32[]{:S(2)}) collective-permute-start(f32[48,128]{1,0:T(8,128)S(1)} %get-tuple-element.41), channel_id=1, source_target_pairs={{0,24},{8,16},{16,8},{24,0},{1,25},{9,17},{17,9},{25,1},{2,26},{10... | collective-permute-start | bytes 73736 | tf_op jit(solution)/shard_map/ppermute | solution.py:61
  31.7 1.6 %collective-permute-done.6.got_a = f32[48,128]{1,0:T(8,128)S(1)} collective-permute-done((f32[48,128]{1,0:T(8,128)S(1)}, f32[48,128]{1,0:T(8,128)S(1)}, u32[]{:S(2)}, u32[]{:S(2)}) %collective-permute-start.6) | collective-permute-done | bytes 24608 | tf_op jit(solution)/shard_map/ppermute | solution.py:58
  33.3 2.4 %collective-permute-done.7.got_b = f32[48,128]{1,0:T(8,128)S(1)} collective-permute-done((f32[48,128]{1,0:T(8,128)S(1)}, f32[48,128]{1,0:T(8,128)S(1)}, u32[]{:S(2)}, u32[]{:S(2)}) %collective-permute-start.7) | collective-permute-done | bytes 24608 | tf_op jit(solution)/shard_map/ppermute | solution.py:61
  35.7 0.2 shard_map.116
  35.9 4.8 %collective-permute-start.8 = (f32[96,128]{1,0:T(8,128)S(1)}, f32[96,128]{1,0:T(8,128)S(1)}, u32[]{:S(2)}, u32[]{:S(2)}) collective-permute-start(f32[96,128]{1,0:T(8,128)S(1)} %get-tuple-element.44), channel_id=1, source_target_pairs={{0,2},{2,0},{4,6},{6,4},{1,3},{3,1},{5,7},{7,5},{8,10},{10,8},{12,... | collective-permute-start | bytes 147464 | tf_op jit(solution)/shard_map/ppermute | solution.py:58
  40.7 0.7 %collective-permute-start.9 = (f32[96,128]{1,0:T(8,128)S(1)}, f32[96,128]{1,0:T(8,128)S(1)}, u32[]{:S(2)}, u32[]{:S(2)}) collective-permute-start(f32[96,128]{1,0:T(8,128)S(1)} %get-tuple-element.45), channel_id=1, source_target_pairs={{2,4},{4,2},{3,5},{5,3},{10,12},{12,10},{11,13},{13,11},{18,20},{2... | collective-permute-start | bytes 147464 | tf_op jit(solution)/shard_map/ppermute | solution.py:61
  41.3 1.4 %collective-permute-done.8.got_a = f32[96,128]{1,0:T(8,128)S(1)} collective-permute-done((f32[96,128]{1,0:T(8,128)S(1)}, f32[96,128]{1,0:T(8,128)S(1)}, u32[]{:S(2)}, u32[]{:S(2)}) %collective-permute-start.8) | collective-permute-done | bytes 49184 | tf_op jit(solution)/shard_map/ppermute | solution.py:58
  42.7 0.0 collective-permute-done.9.got_b
  42.7 0.0 copy-start.2
  42.8 0.0 copy-start.3
  42.8 5.0 %shard_map.117 = (f32[8,3,8,256]{3,2,1,0:T(8,128)S(1)}, f32[8,3,8,256]{3,2,1,0:T(8,128)S(1)}, f32[32,128]{1,0:T(8,128)}) custom-call(f32[24,8,256]{2,1,0:T(8,128)S(1)} %get-tuple-element.42.wide_planes, f32[40,256]{1,0:T(8,128)S(1)} %get-tuple-element.43.columns, f32[96,128]{1,0:T(8,128)S(1)} %collective-permute-done.8.got_a, ...), custom_call_target="tpu_custom_call" | custom-call | tf_op jit(solution)/shard_map/pallas_call | solution.py:865
  47.8 5.5 %all-to-all-start = ((f32[32,1,128]{2,1,0:T(1,128)}), f32[32,1,128]{2,1,0:T(1,128)S(1)}, u32[]{:S(2)}, u32[]{:S(2)}) async-start(f32[32,1,128]{2,1,0:T(1,128)} %bitcast.2), calls=%async_computation | async-start | bytes 32768 | tf_op jit(solution)/shard_map/all_to_all | solution.py:869
  54.0 6.4 %all-to-all-done = f32[32,1,128]{2,1,0:T(1,128)S(1)} async-done(((f32[32,1,128]{2,1,0:T(1,128)}), f32[32,1,128]{2,1,0:T(1,128)S(1)}, u32[]{:S(2)}, u32[]{:S(2)}) %all-to-all-start) | async-done | bytes 16416 | tf_op jit(solution)/shard_map/all_to_all | solution.py:869
  60.4 1.1 %shard_map.118 = (f32[3,8,8,256]{3,2,1,0:T(8,128)}, f32[3,8,8,256]{3,2,1,0:T(8,128)}, f32[3,8,8,256]{3,2,1,0:T(8,128)}, f32[3,8,8,256]{3,2,1,0:T(8,128)}) custom-call(f32[1]{0:T(128)} %bitcast.5.prev_rz, f32[32,128]{1,0:T(8,128)S(1)} %bitcast.6, f32[8,3,8,256]{3,2,1,0:T(8,128)S(1)} %get-tuple-element.56.precond, ...), custom_call_target="tpu_custom_call" | custom-call | tf_op jit(solution)/shard_map/pallas_call | solution.py:871
  (8 shorter events, 0.0 us)
Async XLA Ops:
  1.7 7.5 %collective-permute-start = (f32[18,8,256]{2,1,0:T(8,128)S(1)}, f32[18,8,256]{2,1,0:T(8,128)S(1)}, u32[]{:S(2)}, u32[]{:S(2)}) collective-permute-start(f32[18,8,256]{2,1,0:T(8,128)S(1)} %get-tuple-element.33), channel_id=1, source_target_pairs={{0,8},{8,0},{16,24},{24,16},{1,9},{9,1},{17,25},{25,17},{2,10},{10... | collective-permute-start | bytes 442376 | tf_op jit(solution)/shard_map/ppermute | solution.py:58
  4.7 8.2 %collective-permute-start.1 = (f32[18,8,256]{2,1,0:T(8,128)S(1)}, f32[18,8,256]{2,1,0:T(8,128)S(1)}, u32[]{:S(2)}, u32[]{:S(2)}) collective-permute-start(f32[18,8,256]{2,1,0:T(8,128)S(1)} %get-tuple-element.34), channel_id=1, source_target_pairs={{0,24},{8,16},{16,8},{24,0},{1,25},{9,17},{17,9},{25,1},{2,26},{10... | collective-permute-start | bytes 442376 | tf_op jit(solution)/shard_map/ppermute | solution.py:61
  13.0 8.5 %collective-permute-start.2 = (f32[39,8,256]{2,1,0:T(8,128)S(1)}, f32[39,8,256]{2,1,0:T(8,128)S(1)}, u32[]{:S(2)}, u32[]{:S(2)}) collective-permute-start(f32[39,8,256]{2,1,0:T(8,128)S(1)} %get-tuple-element.35), channel_id=1, source_target_pairs={{0,2},{2,0},{4,6},{6,4},{1,3},{3,1},{5,7},{7,5},{8,10},{10,8},{12,... | collective-permute-start | bytes 958472 | tf_op jit(solution)/shard_map/ppermute | solution.py:58
  14.6 14.6 %copy-start.4 = (f32[1,1,48,48]{3,2,1,0:T(8,128)S(1)}, f32[1,1,48,48]{3,2,1,0:T(8,128)}, u32[]{:S(2)}) copy-start(f32[1,1,48,48]{3,2,1,0:T(8,128)} %refs_2_.1) | copy-start | bytes 27652
  14.6 28.1 %copy-start = (f32[3,8,8,256]{3,2,1,0:T(8,128)S(1)}, f32[3,8,8,256]{3,2,1,0:T(8,128)}, u32[]{:S(2)}) copy-start(f32[3,8,8,256]{3,2,1,0:T(8,128)} %prev_d.3) | copy-start | bytes 589828
  14.6 28.1 %copy-start.1 = (f32[3,8,8,256]{3,2,1,0:T(8,128)S(1)}, f32[3,8,8,256]{3,2,1,0:T(8,128)}, u32[]{:S(2)}) copy-start(f32[3,8,8,256]{3,2,1,0:T(8,128)} %prev_i.3) | copy-start | bytes 589828
  14.6 6.8 %collective-permute-start.3 = (f32[39,8,256]{2,1,0:T(8,128)S(1)}, f32[39,8,256]{2,1,0:T(8,128)S(1)}, u32[]{:S(2)}, u32[]{:S(2)}) collective-permute-start(f32[39,8,256]{2,1,0:T(8,128)S(1)} %get-tuple-element.36), channel_id=1, source_target_pairs={{2,4},{4,2},{3,5},{5,3},{10,12},{12,10},{11,13},{13,11},{18,20},{2... | collective-permute-start | bytes 958472 | tf_op jit(solution)/shard_map/ppermute | solution.py:61
  21.7 1.3 %collective-permute-start.4 = (f32[80,128]{1,0:T(8,128)S(1)}, f32[80,128]{1,0:T(8,128)S(1)}, u32[]{:S(2)}, u32[]{:S(2)}) collective-permute-start(f32[80,128]{1,0:T(8,128)S(1)} %shard_map.113), channel_id=1, source_target_pairs={{0,1},{1,0},{2,3},{3,2},{4,5},{5,4},{6,7},{7,6},{8,9},{9,8},{10,11... | collective-permute-start | bytes 122888 | tf_op jit(solution)/shard_map/ppermute | solution.py:58
  27.9 1.3 %collective-permute-start.5 = (f32[104,128]{1,0:T(8,128)S(1)}, f32[104,128]{1,0:T(8,128)S(1)}, u32[]{:S(2)}, u32[]{:S(2)}) collective-permute-start(f32[104,128]{1,0:T(8,128)S(1)} %get-tuple-element.37.refs_0_), channel_id=1, source_target_pairs={{0,1},{1,0},{2,3},{3,2},{4,5},{5,4},{6,7},{7,6},{8,9},{9,8},{10,11... | collective-permute-start | bytes 159752 | tf_op jit(solution)/shard_map/ppermute | solution.py:58
  29.5 3.8 %collective-permute-start.6 = (f32[48,128]{1,0:T(8,128)S(1)}, f32[48,128]{1,0:T(8,128)S(1)}, u32[]{:S(2)}, u32[]{:S(2)}) collective-permute-start(f32[48,128]{1,0:T(8,128)S(1)} %get-tuple-element.40), channel_id=1, source_target_pairs={{0,8},{8,0},{16,24},{24,16},{1,9},{9,1},{17,25},{25,17},{2,10},{10... | collective-permute-start | bytes 73736 | tf_op jit(solution)/shard_map/ppermute | solution.py:58
  31.0 4.7 %collective-permute-start.7 = (f32[48,128]{1,0:T(8,128)S(1)}, f32[48,128]{1,0:T(8,128)S(1)}, u32[]{:S(2)}, u32[]{:S(2)}) collective-permute-start(f32[48,128]{1,0:T(8,128)S(1)} %get-tuple-element.41), channel_id=1, source_target_pairs={{0,24},{8,16},{16,8},{24,0},{1,25},{9,17},{17,9},{25,1},{2,26},{10... | collective-permute-start | bytes 73736 | tf_op jit(solution)/shard_map/ppermute | solution.py:61
  35.9 6.9 %collective-permute-start.8 = (f32[96,128]{1,0:T(8,128)S(1)}, f32[96,128]{1,0:T(8,128)S(1)}, u32[]{:S(2)}, u32[]{:S(2)}) collective-permute-start(f32[96,128]{1,0:T(8,128)S(1)} %get-tuple-element.44), channel_id=1, source_target_pairs={{0,2},{2,0},{4,6},{6,4},{1,3},{3,1},{5,7},{7,5},{8,10},{10,8},{12,... | collective-permute-start | bytes 147464 | tf_op jit(solution)/shard_map/ppermute | solution.py:58
  40.7 2.1 %collective-permute-start.9 = (f32[96,128]{1,0:T(8,128)S(1)}, f32[96,128]{1,0:T(8,128)S(1)}, u32[]{:S(2)}, u32[]{:S(2)}) collective-permute-start(f32[96,128]{1,0:T(8,128)S(1)} %get-tuple-element.45), channel_id=1, source_target_pairs={{2,4},{4,2},{3,5},{5,3},{10,12},{12,10},{11,13},{13,11},{18,20},{2... | collective-permute-start | bytes 147464 | tf_op jit(solution)/shard_map/ppermute | solution.py:61
  42.7 17.6 %copy-start.2 = (f32[3,8,8,256]{3,2,1,0:T(8,128)S(1)}, f32[3,8,8,256]{3,2,1,0:T(8,128)}, u32[]{:S(2)}) copy-start(f32[3,8,8,256]{3,2,1,0:T(8,128)} %res.1) | copy-start | bytes 589828
  42.8 17.6 %copy-start.3 = (f32[3,8,8,256]{3,2,1,0:T(8,128)S(1)}, f32[3,8,8,256]{3,2,1,0:T(8,128)}, u32[]{:S(2)}) copy-start(f32[3,8,8,256]{3,2,1,0:T(8,128)} %sol.1) | copy-start | bytes 589828
  47.8 12.6 %all-to-all-start = ((f32[32,1,128]{2,1,0:T(1,128)}), f32[32,1,128]{2,1,0:T(1,128)S(1)}, u32[]{:S(2)}, u32[]{:S(2)}) async-start(f32[32,1,128]{2,1,0:T(1,128)} %bitcast.2), calls=%async_computation | async-start | bytes 32768 | tf_op jit(solution)/shard_map/all_to_all | solution.py:869

commit v5 on v4

--- a/solution.py
+++ b/solution.py
@@ -16,6 +16,7 @@
 LANES = Z + 128
 MID_LANES = Z // 2 + 128
 DAMPING = 0.6
+COUPLING = (1.6, 0.7, 0.7)
 ALL = ("gx", "gy", "gz")
 F32 = jnp.float32
 VMEM = pl.BlockSpec(memory_space=pltpu.VMEM)
@@ -117,15 +118,37 @@
     return before + after + (centre + centre)
 
 
+def tri_x_pair(a, b, c, d):
+    near = b + c
+    return (a + b) + near, near + (c + d)
+
+
+def tri_rows(a, below=None, above=None):
+    even, odd = a[:8], a[8:]
+    former, after = pltpu.roll(odd, 1, 0), pltpu.roll(even, 7, 0)
+    if below is not None:
+        row = row_of(even.shape)
+        former = jnp.where(row == 6, below, former)
+        after = jnp.where(row == 5, above, after)
+    both = even + odd
+    return jnp.concatenate([both + (even + former), both + (odd + after)], axis=0)
+
+
 def tree_sum(terms):
     while len(terms) > 1:
         terms = [sum(terms[k : k + 2]) for k in range(0, len(terms), 2)]
     return terms[0]
 
 
-def coupled(parts):
-    total = 0.3 * (parts[0] + parts[1] + parts[2])
-    return [0.7 * part + total for part in parts]
+def to_modes(v0, v1, v2):
+    total = v0 + v1 + v2
+    third = total * (1.0 / 3.0)
+    return total, v0 - third, v1 - third
+
+
+def from_modes(total, a, b):
+    third = total * (1.0 / 3.0)
+    return a + third, b + third, third - a - b
 
 
 def row_of(shape):
@@ -151,12 +174,6 @@
     lane = lane_of((MID_LANES, LANES))
     mid = jnp.where(lane < Z + 64, lane // 2, lane // 2 + 64)
     return jnp.where(mid == row_of((MID_LANES, LANES)), 1.0, 0.0).astype(F32)
-
-
-def every_other(ref, at, size):
-    return jnp.concatenate(
-        [ref[k, pl.ds(at, size, stride=2)] for k in range(ref.shape[0])], axis=1
-    )
 
 
 def dot_exact_weights(a, b):
@@ -181,11 +198,16 @@
 Z_PACK = -(-Z_TILES // 16) * 8
 
 
-def pack_x_body(table_in, index_in, res_in, res, young, pack_even, pack_odd, table, index, sems):
+def pack_x_body(
+    table_in, index_in, res_in, res, young, pack_even, pack_odd, table, index, res_n, young_n, sems
+):
     copies = [
-        pltpu.make_async_copy(source, target, sems.at[k])
-        for k, (source, target) in enumerate(((table_in, table), (index_in, index), (res_in, res)))
+        pltpu.make_async_copy(table_in, table, sems.at[0]),
+        pltpu.make_async_copy(index_in, index, sems.at[1]),
     ]
+    for k in range(2):
+        source = res_in.at[:, :, :, pl.ds(128 * k, 128)]
+        copies.append(pltpu.make_async_copy(source, res_n.at[k], sems.at[2 + k]))
     for copy in copies:
         copy.start()
     copies[0].wait()
@@ -194,8 +216,22 @@
     value = jnp.zeros(levels.shape, F32)
     for level in range(table.shape[0]):
         value = jnp.where(levels == level, table[level], value)
-    young[...] = value
-    copies[2].wait()
+
+    def own_tile(ref, *at):
+        rows = [ref[(*at, pl.ds(start, 4, stride=2), slice(None))] for start in (0, 1)]
+        return jnp.concatenate(rows, axis=0)
+
+    for k in range(2):
+        young_n[k] = value[:, :, 128 * k : 128 * k + 128]
+    for k in range(2):
+        for x in range(X):
+            young[x, :, 128 * k : 128 * k + 128] = own_tile(young_n, k, x)
+    for k in range(2):
+        copies[2 + k].wait()
+        for x in range(X):
+            modes = to_modes(*[own_tile(res_n, k, c, x) for c in range(COMPS)])
+            for c in range(COMPS):
+                res[c, x, :, 128 * k : 128 * k + 128] = modes[c]
     high_first = jnp.where(is_even("gx"), 1, 0)
     for pack, high in ((pack_even, high_first), (pack_odd, 1 - high_first)):
         for c in range(COMPS):
@@ -236,8 +272,8 @@
     def halves(tile, a, b):
         put(
             tile,
-            jnp.where(row < 4, a, up(b, 4)),
-            jnp.where(row < 4, up(a, 4), b),
+            jnp.where(row % 4 < 2, a, up(b, 2)),
+            jnp.where(row % 4 < 2, up(a, -2), b),
         )
 
     for c in range(COMPS):
@@ -250,9 +286,9 @@
         low = high = None
         for k in range(4):
             plane = planes[4 * j + k]
-            a, b = up(plane, 2 * k - 4), up(plane, 2 * k - 2)
-            low = a if k == 0 else jnp.where(row < 2 * k, low, a)
-            high = b if k == 0 else jnp.where(row < 2 * k, high, b)
+            a, b = up(plane, k - 2), up(plane, k - 1)
+            low = a if k == 0 else jnp.where(row % 4 == k, a, low)
+            high = b if k == 0 else jnp.where(row % 4 == k, b, high)
         put(R_TILES + E4_TILES + j, low, high)
 
 
@@ -262,24 +298,23 @@
     row = row_of((Y, width))
     whole = slice(None)
 
-    def rim_tile(tile, second):
+    def with_rims(own, tile, second):
         key = (tile, whole, lanes)
         low, high = lower(key), upper(key)
-        if second:
-            high = up(high, 4)
-        else:
-            low = up(low, 4)
-        return jnp.where(row < 4, high, low)
+        at = 2 if second else 0
+        even = jnp.where(row < 6, up(high, 4 - at), up(low, 6 - at))
+        odd = jnp.where(row < 6, up(high, -at), up(low, 2 - at))
+        return [jnp.where(row < 4, own, even), jnp.where(row < 4, up(own, 4), odd)]
 
     def res_tiles(c, i):
-        return [res_plane(c, i), rim_tile(c * X + i % X, i >= X)]
+        return with_rims(res_plane(c, i), c * X + i % X, i >= X)
 
     def young_tiles(i):
         two = (R_TILES + E4_TILES + i // 4, whole, lanes)
         k = i % 4
-        low2, high2 = up(lower(two), -2 * k), up(upper(two), 2 - 2 * k)
-        side = jnp.where(row < 2, low2, jnp.where(row < 4, high2, 0.0))
-        return [young_plane(i), rim_tile(R_TILES + i % E4_TILES, i >= E4_TILES), side]
+        low2, high2 = up(lower(two), -k), up(upper(two), 1 - k)
+        side = jnp.where(row % 4 == 0, low2, jnp.where(row % 4 == 1, high2, 0.0))
+        return with_rims(young_plane(i), R_TILES + i % E4_TILES, i >= E4_TILES) + [side]
 
     return res_tiles, young_tiles
 
@@ -327,23 +362,31 @@
 MZ_PACK = (LOW_TILE + 1) * 8
 
 
-def fine_apply(s, es, c1, e, i):
-    parts = []
+def fine_parts(s, es, c1, e, i):
+    found = []
     for c in range(COMPS):
-        v = tri_y(tri_x(s[c, i - 1], s[c, i], s[c, i + 1]))
-        ev = tri_y(tri_x(es[c, i - 1], es[c, i], es[c, i + 1]))
-        parts.append(c1[i] * s[c, i] - mixed_z(e[0, i], e[1, i], e[2, i], v, ev))
-    return coupled(parts)
-
-
-def sweep(source, e_source, target, e_target, r, c1, e, w, first, last):
-    def body(k, carry):
-        for i in (first + 2 * k, first + 2 * k + 1):
-            applied = fine_apply(source, e_source, c1, e, i)
+        v = tri_x_pair(*[s[c, i + k] for k in range(-1, 3)])
+        ev = tri_x_pair(*[es[c, i + k] for k in range(-1, 3)])
+        found.append(
+            [
+                c1[i + k] * s[c, i + k]
+                - mixed_z(e[0, i + k], e[1, i + k], e[2, i + k], tri_rows(v[k]), tri_rows(ev[k]))
+                for k in range(2)
+            ]
+        )
+    return found
+
+
+def sweep(source, e_source, target, e_target, s0, c1, e, w, first, last):
+    def body(n, carry):
+        i = first + 2 * n
+        parts = fine_parts(source, e_source, c1, e, i)
+        for k in range(2):
             for c in range(COMPS):
-                value = source[c, i] + w[i] * (r[c, i] - applied[c])
-                target[c, i] = value
-                e_target[c, i] = e[0, i] * value
+                factor = w[0 if c == 0 else 1, i + k]
+                value = (source[c, i + k] + s0[c, i + k]) - factor * parts[c][k]
+                target[c, i + k] = value
+                e_target[c, i + k] = e[0, i + k] * value
         return carry
 
     lax.fori_loop(0, (last - first) // 2, body, 0)
@@ -352,8 +395,8 @@
 def smooth_body(n_z, *refs):
     res, young, xa, xb, ya, yb = refs[:6]
     got_z = refs[6 : 6 + n_z]
-    r, s1, e, c1, w, em, em_side, c1m, wm, pack = refs[6 + n_z : 16 + n_z]
-    wide, wide_z, s0, es0, es1, rest, wide_x = refs[16 + n_z :]
+    s0, s1, e, c1, w, em, em_side, c1m, wm, pack = refs[6 + n_z : 16 + n_z]
+    wide, wide_z, r, es0, es1, to_pool = refs[16 + n_z :]
 
     res_tiles, young_tiles = xy_planes(res, young, (xa, xb), (ya, yb), slice(None), Z)
     rim = z_rims(got_z)
@@ -379,8 +422,10 @@
             e[1, i] = after[:ROWS]
             e[2, i] = before[:ROWS]
         total = wide[2 * k] + wide[2 * k + 1]
-        for t in range(LANES // 128):
-            wide_x[t, pl.ds(24 * k, 24)] = total[:, 128 * t : 128 * t + 128]
+        side = total[ROWS:]
+        start = pl.multiple_of(COMPS * 6 * 8 + 16 * k, 16)
+        to_pool[pl.ds(start, 8)] = total[:8] + total[8:ROWS]
+        to_pool[pl.ds(start + 8, 8)] = side + up(side, 4)
         return carry
 
     lax.fori_loop(0, E_PLANES // 2, shift, 0, unroll=5)
@@ -389,13 +434,12 @@
         for i in (2 * k, 2 * k + 1):
             total = tri_x(wide_z[i + 1], wide_z[i + 2], wide_z[i + 3])
             side = total[ROWS:]
-            below = jnp.concatenate([side, up(side, 3)], axis=0)
-            above = jnp.concatenate([side, up(side, 1)], axis=0)
-            total = tri_y_with(total[:ROWS], below, above, 11)
+            total = tri_rows(total[:ROWS], up(side, 2), up(side, 4))
             centre = e[0, i + 2]
             c1[i] = 72.0 * centre + total
             inverse = jnp.where(centre > 0.0, DAMPING / (56.0 * centre + total), 0.0)
-            w[i] = inverse
+            for n in range(2):
+                w[n, i] = COUPLING[n] * inverse
             for c in range(COMPS):
                 value = inverse * r[c, i]
                 s0[c, i] = value
@@ -404,28 +448,21 @@
 
     lax.fori_loop(0, PLANES // 2, prepare, 0)
     e = e.at[:, 2 : 2 + PLANES]
-    sweep(s0, es0, s1, es1, r, c1, e, w, 1, PLANES - 1)
+    sweep(s0, es0, s1, es1, s0, c1, e, w, 1, PLANES - 1)
 
     def residue(m, carry):
-        first = fine_apply(s1, es1, c1, e, 2 * m + 2)
-        second = fine_apply(s1, es1, c1, e, 2 * m + 3)
+        i = 2 * m + 2
+        parts = fine_parts(s1, es1, c1, e, i)
         for c in range(COMPS):
-            total = (r[c, 2 * m + 2] - first[c]) + (r[c, 2 * m + 3] - second[c])
-            for t in range(LANES // 128):
-                rest[t, pl.ds((c * 6 + m) * ROWS, ROWS)] = total[:, 128 * t : 128 * t + 128]
+            total = (r[c, i] + r[c, i + 1]) - COUPLING[c] * (parts[c][0] + parts[c][1])
+            start = pl.multiple_of((c * 6 + m) * 8, 8)
+            to_pool[pl.ds(start, 8)] = total[:8] + total[8:]
         return carry
 
     lax.fori_loop(0, 6, residue, 0)
 
-    wide_x[:, 24 * EM_PLANES :] = jnp.zeros((LANES // 128, 8, 128), F32)
-    pieces = []
-    for t in range(COMPS * 6):
-        pieces.append(every_other(rest, 16 * t, 8) + every_other(rest, 16 * t + 1, 8))
-    for m in range(EM_PLANES):
-        for at in (24 * m, 24 * m + 16):
-            pieces.append(every_other(wide_x, at, 8) + every_other(wide_x, at + 1, 8))
-    pooled = dot_exact_weights(jnp.concatenate(pieces, axis=0), pool_matrix(0.5))
-    pooled = [pooled[8 * t : 8 * t + 8] for t in range(len(pieces))]
+    pooled = dot_exact_weights(to_pool[...], pool_matrix(0.5))
+    pooled = [pooled[8 * t : 8 * t + 8] for t in range(COMPS * 6 + 2 * EM_PLANES)]
     for m in range(EM_PLANES):
         centre = 0.25 * pooled[COMPS * 6 + 2 * m]
         em[0, m] = centre
@@ -447,26 +484,23 @@
             rhs[c, m] = pooled[c * 6 + m]
             mid[c, m] = wm[m + 1] * rhs[c, m]
             e_mid[c, m] = em[0, m + 2] * mid[c, m]
-    rows = []
     kept = {}
     for m in range(1, 5):
-        parts = []
         for c in range(COMPS):
             v = tri_y(tri_x(mid[c, m - 1], mid[c, m], mid[c, m + 1]))
             ev = tri_y(tri_x(e_mid[c, m - 1], e_mid[c, m], e_mid[c, m + 1]))
             mixed = mixed_z(em[0, m + 2], em[1, m + 2], em[2, m + 2], v, ev)
-            parts.append(c1m[m + 1] * mid[c, m] - mixed)
-        applied = coupled(parts)
-        for c in range(COMPS):
-            left_over = rhs[c, m] - applied[c]
+            left_over = rhs[c, m] - COUPLING[c] * (c1m[m + 1] * mid[c, m] - mixed)
             kept[c, m - 1] = left_over
             value = mid[c, m] + wm[m + 1] * left_over
             tile = c * 4 + m - 1
             pack[8 * tile : 8 * tile + 8] = value[:, :128]
-    for c in range(COMPS):
-        for b in range(2):
-            rows.append(kept[c, 2 * b] + kept[c, 2 * b + 1])
-    stacked = jnp.concatenate(rows, axis=0)
+    rows = {}
+    for b in range(2):
+        found = from_modes(*[kept[c, 2 * b] + kept[c, 2 * b + 1] for c in range(COMPS)])
+        for c in range(COMPS):
+            rows[c, b] = found[c]
+    stacked = jnp.concatenate([rows[c, b] for c in range(COMPS) for b in range(2)], axis=0)
     lane_box = row_of((MID_LANES, 128))
     column = lane_of((MID_LANES, 128))
     boxes = jnp.where(
@@ -538,16 +572,18 @@
     ]
     value = jnp.where(wide < 64, own_a, own_b)
     value = jnp.where(wide < 128, value, jnp.where(wide < 192, after, before))
-    value = jnp.where(row_of((16, MID_LANES)) < 12, value, 0.0)
-    column[...] = value
+    row = row_of((8, MID_LANES))
+    first, second, third = value[:8], up(value[:8], 4), value[8:]
+    total, a, b = to_modes(first, second, third)
+    rest = [jnp.where(row < 4, total, up(a, 4)), jnp.where(row < 4, b, 0.0)]
+    column[:8] = rest[0]
+    column[8:] = rest[1]
 
     even = is_even("gx")
-    row = row_of((8, MID_LANES))
     low, high = [
         [jnp.where(row < 4, planes[c * 4 + p], up(planes[c * 4 + p + 1], 4)) for c in range(COMPS)]
         for p in (0, 2)
     ]
-    rest = [value[:8], value[8:]]
     pack_mid(pack_even, [jnp.where(even, b, a) for a, b in zip(low, high)] + rest)
     pack_mid(pack_odd, [jnp.where(even, a, b) for a, b in zip(low, high)] + rest)
 
@@ -592,8 +628,8 @@
 
 
 def finish_body(
-    wide_planes, columns, got_a, got_b, r, s1, e_all, c1, w, em, em_side, c1m, wm, prev_d, prev_i,
-    precond, operated, sums, cor, cor_side, mid, big, s2, es2, s3, es3, p, ep,
+    wide_planes, columns, got_a, got_b, s0, s1, e_all, c1, w, em, em_side, c1m, wm, prev_d, prev_i,
+    res, precond, operated, sums, cor, cor_side, mid, fine, s2, es2, s3, es3, p, ep,
 ):
     e = e_all.at[:, 2 : 2 + PLANES]
     lower, upper = from_sides((got_a, got_b), "gy")
@@ -619,7 +655,6 @@
         return (m + 1) // 2
 
     for m in range(M_PLANES):
-        parts = []
         for c in range(COMPS):
             near = [cor[c, box(m + k)] for k in range(3)]
             near_side = [cor_side[c, box(m + k)] for k in range(3)]
@@ -630,75 +665,60 @@
             side = tri_x(*e_side)
             ev = tri_y_with(tri_x(*e_near), up(side, 6), up(side, 4), 5)
             mixed = mixed_z(em[0, m + 1], em[1, m + 1], em[2, m + 1], v, ev)
-            parts.append(c1m[m] * near[1] - mixed)
-        applied = coupled(parts)
-        for c in range(COMPS):
+            applied = COUPLING[c] * (c1m[m] * near[1] - mixed)
             tile = wide_planes[c * 8 + m]
             n, k = c * 2 + m // 4, m % 4
             outer = jnp.where(row < 6, up(high_tiles[n], 4 - 2 * k), up(low_tiles[n], 6 - 2 * k))
             tile = jnp.where(row < 4, tile, outer)
             at = (c * 8 + m) * 8
-            mid[at : at + 8] = tile + cor[c, box(m + 1)] - wm[m] * applied[c]
-    spread = dot_exact_weights(mid[...], spread_matrix())
-    for t in range(COMPS * 8):
-        piece = spread[8 * t : 8 * t + 8]
-        for k in range(LANES // 128):
-            tile = piece[:, 128 * k : 128 * k + 128]
-            big[k, pl.ds(16 * t, 8, stride=2)] = tile
-            big[k, pl.ds(16 * t + 1, 8, stride=2)] = tile
+            mid[at : at + 8] = tile + cor[c, box(m + 1)] - wm[m] * applied
+    fine[...] = dot_exact_weights(mid[...], spread_matrix())
 
     def add_up(i, carry):
         for c in range(COMPS):
-            at = pl.multiple_of((c * 8 + i // 2) * 16, 16)
-            more = [big[k, pl.ds(at, 16)] for k in range(LANES // 128)]
-            value = s1[c, i] + jnp.concatenate(more, axis=1)
+            at = pl.multiple_of((c * 8 + i // 2) * 8, 8)
+            more = fine[pl.ds(at, 8)]
+            value = s1[c, i] + jnp.concatenate([more, more], axis=0)
             s2[c, i] = value
             es2[c, i] = e[0, i] * value
         return carry
 
     lax.fori_loop(1, PLANES - 1, add_up, 0)
-    sweep(s2, es2, s3, es3, r, c1, e, w, 2, PLANES - 2)
-    sweep(s3, es3, p, ep, r, c1, e, w, 3, PLANES - 3)
-
-
-    def own(a):
-        return a[:Y]
-
-    def image_of(x):
-        i = x + RIM
-        near = [e[k, i, :Y] for k in range(3)]
-        centre = c1[i, :Y]
-        owned, parts = [], []
-        for c in range(COMPS):
-            owned.append(p[c, i, :Y])
-            v = own(tri_y(tri_x(p[c, i - 1], p[c, i], p[c, i + 1])))
-            ev = own(tri_y(tri_x(ep[c, i - 1], ep[c, i], ep[c, i + 1])))
-            parts.append(centre * owned[c] - mixed_z(*near, v, ev))
-        return owned, coupled(parts)
-
-    def image(k, carry):
-        steps = [2 * k, 2 * k + 1]
-        found = [image_of(x) for x in steps]
-        for x, (owned, applied) in zip(steps, found):
-            for c in range(COMPS):
-                precond[x, c] = owned[c][:, :Z]
-                operated[x, c] = applied[c][:, :Z]
+    sweep(s2, es2, s3, es3, s0, c1, e, w, 2, PLANES - 2)
+    sweep(s3, es3, p, ep, s0, c1, e, w, 3, PLANES - 3)
+
+    def put_rows(target, x, modes):
+        for half in range(2):
+            for c, value in enumerate(from_modes(*[m[8 * half : 8 * half + 8, :Z] for m in modes])):
+                for k in range(Z // 128):
+                    part = value[:4, 128 * k : 128 * k + 128]
+                    target[x, c, k, pl.ds(half, 4, stride=2), :] = part
+
+    def image(n, carry):
+        i = 2 * n + RIM
+        parts = fine_parts(p, ep, c1, e, i)
+        for k in range(2):
+            put_rows(precond, 2 * n + k, [p[c, i + k] for c in range(COMPS)])
+            put_rows(operated, 2 * n + k, [COUPLING[c] * parts[c][k] for c in range(COMPS)])
         return carry
 
     lax.fori_loop(0, X // 2, image, 0)
     found = [[], [], [], []]
     for x in range(X):
         for c in range(COMPS):
-            own_p, own_a = precond[x, c], operated[x, c]
-            d, q = prev_d[c, x], prev_i[c, x]
-            terms = (r[c, x + RIM, :Y, :Z] * own_p, own_p * own_a, own_p * q + d * own_a, d * q)
-            for kept, term in zip(found, terms):
-                kept.append(term)
+            for k in range(Z // 128):
+                lanes = slice(128 * k, 128 * k + 128)
+                own_p, own_a = precond[x, c, k], operated[x, c, k]
+                d, q = prev_d[c, x, :, lanes], prev_i[c, x, :, lanes]
+                own_r = res[c, x, :, lanes]
+                terms = (own_r * own_p, own_p * own_a, own_p * q + d * own_a, d * q)
+                for kept, term in zip(found, terms):
+                    kept.append(term)
     found = [tree_sum(kept) for kept in found]
     row = row_of((8, 128))
     total = jnp.zeros((8, 128), F32)
     for k, value in enumerate(found):
-        line = jnp.sum(value[:, :128] + value[:, 128:], axis=0, keepdims=True)
+        line = jnp.sum(value, axis=0, keepdims=True)
         total = jnp.where(row == k, jnp.broadcast_to(line, (8, 128)), total)
     total = total + pltpu.roll(total, 64, 1)
     total = total + pltpu.roll(total, 32, 1)
@@ -722,18 +742,20 @@
     rz = entry(0)
     beta = rz / prev_rz[0]
     alpha = rz / (entry(1) + beta * (entry(2) + beta * entry(3)))
-    beta = jnp.broadcast_to(beta, (Y, Z))
-    alpha = jnp.broadcast_to(alpha, (Y, Z))
+    beta = jnp.broadcast_to(beta, (Y, 128))
+    alpha = jnp.broadcast_to(alpha, (Y, 128))
     leaving = []
     for step in range(X // STEP):
         for x in range(step * STEP, step * STEP + STEP):
             for c in range(COMPS):
-                d = precond[x, c] + beta * prev_d[c, x]
-                q = operated[x, c] + beta * prev_i[c, x]
-                news[2, c, x] = d
-                news[3, c, x] = q
-                news[0, c, x] = sol[c, x] + alpha * d
-                news[1, c, x] = res[c, x] - alpha * q
+                for k in range(Z // 128):
+                    at = (c, x, slice(None), slice(128 * k, 128 * k + 128))
+                    d = precond[x, c, k] + beta * prev_d[at]
+                    q = operated[x, c, k] + beta * prev_i[at]
+                    news[(2, *at)] = d
+                    news[(3, *at)] = q
+                    news[(0, *at)] = sol[at] + alpha * d
+                    news[(1, *at)] = res[at] - alpha * q
         part = pl.ds(step * STEP, STEP)
         for k, target in enumerate((new_s_out, new_r_out, new_d_out, new_i_out)):
             copy = pltpu.make_async_copy(
@@ -756,7 +778,7 @@
         shape(*FIELD),
         shape(3, E_PLANES, ROWS, LANES),
         shape(PLANES, ROWS, LANES),
-        shape(PLANES, ROWS, LANES),
+        shape(2, PLANES, ROWS, LANES),
         shape(3, EM_PLANES, 8, MID_LANES),
         shape(EM_PLANES, 8, MID_LANES),
         shape(M_PLANES, 8, MID_LANES),
@@ -775,8 +797,7 @@
             pltpu.VMEM(FIELD, F32),
             pltpu.VMEM(FIELD, F32),
             pltpu.VMEM(FIELD, F32),
-            pltpu.VMEM((LANES // 128, 18 * ROWS, 128), F32),
-            pltpu.VMEM((LANES // 128, 24 * EM_PLANES + 8, 128), F32),
+            pltpu.VMEM((COMPS * 6 * 8 + 16 * EM_PLANES, LANES), F32),
         ],
         n_in=6 + n_z,
         vmem=30 << 20,
@@ -786,15 +807,15 @@
 def finish_call(n_all):
     return call(
         finish_body,
-        [pltpu.VMEM((X, COMPS, Y, Z), F32)] * 2 + [shape(n_all, 128)],
+        [pltpu.VMEM((X, COMPS, Z // 128, Y, 128), F32)] * 2 + [shape(n_all, 128)],
         scratch=[
             pltpu.VMEM((COMPS, 6, 8, MID_LANES), F32),
             pltpu.VMEM((COMPS, 6, 8, MID_LANES), F32),
             pltpu.VMEM((COMPS * 64, MID_LANES), F32),
-            pltpu.VMEM((LANES // 128, COMPS * 128, 128), F32),
+            pltpu.VMEM((COMPS * 64, LANES), F32),
         ]
         + [pltpu.VMEM(FIELD, F32)] * 6,
-        n_in=15,
+        n_in=16,
         vmem=30 << 20,
     )
 
@@ -821,7 +842,9 @@
         scratch=[
             pltpu.SMEM(stiffness_table.shape, F32),
             pltpu.VMEM((X, Y, Z), jnp.int32),
-            pltpu.SemaphoreType.DMA((3,)),
+            pltpu.VMEM((2, COMPS, X, Y, 128), F32),
+            pltpu.VMEM((2, X, Y, 128), F32),
+            pltpu.SemaphoreType.DMA((4,)),
         ],
         n_in=3,
         hbm=(0, 1, 2),
@@ -832,7 +855,7 @@
     packs = call(pack_z_body, [shape(Z_PACK, 128)] * n_z, n_in=6)(res, young, *got_x, *got_y)
     got_z = swap("gz", packs[0], packs[-1])
 
-    r, s1, e, c1, w, em, em_side, c1m, wm, pack = smooth_call(n_z)(res, young, *got_x, *got_y, *got_z)
+    s0, s1, e, c1, w, em, em_side, c1m, wm, pack = smooth_call(n_z)(res, young, *got_x, *got_y, *got_z)
 
     got_z = swap("gz", pack, pack)
     gathered = []
@@ -863,7 +886,8 @@
     )(mid_planes, column, *got_x)
     got_y = swap("gy", py, qy, closed=False)
     precond, operated, sums = finish_call(n_all)(
-        mid_planes, columns, *got_y, r, s1, e, c1, w, em, em_side, c1m, wm, prev_direction, prev_image
+        mid_planes, columns, *got_y, s0, s1, e, c1, w, em, em_side, c1m, wm,
+        prev_direction, prev_image, residual,
     )
     precond, operated = in_vmem(precond), in_vmem(operated)
     sums = lax.all_to_all(sums, ALL, 0, 0, tiled=True)

time: 61.7 us -> 60.9 us (0.987)
  Pallas kernels: 12.8 us -> 12 us
where the time goes in v5:
time: 60.9 us; the launch traced here: 60.7 us
  waiting for transfers between devices  26.9 us (44%)
  starting transfers between devices  20.4 us (33%)
  Pallas kernels  12 us (20%)
  between operations  1.37 us (2%)
    ppermute x6, waiting for transfers between devices, swap(): got_even = lax.ppermute(even_pack, axis, pairs(count, False, closed))  14.4 us
    ppermute x6, starting transfers between devices, swap(): got_even = lax.ppermute(even_pack, axis, pairs(count, False, closed))  11.3 us
    all_to_all x1, waiting for transfers between devices, on_device(): sums = lax.all_to_all(sums, ALL, 0, 0, tiled=True)  6.42 us
    ppermute x4, waiting for transfers between devices, swap(): return [got_even, lax.ppermute(odd_pack, axis, pairs(count, True, closed))]  6.09 us
    all_to_all x1, starting transfers between devices, on_device(): sums = lax.all_to_all(sums, ALL, 0, 0, tiled=True)  5.52 us
    pallas_call x1, Pallas kernels, on_device(): smooth_call(n_z)(res, young, *got_x, *got_y, *got_z)  4.56 us
    pallas_call x1, Pallas kernels, on_device(): finish_call(n_all)  4.51 us
    ppermute x4, starting transfers between devices, swap(): return [got_even, lax.ppermute(odd_pack, axis, pairs(count, True, closed))]  3.65 us
  transfers between devices with their start and end apart: 11, of which 9 were waited for; matrix products, arithmetic and copies ran while one was open for 0% of the time, Pallas kernels for 0%

profile of v5, /device:TPU:0, one launch (start us, length us, event | category | flops | bytes accessed | tf_op | source)
XLA Modules:
  0.0 60.7 jit_solution(5419811570309097778)
XLA Ops:
  0.6 1.1 %shard_map.111 = (f32[3,8,8,256]{3,2,1,0:T(8,128)S(1)}, f32[8,8,256]{2,1,0:T(8,128)S(1)}, f32[18,8,256]{2,1,0:T(8,128)S(1)}, f32[18,8,256]{2,1,0:T(8,128)S(1)}) custom-call(f32[16]{0:T(128)} %table_in.1, s32[8,8,256]{2,1,0:T(8,128)} %index_in.1, f32[3,8,8,256]{3,2,1,0:T(8,128)} %res.3), custom_call_target="tpu_custom_call" | custom-call | tf_op jit(solution)/shard_map/pallas_call | solution.py:839
  1.7 3.0 %collective-permute-start = (f32[18,8,256]{2,1,0:T(8,128)S(1)}, f32[18,8,256]{2,1,0:T(8,128)S(1)}, u32[]{:S(2)}, u32[]{:S(2)}) collective-permute-start(f32[18,8,256]{2,1,0:T(8,128)S(1)} %get-tuple-element.33), channel_id=1, source_target_pairs={{0,8},{8,0},{16,24},{24,16},{1,9},{9,1},{17,25},{25,17},{2,10},{10... | collective-permute-start | bytes 442376 | tf_op jit(solution)/shard_map/ppermute | solution.py:59
  4.7 1.5 %collective-permute-start.1 = (f32[18,8,256]{2,1,0:T(8,128)S(1)}, f32[18,8,256]{2,1,0:T(8,128)S(1)}, u32[]{:S(2)}, u32[]{:S(2)}) collective-permute-start(f32[18,8,256]{2,1,0:T(8,128)S(1)} %get-tuple-element.34), channel_id=1, source_target_pairs={{0,24},{8,16},{16,8},{24,0},{1,25},{9,17},{17,9},{25,1},{2,26},{10... | collective-permute-start | bytes 442376 | tf_op jit(solution)/shard_map/ppermute | solution.py:62
  6.2 3.0 %collective-permute-done.got_a.xa.refs_2_ = f32[18,8,256]{2,1,0:T(8,128)S(1)} collective-permute-done((f32[18,8,256]{2,1,0:T(8,128)S(1)}, f32[18,8,256]{2,1,0:T(8,128)S(1)}, u32[]{:S(2)}, u32[]{:S(2)}) %collective-permute-start) | collective-permute-done | bytes 147488 | tf_op jit(solution)/shard_map/ppermute | solution.py:59
  9.2 3.7 %collective-permute-done.1.got_b.xb.refs_3_ = f32[18,8,256]{2,1,0:T(8,128)S(1)} collective-permute-done((f32[18,8,256]{2,1,0:T(8,128)S(1)}, f32[18,8,256]{2,1,0:T(8,128)S(1)}, u32[]{:S(2)}, u32[]{:S(2)}) %collective-permute-start.1) | collective-permute-done | bytes 147488 | tf_op jit(solution)/shard_map/ppermute | solution.py:62
  12.9 0.1 shard_map.112
  13.0 1.6 %collective-permute-start.2 = (f32[39,8,256]{2,1,0:T(8,128)S(1)}, f32[39,8,256]{2,1,0:T(8,128)S(1)}, u32[]{:S(2)}, u32[]{:S(2)}) collective-permute-start(f32[39,8,256]{2,1,0:T(8,128)S(1)} %get-tuple-element.35), channel_id=1, source_target_pairs={{0,2},{2,0},{4,6},{6,4},{1,3},{3,1},{5,7},{7,5},{8,10},{10,8},{12,... | collective-permute-start | bytes 958472 | tf_op jit(solution)/shard_map/ppermute | solution.py:59
  14.7 0.8 %collective-permute-start.3 = (f32[39,8,256]{2,1,0:T(8,128)S(1)}, f32[39,8,256]{2,1,0:T(8,128)S(1)}, u32[]{:S(2)}, u32[]{:S(2)}) collective-permute-start(f32[39,8,256]{2,1,0:T(8,128)S(1)} %get-tuple-element.36), channel_id=1, source_target_pairs={{2,4},{4,2},{3,5},{5,3},{10,12},{12,10},{11,13},{13,11},{18,20},{2... | collective-permute-start | bytes 958472 | tf_op jit(solution)/shard_map/ppermute | solution.py:62
  15.5 6.0 %collective-permute-done.2.ya.refs_4_ = f32[39,8,256]{2,1,0:T(8,128)S(1)} collective-permute-done((f32[39,8,256]{2,1,0:T(8,128)S(1)}, f32[39,8,256]{2,1,0:T(8,128)S(1)}, u32[]{:S(2)}, u32[]{:S(2)}) %collective-permute-start.2) | collective-permute-done | bytes 319520 | tf_op jit(solution)/shard_map/ppermute | solution.py:59
  21.5 0.0 collective-permute-done.3.yb.refs_5_
  21.5 0.2 shard_map.113
  21.7 0.1 collective-permute-start.4
  21.8 1.2 %collective-permute-done.4.refs_6_ = f32[80,128]{1,0:T(8,128)S(1)} collective-permute-done((f32[80,128]{1,0:T(8,128)S(1)}, f32[80,128]{1,0:T(8,128)S(1)}, u32[]{:S(2)}, u32[]{:S(2)}) %collective-permute-start.4) | collective-permute-done | bytes 40992 | tf_op jit(solution)/shard_map/ppermute | solution.py:59
  23.0 4.6 %shard_map.114 = (f32[3,16,16,384]{3,2,1,0:T(8,128)S(1)}, f32[3,16,16,384]{3,2,1,0:T(8,128)S(1)}, f32[3,20,16,384]{3,2,1,0:T(8,128)S(1)}, f32[16,16,384]{2,1,0:T...) custom-call(f32[3,8,8,256]{3,2,1,0:T(8,128)S(1)} %get-tuple-element., ...), custom_call_target="tpu_custom_call" | custom-call | tf_op jit(solution)/shard_map/pallas_call | solution.py:858
  27.6 0.2 collective-permute-start.5
  27.8 1.1 %collective-permute-done.5.refs_1_ = f32[104,128]{1,0:T(8,128)S(1)} collective-permute-done((f32[104,128]{1,0:T(8,128)S(1)}, f32[104,128]{1,0:T(8,128)S(1)}, u32[]{:S(2)}, u32[]{:S(2)}) %collective-permute-start.5) | collective-permute-done | bytes 53280 | tf_op jit(solution)/shard_map/ppermute | solution.py:59
  28.9 0.2 shard_map.115
  29.1 1.5 %collective-permute-start.6 = (f32[48,128]{1,0:T(8,128)S(1)}, f32[48,128]{1,0:T(8,128)S(1)}, u32[]{:S(2)}, u32[]{:S(2)}) collective-permute-start(f32[48,128]{1,0:T(8,128)S(1)} %get-tuple-element.40), channel_id=1, source_target_pairs={{0,8},{8,0},{16,24},{24,16},{1,9},{9,1},{17,25},{25,17},{2,10},{10... | collective-permute-start | bytes 73736 | tf_op jit(solution)/shard_map/ppermute | solution.py:59
  30.6 0.7 %collective-permute-start.7 = (f32[48,128]{1,0:T(8,128)S(1)}, f32[48,128]{1,0:T(8,128)S(1)}, u32[]{:S(2)}, u32[]{:S(2)}) collective-permute-start(f32[48,128]{1,0:T(8,128)S(1)} %get-tuple-element.41), channel_id=1, source_target_pairs={{0,24},{8,16},{16,8},{24,0},{1,25},{9,17},{17,9},{25,1},{2,26},{10... | collective-permute-start | bytes 73736 | tf_op jit(solution)/shard_map/ppermute | solution.py:62
  31.3 1.6 %collective-permute-done.6.got_a = f32[48,128]{1,0:T(8,128)S(1)} collective-permute-done((f32[48,128]{1,0:T(8,128)S(1)}, f32[48,128]{1,0:T(8,128)S(1)}, u32[]{:S(2)}, u32[]{:S(2)}) %collective-permute-start.6) | collective-permute-done | bytes 24608 | tf_op jit(solution)/shard_map/ppermute | solution.py:59
  33.0 2.4 %collective-permute-done.7.got_b = f32[48,128]{1,0:T(8,128)S(1)} collective-permute-done((f32[48,128]{1,0:T(8,128)S(1)}, f32[48,128]{1,0:T(8,128)S(1)}, u32[]{:S(2)}, u32[]{:S(2)}) %collective-permute-start.7) | collective-permute-done | bytes 24608 | tf_op jit(solution)/shard_map/ppermute | solution.py:62
  35.4 0.2 shard_map.116
  35.5 4.8 %collective-permute-start.8 = (f32[96,128]{1,0:T(8,128)S(1)}, f32[96,128]{1,0:T(8,128)S(1)}, u32[]{:S(2)}, u32[]{:S(2)}) collective-permute-start(f32[96,128]{1,0:T(8,128)S(1)} %get-tuple-element.44), channel_id=1, source_target_pairs={{0,2},{2,0},{4,6},{6,4},{1,3},{3,1},{5,7},{7,5},{8,10},{10,8},{12,... | collective-permute-start | bytes 147464 | tf_op jit(solution)/shard_map/ppermute | solution.py:59
  40.4 0.7 %collective-permute-start.9 = (f32[96,128]{1,0:T(8,128)S(1)}, f32[96,128]{1,0:T(8,128)S(1)}, u32[]{:S(2)}, u32[]{:S(2)}) collective-permute-start(f32[96,128]{1,0:T(8,128)S(1)} %get-tuple-element.45), channel_id=1, source_target_pairs={{2,4},{4,2},{3,5},{5,3},{10,12},{12,10},{11,13},{13,11},{18,20},{2... | collective-permute-start | bytes 147464 | tf_op jit(solution)/shard_map/ppermute | solution.py:62
  41.0 1.4 %collective-permute-done.8.got_a = f32[96,128]{1,0:T(8,128)S(1)} collective-permute-done((f32[96,128]{1,0:T(8,128)S(1)}, f32[96,128]{1,0:T(8,128)S(1)}, u32[]{:S(2)}, u32[]{:S(2)}) %collective-permute-start.8) | collective-permute-done | bytes 49184 | tf_op jit(solution)/shard_map/ppermute | solution.py:59
  42.4 0.0 collective-permute-done.9.got_b
  42.4 0.0 copy-done.2
  42.4 0.0 copy-start.3
  42.5 4.5 %shard_map.117 = (f32[8,3,2,8,128]{4,3,2,1,0:T(8,128)S(1)}, f32[8,3,2,8,128]{4,3,2,1,0:T(8,128)S(1)}, f32[32,128]{1,0:T(8,128)}) custom-call(f32[24,8,256]{2,1,0:T(8,128)S(1)} %get-tuple-element.42.wide_planes, f32[40,256]{1,0:T(8,128)S(1)} %get-tuple-element.43.columns, f32[96,128]{1,0:T(8,128)S(1)} %collective-permute-done.8.got_a, ...), custom_call_target="tpu_custom_call" | custom-call | tf_op jit(solution)/shard_map/pallas_call | solution.py:888
  47.0 5.5 %all-to-all-start = ((f32[32,1,128]{2,1,0:T(1,128)}), f32[32,1,128]{2,1,0:T(1,128)S(1)}, u32[]{:S(2)}, u32[]{:S(2)}) async-start(f32[32,1,128]{2,1,0:T(1,128)} %bitcast.2), calls=%async_computation | async-start | bytes 32768 | tf_op jit(solution)/shard_map/all_to_all | solution.py:893
  53.1 6.4 %all-to-all-done = f32[32,1,128]{2,1,0:T(1,128)S(1)} async-done(((f32[32,1,128]{2,1,0:T(1,128)}), f32[32,1,128]{2,1,0:T(1,128)S(1)}, u32[]{:S(2)}, u32[]{:S(2)}) %all-to-all-start) | async-done | bytes 16416 | tf_op jit(solution)/shard_map/all_to_all | solution.py:893
  59.6 1.1 %shard_map.118 = (f32[3,8,8,256]{3,2,1,0:T(8,128)}, f32[3,8,8,256]{3,2,1,0:T(8,128)}, f32[3,8,8,256]{3,2,1,0:T(8,128)}, f32[3,8,8,256]{3,2,1,0:T(8,128)}) custom-call(f32[1]{0:T(128)} %bitcast.5.prev_rz, f32[32,128]{1,0:T(8,128)S(1)} %bitcast.6, f32[8,3,2,8,128]{4,3,2,1,0:T(8,128)S(1)} %get-tuple-element.56.precond, ...), custom_call_target="tpu_custom_call" | custom-call | tf_op jit(solution)/shard_map/pallas_call | solution.py:895
  (8 shorter events, 0.0 us)
Async XLA Ops:
  1.7 7.5 %collective-permute-start = (f32[18,8,256]{2,1,0:T(8,128)S(1)}, f32[18,8,256]{2,1,0:T(8,128)S(1)}, u32[]{:S(2)}, u32[]{:S(2)}) collective-permute-start(f32[18,8,256]{2,1,0:T(8,128)S(1)} %get-tuple-element.33), channel_id=1, source_target_pairs={{0,8},{8,0},{16,24},{24,16},{1,9},{9,1},{17,25},{25,17},{2,10},{10... | collective-permute-start | bytes 442376 | tf_op jit(solution)/shard_map/ppermute | solution.py:59
  4.7 8.2 %collective-permute-start.1 = (f32[18,8,256]{2,1,0:T(8,128)S(1)}, f32[18,8,256]{2,1,0:T(8,128)S(1)}, u32[]{:S(2)}, u32[]{:S(2)}) collective-permute-start(f32[18,8,256]{2,1,0:T(8,128)S(1)} %get-tuple-element.34), channel_id=1, source_target_pairs={{0,24},{8,16},{16,8},{24,0},{1,25},{9,17},{17,9},{25,1},{2,26},{10... | collective-permute-start | bytes 442376 | tf_op jit(solution)/shard_map/ppermute | solution.py:62
  13.0 8.5 %collective-permute-start.2 = (f32[39,8,256]{2,1,0:T(8,128)S(1)}, f32[39,8,256]{2,1,0:T(8,128)S(1)}, u32[]{:S(2)}, u32[]{:S(2)}) collective-permute-start(f32[39,8,256]{2,1,0:T(8,128)S(1)} %get-tuple-element.35), channel_id=1, source_target_pairs={{0,2},{2,0},{4,6},{6,4},{1,3},{3,1},{5,7},{7,5},{8,10},{10,8},{12,... | collective-permute-start | bytes 958472 | tf_op jit(solution)/shard_map/ppermute | solution.py:59
  14.7 14.2 %copy-start.4 = (f32[1,1,48,48]{3,2,1,0:T(8,128)S(1)}, f32[1,1,48,48]{3,2,1,0:T(8,128)}, u32[]{:S(2)}) copy-start(f32[1,1,48,48]{3,2,1,0:T(8,128)} %refs_2_.1) | copy-start | bytes 27652
  14.7 27.8 %copy-start = (f32[3,8,8,256]{3,2,1,0:T(8,128)S(1)}, f32[3,8,8,256]{3,2,1,0:T(8,128)}, u32[]{:S(2)}) copy-start(f32[3,8,8,256]{3,2,1,0:T(8,128)} %res.3) | copy-start | bytes 589828
  14.7 27.8 %copy-start.1 = (f32[3,8,8,256]{3,2,1,0:T(8,128)S(1)}, f32[3,8,8,256]{3,2,1,0:T(8,128)}, u32[]{:S(2)}) copy-start(f32[3,8,8,256]{3,2,1,0:T(8,128)} %prev_d.3) | copy-start | bytes 589828
  14.7 27.8 %copy-start.2 = (f32[3,8,8,256]{3,2,1,0:T(8,128)S(1)}, f32[3,8,8,256]{3,2,1,0:T(8,128)}, u32[]{:S(2)}) copy-start(f32[3,8,8,256]{3,2,1,0:T(8,128)} %prev_i.3) | copy-start | bytes 589828
  14.7 6.8 %collective-permute-start.3 = (f32[39,8,256]{2,1,0:T(8,128)S(1)}, f32[39,8,256]{2,1,0:T(8,128)S(1)}, u32[]{:S(2)}, u32[]{:S(2)}) collective-permute-start(f32[39,8,256]{2,1,0:T(8,128)S(1)} %get-tuple-element.36), channel_id=1, source_target_pairs={{2,4},{4,2},{3,5},{5,3},{10,12},{12,10},{11,13},{13,11},{18,20},{2... | collective-permute-start | bytes 958472 | tf_op jit(solution)/shard_map/ppermute | solution.py:62
  21.7 1.3 %collective-permute-start.4 = (f32[80,128]{1,0:T(8,128)S(1)}, f32[80,128]{1,0:T(8,128)S(1)}, u32[]{:S(2)}, u32[]{:S(2)}) collective-permute-start(f32[80,128]{1,0:T(8,128)S(1)} %shard_map.113), channel_id=1, source_target_pairs={{0,1},{1,0},{2,3},{3,2},{4,5},{5,4},{6,7},{7,6},{8,9},{9,8},{10,11... | collective-permute-start | bytes 122888 | tf_op jit(solution)/shard_map/ppermute | solution.py:59
  27.6 1.3 %collective-permute-start.5 = (f32[104,128]{1,0:T(8,128)S(1)}, f32[104,128]{1,0:T(8,128)S(1)}, u32[]{:S(2)}, u32[]{:S(2)}) collective-permute-start(f32[104,128]{1,0:T(8,128)S(1)} %get-tuple-element.37.refs_0_), channel_id=1, source_target_pairs={{0,1},{1,0},{2,3},{3,2},{4,5},{5,4},{6,7},{7,6},{8,9},{9,8},{10,11... | collective-permute-start | bytes 159752 | tf_op jit(solution)/shard_map/ppermute | solution.py:59
  29.1 3.8 %collective-permute-start.6 = (f32[48,128]{1,0:T(8,128)S(1)}, f32[48,128]{1,0:T(8,128)S(1)}, u32[]{:S(2)}, u32[]{:S(2)}) collective-permute-start(f32[48,128]{1,0:T(8,128)S(1)} %get-tuple-element.40), channel_id=1, source_target_pairs={{0,8},{8,0},{16,24},{24,16},{1,9},{9,1},{17,25},{25,17},{2,10},{10... | collective-permute-start | bytes 73736 | tf_op jit(solution)/shard_map/ppermute | solution.py:59
  30.6 4.7 %collective-permute-start.7 = (f32[48,128]{1,0:T(8,128)S(1)}, f32[48,128]{1,0:T(8,128)S(1)}, u32[]{:S(2)}, u32[]{:S(2)}) collective-permute-start(f32[48,128]{1,0:T(8,128)S(1)} %get-tuple-element.41), channel_id=1, source_target_pairs={{0,24},{8,16},{16,8},{24,0},{1,25},{9,17},{17,9},{25,1},{2,26},{10... | collective-permute-start | bytes 73736 | tf_op jit(solution)/shard_map/ppermute | solution.py:62
  35.5 6.9 %collective-permute-start.8 = (f32[96,128]{1,0:T(8,128)S(1)}, f32[96,128]{1,0:T(8,128)S(1)}, u32[]{:S(2)}, u32[]{:S(2)}) collective-permute-start(f32[96,128]{1,0:T(8,128)S(1)} %get-tuple-element.44), channel_id=1, source_target_pairs={{0,2},{2,0},{4,6},{6,4},{1,3},{3,1},{5,7},{7,5},{8,10},{10,8},{12,... | collective-permute-start | bytes 147464 | tf_op jit(solution)/shard_map/ppermute | solution.py:59
  40.4 2.1 %collective-permute-start.9 = (f32[96,128]{1,0:T(8,128)S(1)}, f32[96,128]{1,0:T(8,128)S(1)}, u32[]{:S(2)}, u32[]{:S(2)}) collective-permute-start(f32[96,128]{1,0:T(8,128)S(1)} %get-tuple-element.45), channel_id=1, source_target_pairs={{2,4},{4,2},{3,5},{5,3},{10,12},{12,10},{11,13},{13,11},{18,20},{2... | collective-permute-start | bytes 147464 | tf_op jit(solution)/shard_map/ppermute | solution.py:62
  42.4 17.1 %copy-start.3 = (f32[3,8,8,256]{3,2,1,0:T(8,128)S(1)}, f32[3,8,8,256]{3,2,1,0:T(8,128)}, u32[]{:S(2)}) copy-start(f32[3,8,8,256]{3,2,1,0:T(8,128)} %sol.1) | copy-start | bytes 589828
  47.0 12.6 %all-to-all-start = ((f32[32,1,128]{2,1,0:T(1,128)}), f32[32,1,128]{2,1,0:T(1,128)S(1)}, u32[]{:S(2)}, u32[]{:S(2)}) async-start(f32[32,1,128]{2,1,0:T(1,128)} %bitcast.2), calls=%async_computation | async-start | bytes 32768 | tf_op jit(solution)/shard_map/all_to_all | solution.py:893

commit v6 on v5

--- a/solution.py
+++ b/solution.py
@@ -62,6 +62,23 @@
     return [got_even, lax.ppermute(odd_pack, axis, pairs(count, True, closed))]
 
 
+def swap_yz(even_packs, odd_packs):
+    count_y, count_z = lax.axis_size("gy"), lax.axis_size("gz")
+    got = []
+    for odd_z in range(len(even_packs)):
+        found = []
+        for odd_y, packs in enumerate((even_packs, odd_packs)):
+            pairs_z = pairs(count_z, odd_z, True)
+            made = [
+                (a * count_z + c, b * count_z + d)
+                for a, b in pairs(count_y, odd_y, False)
+                for c, d in pairs_z
+            ]
+            found.append(lax.ppermute(packs[odd_z], ("gy", "gz"), made))
+        got.append(found)
+    return got
+
+
 def is_even(axis):
     return lax.rem(lax.axis_index(axis), 2) == 0
 
@@ -194,8 +211,9 @@
 E4_TILES = E_PLANES // 2
 E2_TILES = E_PLANES // 4
 Y_PACK = R_TILES + E4_TILES + E2_TILES
-Z_TILES = COMPS * (X + 2 * RIM) * (ROWS // 8) + E_PLANES * 3
+Z_TILES = COMPS * (X + 2 * RIM) + E_PLANES
 Z_PACK = -(-Z_TILES // 16) * 8
+YZ_PACK = -(-Y_PACK // 16) * 8
 
 
 def pack_x_body(
@@ -239,9 +257,9 @@
         pack[COMPS * RIM :] = young[pl.ds(high * (X - WIDE), WIDE)]
 
 
-def x_planes(res, young, got_x, lanes=slice(None)):
+def x_planes(res, young, got_x):
     lower, upper = from_sides(got_x, "gx")
-    whole = slice(None)
+    whole = lanes = slice(None)
 
     def res_plane(c, i):
         if i < RIM:
@@ -260,10 +278,22 @@
     return res_plane, young_plane
 
 
+def pack_lanes(pack, tiles, high):
+    lane = lane_of((8, 128))
+    for first in range(0, len(tiles), 16):
+        packed = None
+        for j, tile in enumerate(tiles[first : first + 16]):
+            edge = jnp.where(high == 1, tile[:, Z - 128 :], tile[:, :128])
+            moved = pltpu.roll(edge, lax.rem(8 * j + 8 * high, 128), 1)
+            packed = moved if j == 0 else jnp.where(lane < 8 * j, packed, moved)
+        pack[first // 2 : first // 2 + 8] = packed
+
+
 def pack_y_body(res, young, got_a, got_b, pack_even, pack_odd):
     res_plane, young_plane = x_planes(res, young, (got_a, got_b))
     row = row_of((Y, Z))
     even = is_even("gy")
+
 
     def put(tile, low, high):
         pack_even[tile] = jnp.where(even, high, low)
@@ -292,15 +322,22 @@
         put(R_TILES + E4_TILES + j, low, high)
 
 
-def xy_planes(res, young, got_x, got_y, lanes, width):
-    res_plane, young_plane = x_planes(res, young, got_x, lanes)
-    lower, upper = from_sides(got_y, "gy")
+def pack_z_body(n_z, res, young, got_a, got_b, sent_even, sent_odd, *packs):
+    res_plane, young_plane = x_planes(res, young, (got_a, got_b))
+    own = [res_plane(c, i) for c in range(COMPS) for i in range(X + 2 * RIM)]
+    own += [young_plane(i) for i in range(E_PLANES)]
+    high_first = jnp.where(is_even("gz"), 1, 0)
+    for k, high in enumerate((high_first, 1 - high_first)[:n_z]):
+        pack_lanes(packs[k], own, high)
+        for y, sent in enumerate((sent_even, sent_odd)):
+            pack_lanes(packs[n_z * (1 + y) + k], [sent[t] for t in range(Y_PACK)], high)
+
+
+def y_tiles(res_plane, young_plane, lower, upper, width):
     row = row_of((Y, width))
-    whole = slice(None)
 
     def with_rims(own, tile, second):
-        key = (tile, whole, lanes)
-        low, high = lower(key), upper(key)
+        low, high = lower(tile), upper(tile)
         at = 2 if second else 0
         even = jnp.where(row < 6, up(high, 4 - at), up(low, 6 - at))
         odd = jnp.where(row < 6, up(high, -at), up(low, 2 - at))
@@ -310,7 +347,7 @@
         return with_rims(res_plane(c, i), c * X + i % X, i >= X)
 
     def young_tiles(i):
-        two = (R_TILES + E4_TILES + i // 4, whole, lanes)
+        two = R_TILES + E4_TILES + i // 4
         k = i % 4
         low2, high2 = up(lower(two), -k), up(upper(two), 1 - k)
         side = jnp.where(row % 4 == 0, low2, jnp.where(row % 4 == 1, high2, 0.0))
@@ -319,38 +356,22 @@
     return res_tiles, young_tiles
 
 
-def pack_z_body(res, young, xa, xb, ya, yb, *packs):
-    high_first = jnp.where(is_even("gz"), 1, 0)
-    lane = lane_of((8, 128))
-    for pack, high in zip(packs, (high_first, 1 - high_first)):
-        lanes = pl.ds(pl.multiple_of(high * (Z - 128), 128), 128)
-        res_tiles, young_tiles = xy_planes(res, young, (xa, xb), (ya, yb), lanes, 128)
-        tiles = [t for c in range(COMPS) for i in range(X + 2 * RIM) for t in res_tiles(c, i)]
-        tiles += [t for i in range(E_PLANES) for t in young_tiles(i)]
-        for first in range(0, len(tiles), 16):
-            packed = None
-            for j, tile in enumerate(tiles[first : first + 16]):
-                moved = pltpu.roll(tile, lax.rem(8 * j + 8 * high, 128), 1)
-                packed = moved if j == 0 else jnp.where(lane < 8 * j, packed, moved)
-            pack[first // 2 : first // 2 + 8] = packed
-
-
-def z_rims(got_z):
+def z_rims(sources):
     lane = lane_of((8, 128))
     even = is_even("gz")
 
-    def piece(got, t, right):
+    def piece(source, t, right):
         start = jnp.where(right, 0, 120)
-        tile = got[8 * (t // 16) : 8 * (t // 16) + 8, :]
+        tile = source((slice(8 * (t // 16), 8 * (t // 16) + 8), slice(None)))
         moved = pltpu.roll(tile, lax.rem(start + 128 - 8 * (t % 16), 128), 1)
         inside = jnp.logical_and(lane >= start, lane < start + 8)
         return jnp.where(inside, moved, 0.0)
 
     def rim(t):
-        first = piece(got_z[0], t, even)
-        if len(got_z) == 1:
+        first = piece(sources[0], t, even)
+        if len(sources) == 1:
             return first
-        second = piece(got_z[1], t, jnp.logical_not(even))
+        second = piece(sources[1], t, jnp.logical_not(even))
         return first + jnp.where(inner("gz"), second, 0.0)
 
     return rim
@@ -389,29 +410,43 @@
                 e_target[c, i + k] = e[0, i + k] * value
         return carry
 
-    lax.fori_loop(0, (last - first) // 2, body, 0)
+    lax.fori_loop(0, (last - first) // 2, body, 0, unroll=True)
 
 
 def smooth_body(n_z, *refs):
+    n_in = 6 + 3 * n_z
     res, young, xa, xb, ya, yb = refs[:6]
     got_z = refs[6 : 6 + n_z]
-    s0, s1, e, c1, w, em, em_side, c1m, wm, pack = refs[6 + n_z : 16 + n_z]
-    wide, wide_z, r, es0, es1, to_pool = refs[16 + n_z :]
-
-    res_tiles, young_tiles = xy_planes(res, young, (xa, xb), (ya, yb), slice(None), Z)
-    rim = z_rims(got_z)
-    at = 0
+    got_yz = [refs[6 + n_z + 2 * k : 8 + n_z + 2 * k] for k in range(n_z)]
+    s0, s1, e, c1, w, em, em_side, c1m, wm, pack = refs[n_in : n_in + 10]
+    wide, wide_z, r, es0, es1, to_pool = refs[n_in + 10 :]
+
+    whole = slice(None)
+    lower, upper = from_sides((ya, yb), "gy")
+    res_tiles, young_tiles = y_tiles(
+        *x_planes(res, young, (xa, xb)),
+        lambda t: lower((t, whole, whole)),
+        lambda t: upper((t, whole, whole)),
+        Z,
+    )
+    own_rim = z_rims([functools.partial(lambda ref, key: ref[key], ref) for ref in got_z])
+    corners = [from_sides(got, "gy") for got in got_yz]
+    res_rims, young_rims = y_tiles(
+        lambda c, i: own_rim(c * PLANES + i),
+        lambda i: own_rim(COMPS * PLANES + i),
+        z_rims([low for low, _ in corners]),
+        z_rims([high for _, high in corners]),
+        128,
+    )
     for c in range(COMPS):
         for i in range(PLANES):
-            for t, tile in enumerate(res_tiles(c, i)):
+            for t, (tile, rim) in enumerate(zip(res_tiles(c, i), res_rims(c, i))):
                 r[c, i, 8 * t : 8 * t + 8, :Z] = tile
-                r[c, i, 8 * t : 8 * t + 8, Z:] = rim(at)
-                at += 1
+                r[c, i, 8 * t : 8 * t + 8, Z:] = rim
     for i in range(E_PLANES):
-        for t, tile in enumerate(young_tiles(i)):
+        for t, (tile, rim) in enumerate(zip(young_tiles(i), young_rims(i))):
             wide[i, 8 * t : 8 * t + 8, :Z] = tile * 0.0125
-            wide[i, 8 * t : 8 * t + 8, Z:] = rim(at) * 0.0125
-            at += 1
+            wide[i, 8 * t : 8 * t + 8, Z:] = rim * 0.0125
 
     def shift(k, carry):
         for i in (2 * k, 2 * k + 1):
@@ -446,7 +481,7 @@
                 es0[c, i] = centre * value
         return carry
 
-    lax.fori_loop(0, PLANES // 2, prepare, 0)
+    lax.fori_loop(0, PLANES // 2, prepare, 0, unroll=True)
     e = e.at[:, 2 : 2 + PLANES]
     sweep(s0, es0, s1, es1, s0, c1, e, w, 1, PLANES - 1)
 
@@ -459,7 +494,7 @@
             to_pool[pl.ds(start, 8)] = total[:8] + total[8:]
         return carry
 
-    lax.fori_loop(0, 6, residue, 0)
+    lax.fori_loop(0, 6, residue, 0, unroll=True)
 
     pooled = dot_exact_weights(to_pool[...], pool_matrix(0.5))
     pooled = [pooled[8 * t : 8 * t + 8] for t in range(COMPS * 6 + 2 * EM_PLANES)]
@@ -683,7 +718,7 @@
             es2[c, i] = e[0, i] * value
         return carry
 
-    lax.fori_loop(1, PLANES - 1, add_up, 0)
+    lax.fori_loop(1, PLANES - 1, add_up, 0, unroll=2)
     sweep(s2, es2, s3, es3, s0, c1, e, w, 2, PLANES - 2)
     sweep(s3, es3, p, ep, s0, c1, e, w, 3, PLANES - 3)
 
@@ -702,7 +737,7 @@
             put_rows(operated, 2 * n + k, [COUPLING[c] * parts[c][k] for c in range(COMPS)])
         return carry
 
-    lax.fori_loop(0, X // 2, image, 0)
+    lax.fori_loop(0, X // 2, image, 0, unroll=True)
     found = [[], [], [], []]
     for x in range(X):
         for c in range(COMPS):
@@ -799,7 +834,7 @@
             pltpu.VMEM(FIELD, F32),
             pltpu.VMEM((COMPS * 6 * 8 + 16 * EM_PLANES, LANES), F32),
         ],
-        n_in=6 + n_z,
+        n_in=6 + 3 * n_z,
         vmem=30 << 20,
     )
 
@@ -851,11 +886,19 @@
     )(*[in_hbm(a) for a in (stiffness_table, density_index, residual)])
     got_x = swap("gx", px, qx)
     py, qy = call(pack_y_body, [shape(Y_PACK, Y, Z)] * 2, n_in=4)(res, young, *got_x)
+    packs = call(
+        functools.partial(pack_z_body, n_z),
+        [shape(Z_PACK, 128)] * n_z + [shape(YZ_PACK, 128)] * (2 * n_z),
+        n_in=6,
+    )(res, young, *got_x, py, qy)
     got_y = swap("gy", py, qy, closed=False)
-    packs = call(pack_z_body, [shape(Z_PACK, 128)] * n_z, n_in=6)(res, young, *got_x, *got_y)
-    got_z = swap("gz", packs[0], packs[-1])
-
-    s0, s1, e, c1, w, em, em_side, c1m, wm, pack = smooth_call(n_z)(res, young, *got_x, *got_y, *got_z)
+    got_z = swap("gz", packs[0], packs[n_z - 1])
+    got_yz = swap_yz(packs[n_z : 2 * n_z], packs[2 * n_z :])
+    corners = [got for both in got_yz for got in both]
+
+    s0, s1, e, c1, w, em, em_side, c1m, wm, pack = smooth_call(n_z)(
+        res, young, *got_x, *got_y, *got_z, *corners
+    )
 
     got_z = swap("gz", pack, pack)
     gathered = []

time: 60.9 us -> 58.7 us (0.964)
  waiting for transfers between devices: 26.9 us -> 20.6 us
  starting transfers between devices: 20.4 us -> 25.3 us
  Pallas kernels: 12 us -> 11.2 us
    ppermute x6, waiting for transfers between devices: 14.4 us -> 7.31 us  [swap(): got_even = lax.ppermute(even_pack, axis, pairs(count, False, closed))]
    ppermute x0 -> x2, starting transfers between devices: none -> 5.15 us  [swap_yz(): found.append(lax.ppermute(packs[odd_z], ('gy', 'gz'), made))]
    ppermute x0 -> x2, waiting for transfers between devices: none -> 0.75 us  [swap_yz(): found.append(lax.ppermute(packs[odd_z], ('gy', 'gz'), made))]
  transfers between devices with their start and end apart: 11 -> 13, of which waited for: 9 -> 8; matrix products, arithmetic and copies ran while one was open for 0% -> 0% of each run, Pallas kernels for 0% -> 0%
where the time goes in v6:
time: 58.7 us; the launch traced here: 58.5 us
  starting transfers between devices  25.3 us (43%)
  waiting for transfers between devices  20.6 us (35%)
  Pallas kernels  11.2 us (19%)
  between operations  1.39 us (2%)
    ppermute x6, starting transfers between devices, swap(): got_even = lax.ppermute(even_pack, axis, pairs(count, False, closed))  11 us
    ppermute x6, waiting for transfers between devices, swap(): got_even = lax.ppermute(even_pack, axis, pairs(count, False, closed))  7.31 us
    all_to_all x1, waiting for transfers between devices, on_device(): sums = lax.all_to_all(sums, ALL, 0, 0, tiled=True)  6.42 us
    ppermute x4, waiting for transfers between devices, swap(): return [got_even, lax.ppermute(odd_pack, axis, pairs(count, True, closed))]  6.09 us
    all_to_all x1, starting transfers between devices, on_device(): sums = lax.all_to_all(sums, ALL, 0, 0, tiled=True)  5.52 us
    ppermute x2, starting transfers between devices, swap_yz(): found.append(lax.ppermute(packs[odd_z], ('gy', 'gz'), made))  5.15 us
    pallas_call x1, Pallas kernels, on_device(): smooth_call(n_z)(res, young, *got_x, *got_y, *got_z, *corners)  4.27 us
    pallas_call x1, Pallas kernels, on_device(): finish_call(n_all)  4.01 us
  transfers between devices with their start and end apart: 13, of which 8 were waited for; matrix products, arithmetic and copies ran while one was open for 0% of the time, Pallas kernels for 0%

profile of v6, /device:TPU:0, one launch (start us, length us, event | category | flops | bytes accessed | tf_op | source)
XLA Modules:
  0.0 58.5 jit_solution(12833361352692591247)
XLA Ops:
  0.6 1.1 %shard_map.111 = (f32[3,8,8,256]{3,2,1,0:T(8,128)S(1)}, f32[8,8,256]{2,1,0:T(8,128)S(1)}, f32[18,8,256]{2,1,0:T(8,128)S(1)}, f32[18,8,256]{2,1,0:T(8,128)S(1)}) custom-call(f32[16]{0:T(128)} %table_in.1, s32[8,8,256]{2,1,0:T(8,128)} %index_in.1, f32[3,8,8,256]{3,2,1,0:T(8,128)} %res.3), custom_call_target="tpu_custom_call" | custom-call | tf_op jit(solution)/shard_map/pallas_call | solution.py:874
  1.7 3.0 %collective-permute-start = (f32[18,8,256]{2,1,0:T(8,128)S(1)}, f32[18,8,256]{2,1,0:T(8,128)S(1)}, u32[]{:S(2)}, u32[]{:S(2)}) collective-permute-start(f32[18,8,256]{2,1,0:T(8,128)S(1)} %get-tuple-element.36), channel_id=1, source_target_pairs={{0,8},{8,0},{16,24},{24,16},{1,9},{9,1},{17,25},{25,17},{2,10},{10... | collective-permute-start | bytes 442376 | tf_op jit(solution)/shard_map/ppermute | solution.py:59
  4.7 1.5 %collective-permute-start.1 = (f32[18,8,256]{2,1,0:T(8,128)S(1)}, f32[18,8,256]{2,1,0:T(8,128)S(1)}, u32[]{:S(2)}, u32[]{:S(2)}) collective-permute-start(f32[18,8,256]{2,1,0:T(8,128)S(1)} %get-tuple-element.37), channel_id=1, source_target_pairs={{0,24},{8,16},{16,8},{24,0},{1,25},{9,17},{17,9},{25,1},{2,26},{10... | collective-permute-start | bytes 442376 | tf_op jit(solution)/shard_map/ppermute | solution.py:62
  6.2 3.0 %collective-permute-done.got_a.refs_2_ = f32[18,8,256]{2,1,0:T(8,128)S(1)} collective-permute-done((f32[18,8,256]{2,1,0:T(8,128)S(1)}, f32[18,8,256]{2,1,0:T(8,128)S(1)}, u32[]{:S(2)}, u32[]{:S(2)}) %collective-permute-start) | collective-permute-done | bytes 147488 | tf_op jit(solution)/shard_map/ppermute | solution.py:59
  9.2 3.7 %collective-permute-done.1.got_b.refs_3_ = f32[18,8,256]{2,1,0:T(8,128)S(1)} collective-permute-done((f32[18,8,256]{2,1,0:T(8,128)S(1)}, f32[18,8,256]{2,1,0:T(8,128)S(1)}, u32[]{:S(2)}, u32[]{:S(2)}) %collective-permute-start.1) | collective-permute-done | bytes 147488 | tf_op jit(solution)/shard_map/ppermute | solution.py:62
  12.9 0.1 shard_map.112
  13.0 1.6 %collective-permute-start.2 = (f32[39,8,256]{2,1,0:T(8,128)S(1)}, f32[39,8,256]{2,1,0:T(8,128)S(1)}, u32[]{:S(2)}, u32[]{:S(2)}) collective-permute-start(f32[39,8,256]{2,1,0:T(8,128)S(1)} %get-tuple-element.38.sent_even), channel_id=1, source_target_pairs={{0,2},{2,0},{4,6},{6,4},{1,3},{3,1},{5,7},{7,5},{8,10},{10,8},{12,... | collective-permute-start | bytes 958472 | tf_op jit(solution)/shard_map/ppermute | solution.py:59
  14.7 0.8 %collective-permute-start.3 = (f32[39,8,256]{2,1,0:T(8,128)S(1)}, f32[39,8,256]{2,1,0:T(8,128)S(1)}, u32[]{:S(2)}, u32[]{:S(2)}) collective-permute-start(f32[39,8,256]{2,1,0:T(8,128)S(1)} %get-tuple-element.39.sent_odd), channel_id=1, source_target_pairs={{2,4},{4,2},{3,5},{5,3},{10,12},{12,10},{11,13},{13,11},{18,20},{2... | collective-permute-start | bytes 958472 | tf_op jit(solution)/shard_map/ppermute | solution.py:62
  15.5 0.2 shard_map.113
  15.7 0.1 collective-permute-start.4
  15.8 4.5 %collective-permute-start.5 = (f32[24,128]{1,0:T(8,128)S(1)}, f32[24,128]{1,0:T(8,128)S(1)}, u32[]{:S(2)}, u32[]{:S(2)}) collective-permute-start(f32[24,128]{1,0:T(8,128)S(1)} %get-tuple-element.41), channel_id=1, source_target_pairs={{0,3},{1,2},{2,1},{3,0},{4,7},{5,6},{6,5},{7,4},{8,11},{9,10},{10,... | collective-permute-start | bytes 36872 | tf_op jit(solution)/shard_map/ppermute | solution.py:77
  20.3 0.7 %collective-permute-start.6 = (f32[24,128]{1,0:T(8,128)S(1)}, f32[24,128]{1,0:T(8,128)S(1)}, u32[]{:S(2)}, u32[]{:S(2)}) collective-permute-start(f32[24,128]{1,0:T(8,128)S(1)} %get-tuple-element.42), channel_id=1, source_target_pairs={{2,5},{3,4},{4,3},{5,2},{10,13},{11,12},{12,11},{13,10},{18,21},{1... | collective-permute-start | bytes 36872 | tf_op jit(solution)/shard_map/ppermute | solution.py:77
  21.0 0.7 %collective-permute-done.5.refs_7_ = f32[24,128]{1,0:T(8,128)S(1)} collective-permute-done((f32[24,128]{1,0:T(8,128)S(1)}, f32[24,128]{1,0:T(8,128)S(1)}, u32[]{:S(2)}, u32[]{:S(2)}) %collective-permute-start.5) | collective-permute-done | bytes 12320 | tf_op jit(solution)/shard_map/ppermute | solution.py:77
  21.7 0.0 collective-permute-done.6.refs_8_
  21.7 0.0 collective-permute-done.4.refs_6_
  21.7 4.3 %shard_map.114 = (f32[3,16,16,384]{3,2,1,0:T(8,128)S(1)}, f32[3,16,16,384]{3,2,1,0:T(8,128)S(1)}, f32[3,20,16,384]{3,2,1,0:T(8,128)S(1)}, f32[16,16,384]{2,1,0:T...) custom-call(f32[3,8,8,256]{3,2,1,0:T(8,128)S(1)} %get-tuple-element., ...), custom_call_target="tpu_custom_call" | custom-call | tf_op jit(solution)/shard_map/pallas_call | solution.py:899
  26.0 0.1 collective-permute-start.7
  26.2 1.2 %collective-permute-done.7.refs_1_ = f32[104,128]{1,0:T(8,128)S(1)} collective-permute-done((f32[104,128]{1,0:T(8,128)S(1)}, f32[104,128]{1,0:T(8,128)S(1)}, u32[]{:S(2)}, u32[]{:S(2)}) %collective-permute-start.7) | collective-permute-done | bytes 53280 | tf_op jit(solution)/shard_map/ppermute | solution.py:59
  27.3 0.2 shard_map.115
  27.6 1.5 %collective-permute-start.8 = (f32[48,128]{1,0:T(8,128)S(1)}, f32[48,128]{1,0:T(8,128)S(1)}, u32[]{:S(2)}, u32[]{:S(2)}) collective-permute-start(f32[48,128]{1,0:T(8,128)S(1)} %get-tuple-element.46), channel_id=1, source_target_pairs={{0,8},{8,0},{16,24},{24,16},{1,9},{9,1},{17,25},{25,17},{2,10},{10... | collective-permute-start | bytes 73736 | tf_op jit(solution)/shard_map/ppermute | solution.py:59
  29.1 0.6 %collective-permute-start.9 = (f32[48,128]{1,0:T(8,128)S(1)}, f32[48,128]{1,0:T(8,128)S(1)}, u32[]{:S(2)}, u32[]{:S(2)}) collective-permute-start(f32[48,128]{1,0:T(8,128)S(1)} %get-tuple-element.47), channel_id=1, source_target_pairs={{0,24},{8,16},{16,8},{24,0},{1,25},{9,17},{17,9},{25,1},{2,26},{10... | collective-permute-start | bytes 73736 | tf_op jit(solution)/shard_map/ppermute | solution.py:62
  29.7 1.7 %collective-permute-done.8.got_a = f32[48,128]{1,0:T(8,128)S(1)} collective-permute-done((f32[48,128]{1,0:T(8,128)S(1)}, f32[48,128]{1,0:T(8,128)S(1)}, u32[]{:S(2)}, u32[]{:S(2)}) %collective-permute-start.8) | collective-permute-done | bytes 24608 | tf_op jit(solution)/shard_map/ppermute | solution.py:59
  31.4 2.4 %collective-permute-done.9.got_b = f32[48,128]{1,0:T(8,128)S(1)} collective-permute-done((f32[48,128]{1,0:T(8,128)S(1)}, f32[48,128]{1,0:T(8,128)S(1)}, u32[]{:S(2)}, u32[]{:S(2)}) %collective-permute-start.9) | collective-permute-done | bytes 24608 | tf_op jit(solution)/shard_map/ppermute | solution.py:62
  33.8 0.2 shard_map.116
  34.0 4.7 %collective-permute-start.10 = (f32[96,128]{1,0:T(8,128)S(1)}, f32[96,128]{1,0:T(8,128)S(1)}, u32[]{:S(2)}, u32[]{:S(2)}) collective-permute-start(f32[96,128]{1,0:T(8,128)S(1)} %get-tuple-element.50), channel_id=1, source_target_pairs={{0,2},{2,0},{4,6},{6,4},{1,3},{3,1},{5,7},{7,5},{8,10},{10,8},{12,... | collective-permute-start | bytes 147464 | tf_op jit(solution)/shard_map/ppermute | solution.py:59
  38.6 0.7 %collective-permute-start.11 = (f32[96,128]{1,0:T(8,128)S(1)}, f32[96,128]{1,0:T(8,128)S(1)}, u32[]{:S(2)}, u32[]{:S(2)}) collective-permute-start(f32[96,128]{1,0:T(8,128)S(1)} %get-tuple-element.51), channel_id=1, source_target_pairs={{2,4},{4,2},{3,5},{5,3},{10,12},{12,10},{11,13},{13,11},{18,20},{2... | collective-permute-start | bytes 147464 | tf_op jit(solution)/shard_map/ppermute | solution.py:62
  39.3 1.4 %collective-permute-done.10.got_a = f32[96,128]{1,0:T(8,128)S(1)} collective-permute-done((f32[96,128]{1,0:T(8,128)S(1)}, f32[96,128]{1,0:T(8,128)S(1)}, u32[]{:S(2)}, u32[]{:S(2)}) %collective-permute-start.10) | collective-permute-done | bytes 49184 | tf_op jit(solution)/shard_map/ppermute | solution.py:59
  40.7 0.0 copy-start.3
  40.7 4.0 %shard_map.117 = (f32[8,3,2,8,128]{4,3,2,1,0:T(8,128)S(1)}, f32[8,3,2,8,128]{4,3,2,1,0:T(8,128)S(1)}, f32[32,128]{1,0:T(8,128)}) custom-call(f32[24,8,256]{2,1,0:T(8,128)S(1)} %get-tuple-element.48.wide_planes, f32[40,256]{1,0:T(8,128)S(1)} %get-tuple-element.49.columns, f32[96,128]{1,0:T(8,128)S(1)} %collective-permute-done.10.got_a, ...), custom_call_target="tpu_custom_call" | custom-call | tf_op jit(solution)/shard_map/pallas_call | solution.py:931
  44.7 5.5 %all-to-all-start = ((f32[32,1,128]{2,1,0:T(1,128)}), f32[32,1,128]{2,1,0:T(1,128)S(1)}, u32[]{:S(2)}, u32[]{:S(2)}) async-start(f32[32,1,128]{2,1,0:T(1,128)} %bitcast.2), calls=%async_computation | async-start | bytes 32768 | tf_op jit(solution)/shard_map/all_to_all | solution.py:936
  50.9 6.4 %all-to-all-done = f32[32,1,128]{2,1,0:T(1,128)S(1)} async-done(((f32[32,1,128]{2,1,0:T(1,128)}), f32[32,1,128]{2,1,0:T(1,128)S(1)}, u32[]{:S(2)}, u32[]{:S(2)}) %all-to-all-start) | async-done | bytes 16416 | tf_op jit(solution)/shard_map/all_to_all | solution.py:936
  57.3 1.1 %shard_map.118 = (f32[3,8,8,256]{3,2,1,0:T(8,128)}, f32[3,8,8,256]{3,2,1,0:T(8,128)}, f32[3,8,8,256]{3,2,1,0:T(8,128)}, f32[3,8,8,256]{3,2,1,0:T(8,128)}) custom-call(f32[1]{0:T(128)} %bitcast.5.prev_rz, f32[32,128]{1,0:T(8,128)S(1)} %bitcast.6, f32[8,3,2,8,128]{4,3,2,1,0:T(8,128)S(1)} %get-tuple-element.62.precond, ...), custom_call_target="tpu_custom_call" | custom-call | tf_op jit(solution)/shard_map/pallas_call | solution.py:938
  (12 shorter events, 0.0 us)
Async XLA Ops:
  1.7 7.5 %collective-permute-start = (f32[18,8,256]{2,1,0:T(8,128)S(1)}, f32[18,8,256]{2,1,0:T(8,128)S(1)}, u32[]{:S(2)}, u32[]{:S(2)}) collective-permute-start(f32[18,8,256]{2,1,0:T(8,128)S(1)} %get-tuple-element.36), channel_id=1, source_target_pairs={{0,8},{8,0},{16,24},{24,16},{1,9},{9,1},{17,25},{25,17},{2,10},{10... | collective-permute-start | bytes 442376 | tf_op jit(solution)/shard_map/ppermute | solution.py:59
  4.7 8.2 %collective-permute-start.1 = (f32[18,8,256]{2,1,0:T(8,128)S(1)}, f32[18,8,256]{2,1,0:T(8,128)S(1)}, u32[]{:S(2)}, u32[]{:S(2)}) collective-permute-start(f32[18,8,256]{2,1,0:T(8,128)S(1)} %get-tuple-element.37), channel_id=1, source_target_pairs={{0,24},{8,16},{16,8},{24,0},{1,25},{9,17},{17,9},{25,1},{2,26},{10... | collective-permute-start | bytes 442376 | tf_op jit(solution)/shard_map/ppermute | solution.py:62
  13.0 8.7 %collective-permute-start.2 = (f32[39,8,256]{2,1,0:T(8,128)S(1)}, f32[39,8,256]{2,1,0:T(8,128)S(1)}, u32[]{:S(2)}, u32[]{:S(2)}) collective-permute-start(f32[39,8,256]{2,1,0:T(8,128)S(1)} %get-tuple-element.38.sent_even), channel_id=1, source_target_pairs={{0,2},{2,0},{4,6},{6,4},{1,3},{3,1},{5,7},{7,5},{8,10},{10,8},{12,... | collective-permute-start | bytes 958472 | tf_op jit(solution)/shard_map/ppermute | solution.py:59
  14.7 12.7 %copy-start.4 = (f32[1,1,48,48]{3,2,1,0:T(8,128)S(1)}, f32[1,1,48,48]{3,2,1,0:T(8,128)}, u32[]{:S(2)}) copy-start(f32[1,1,48,48]{3,2,1,0:T(8,128)} %refs_2_.1) | copy-start | bytes 27652
  14.7 26.0 %copy-start = (f32[3,8,8,256]{3,2,1,0:T(8,128)S(1)}, f32[3,8,8,256]{3,2,1,0:T(8,128)}, u32[]{:S(2)}) copy-start(f32[3,8,8,256]{3,2,1,0:T(8,128)} %res.3) | copy-start | bytes 589828
  14.7 26.0 %copy-start.1 = (f32[3,8,8,256]{3,2,1,0:T(8,128)S(1)}, f32[3,8,8,256]{3,2,1,0:T(8,128)}, u32[]{:S(2)}) copy-start(f32[3,8,8,256]{3,2,1,0:T(8,128)} %prev_d.3) | copy-start | bytes 589828
  14.7 26.0 %copy-start.2 = (f32[3,8,8,256]{3,2,1,0:T(8,128)S(1)}, f32[3,8,8,256]{3,2,1,0:T(8,128)}, u32[]{:S(2)}) copy-start(f32[3,8,8,256]{3,2,1,0:T(8,128)} %prev_i.3) | copy-start | bytes 589828
  14.7 7.1 %collective-permute-start.3 = (f32[39,8,256]{2,1,0:T(8,128)S(1)}, f32[39,8,256]{2,1,0:T(8,128)S(1)}, u32[]{:S(2)}, u32[]{:S(2)}) collective-permute-start(f32[39,8,256]{2,1,0:T(8,128)S(1)} %get-tuple-element.39.sent_odd), channel_id=1, source_target_pairs={{2,4},{4,2},{3,5},{5,3},{10,12},{12,10},{11,13},{13,11},{18,20},{2... | collective-permute-start | bytes 958472 | tf_op jit(solution)/shard_map/ppermute | solution.py:62
  15.7 6.0 %collective-permute-start.4 = (f32[40,128]{1,0:T(8,128)S(1)}, f32[40,128]{1,0:T(8,128)S(1)}, u32[]{:S(2)}, u32[]{:S(2)}) collective-permute-start(f32[40,128]{1,0:T(8,128)S(1)} %get-tuple-element.40), channel_id=1, source_target_pairs={{0,1},{1,0},{2,3},{3,2},{4,5},{5,4},{6,7},{7,6},{8,9},{9,8},{10,11... | collective-permute-start | bytes 61448 | tf_op jit(solution)/shard_map/ppermute | solution.py:59
  15.8 5.9 %collective-permute-start.5 = (f32[24,128]{1,0:T(8,128)S(1)}, f32[24,128]{1,0:T(8,128)S(1)}, u32[]{:S(2)}, u32[]{:S(2)}) collective-permute-start(f32[24,128]{1,0:T(8,128)S(1)} %get-tuple-element.41), channel_id=1, source_target_pairs={{0,3},{1,2},{2,1},{3,0},{4,7},{5,6},{6,5},{7,4},{8,11},{9,10},{10,... | collective-permute-start | bytes 36872 | tf_op jit(solution)/shard_map/ppermute | solution.py:77
  20.3 1.4 %collective-permute-start.6 = (f32[24,128]{1,0:T(8,128)S(1)}, f32[24,128]{1,0:T(8,128)S(1)}, u32[]{:S(2)}, u32[]{:S(2)}) collective-permute-start(f32[24,128]{1,0:T(8,128)S(1)} %get-tuple-element.42), channel_id=1, source_target_pairs={{2,5},{3,4},{4,3},{5,2},{10,13},{11,12},{12,11},{13,10},{18,21},{1... | collective-permute-start | bytes 36872 | tf_op jit(solution)/shard_map/ppermute | solution.py:77
  26.0 1.3 %collective-permute-start.7 = (f32[104,128]{1,0:T(8,128)S(1)}, f32[104,128]{1,0:T(8,128)S(1)}, u32[]{:S(2)}, u32[]{:S(2)}) collective-permute-start(f32[104,128]{1,0:T(8,128)S(1)} %get-tuple-element.43.refs_0_), channel_id=1, source_target_pairs={{0,1},{1,0},{2,3},{3,2},{4,5},{5,4},{6,7},{7,6},{8,9},{9,8},{10,11... | collective-permute-start | bytes 159752 | tf_op jit(solution)/shard_map/ppermute | solution.py:59
  27.6 3.8 %collective-permute-start.8 = (f32[48,128]{1,0:T(8,128)S(1)}, f32[48,128]{1,0:T(8,128)S(1)}, u32[]{:S(2)}, u32[]{:S(2)}) collective-permute-start(f32[48,128]{1,0:T(8,128)S(1)} %get-tuple-element.46), channel_id=1, source_target_pairs={{0,8},{8,0},{16,24},{24,16},{1,9},{9,1},{17,25},{25,17},{2,10},{10... | collective-permute-start | bytes 73736 | tf_op jit(solution)/shard_map/ppermute | solution.py:59
  29.1 4.7 %collective-permute-start.9 = (f32[48,128]{1,0:T(8,128)S(1)}, f32[48,128]{1,0:T(8,128)S(1)}, u32[]{:S(2)}, u32[]{:S(2)}) collective-permute-start(f32[48,128]{1,0:T(8,128)S(1)} %get-tuple-element.47), channel_id=1, source_target_pairs={{0,24},{8,16},{16,8},{24,0},{1,25},{9,17},{17,9},{25,1},{2,26},{10... | collective-permute-start | bytes 73736 | tf_op jit(solution)/shard_map/ppermute | solution.py:62
  34.0 6.7 %collective-permute-start.10 = (f32[96,128]{1,0:T(8,128)S(1)}, f32[96,128]{1,0:T(8,128)S(1)}, u32[]{:S(2)}, u32[]{:S(2)}) collective-permute-start(f32[96,128]{1,0:T(8,128)S(1)} %get-tuple-element.50), channel_id=1, source_target_pairs={{0,2},{2,0},{4,6},{6,4},{1,3},{3,1},{5,7},{7,5},{8,10},{10,8},{12,... | collective-permute-start | bytes 147464 | tf_op jit(solution)/shard_map/ppermute | solution.py:59
  38.6 2.1 %collective-permute-start.11 = (f32[96,128]{1,0:T(8,128)S(1)}, f32[96,128]{1,0:T(8,128)S(1)}, u32[]{:S(2)}, u32[]{:S(2)}) collective-permute-start(f32[96,128]{1,0:T(8,128)S(1)} %get-tuple-element.51), channel_id=1, source_target_pairs={{2,4},{4,2},{3,5},{5,3},{10,12},{12,10},{11,13},{13,11},{18,20},{2... | collective-permute-start | bytes 147464 | tf_op jit(solution)/shard_map/ppermute | solution.py:62
  40.7 16.6 %copy-start.3 = (f32[3,8,8,256]{3,2,1,0:T(8,128)S(1)}, f32[3,8,8,256]{3,2,1,0:T(8,128)}, u32[]{:S(2)}) copy-start(f32[3,8,8,256]{3,2,1,0:T(8,128)} %sol.1) | copy-start | bytes 589828
  44.7 12.6 %all-to-all-start = ((f32[32,1,128]{2,1,0:T(1,128)}), f32[32,1,128]{2,1,0:T(1,128)S(1)}, u32[]{:S(2)}, u32[]{:S(2)}) async-start(f32[32,1,128]{2,1,0:T(1,128)} %bitcast.2), calls=%async_computation | async-start | bytes 32768 | tf_op jit(solution)/shard_map/all_to_all | solution.py:936

commit v7 on v6

--- a/solution.py
+++ b/solution.py
@@ -194,15 +194,11 @@
 
 
 def dot_exact_weights(a, b):
-    b = b.astype(jnp.bfloat16)
-    total = None
-    for k in range(3):
-        part = a.astype(jnp.bfloat16)
-        found = jnp.dot(part, b, preferred_element_type=F32)
-        total = found if total is None else total + found
-        if k < 2:
-            a = a - part.astype(F32)
-    return total
+    high = a.astype(jnp.bfloat16)
+    low = (a - high.astype(F32)).astype(jnp.bfloat16)
+    both = jnp.concatenate([high, low], axis=0)
+    found = jnp.dot(both, b.astype(jnp.bfloat16), preferred_element_type=F32)
+    return found[: a.shape[0]] + found[a.shape[0] :]
 
 
 X_PACK = COMPS * RIM + WIDE
@@ -463,7 +459,7 @@
         to_pool[pl.ds(start + 8, 8)] = side + up(side, 4)
         return carry
 
-    lax.fori_loop(0, E_PLANES // 2, shift, 0, unroll=5)
+    lax.fori_loop(0, E_PLANES // 2, shift, 0, unroll=True)
 
     def prepare(k, carry):
         for i in (2 * k, 2 * k + 1):
@@ -718,7 +714,7 @@
             es2[c, i] = e[0, i] * value
         return carry
 
-    lax.fori_loop(1, PLANES - 1, add_up, 0, unroll=2)
+    lax.fori_loop(1, PLANES - 1, add_up, 0, unroll=True)
     sweep(s2, es2, s3, es3, s0, c1, e, w, 2, PLANES - 2)
     sweep(s3, es3, p, ep, s0, c1, e, w, 3, PLANES - 3)
 
@@ -761,7 +757,7 @@
     sums[...] = jnp.broadcast_to(jnp.sum(total, axis=0, keepdims=True), sums.shape)
 
 
-STEP = 2
+STEP = 4
 
 
 def last_body(

time: 58.7 us -> 58 us (0.988)
  Pallas kernels: 11.2 us -> 10.5 us
where the time goes in v7:
time: 58 us; the launch traced here: 57.8 us
  starting transfers between devices  25.3 us (44%)
  waiting for transfers between devices  20.6 us (36%)
  Pallas kernels  10.5 us (18%)
  between operations  1.4 us (2%)
    ppermute x6, starting transfers between devices, swap(): got_even = lax.ppermute(even_pack, axis, pairs(count, False, closed))  11 us
    ppermute x6, waiting for transfers between devices, swap(): got_even = lax.ppermute(even_pack, axis, pairs(count, False, closed))  7.31 us
    all_to_all x1, waiting for transfers between devices, on_device(): sums = lax.all_to_all(sums, ALL, 0, 0, tiled=True)  6.42 us
    ppermute x4, waiting for transfers between devices, swap(): return [got_even, lax.ppermute(odd_pack, axis, pairs(count, True, closed))]  6.09 us
    all_to_all x1, starting transfers between devices, on_device(): sums = lax.all_to_all(sums, ALL, 0, 0, tiled=True)  5.53 us
    ppermute x2, starting transfers between devices, swap_yz(): found.append(lax.ppermute(packs[odd_z], ('gy', 'gz'), made))  5.15 us
    pallas_call x1, Pallas kernels, on_device(): smooth_call(n_z)(res, young, *got_x, *got_y, *got_z, *corners)  3.83 us
    pallas_call x1, Pallas kernels, on_device(): finish_call(n_all)  3.82 us
  transfers between devices with their start and end apart: 13, of which 8 were waited for; matrix products, arithmetic and copies ran while one was open for 0% of the time, Pallas kernels for 0%

profile of v7, /device:TPU:0, one launch (start us, length us, event | category | flops | bytes accessed | tf_op | source)
XLA Modules:
  0.0 57.8 jit_solution(13546307996030639706)
XLA Ops:
  0.6 1.1 %shard_map.111 = (f32[3,8,8,256]{3,2,1,0:T(8,128)S(1)}, f32[8,8,256]{2,1,0:T(8,128)S(1)}, f32[18,8,256]{2,1,0:T(8,128)S(1)}, f32[18,8,256]{2,1,0:T(8,128)S(1)}) custom-call(f32[16]{0:T(128)} %table_in.1, s32[8,8,256]{2,1,0:T(8,128)} %index_in.1, f32[3,8,8,256]{3,2,1,0:T(8,128)} %res.3), custom_call_target="tpu_custom_call" | custom-call | tf_op jit(solution)/shard_map/pallas_call | solution.py:870
  1.7 3.0 %collective-permute-start = (f32[18,8,256]{2,1,0:T(8,128)S(1)}, f32[18,8,256]{2,1,0:T(8,128)S(1)}, u32[]{:S(2)}, u32[]{:S(2)}) collective-permute-start(f32[18,8,256]{2,1,0:T(8,128)S(1)} %get-tuple-element.36), channel_id=1, source_target_pairs={{0,8},{8,0},{16,24},{24,16},{1,9},{9,1},{17,25},{25,17},{2,10},{10... | collective-permute-start | bytes 442376 | tf_op jit(solution)/shard_map/ppermute | solution.py:59
  4.7 1.5 %collective-permute-start.1 = (f32[18,8,256]{2,1,0:T(8,128)S(1)}, f32[18,8,256]{2,1,0:T(8,128)S(1)}, u32[]{:S(2)}, u32[]{:S(2)}) collective-permute-start(f32[18,8,256]{2,1,0:T(8,128)S(1)} %get-tuple-element.37), channel_id=1, source_target_pairs={{0,24},{8,16},{16,8},{24,0},{1,25},{9,17},{17,9},{25,1},{2,26},{10... | collective-permute-start | bytes 442376 | tf_op jit(solution)/shard_map/ppermute | solution.py:62
  6.2 3.0 %collective-permute-done.got_a.refs_2_ = f32[18,8,256]{2,1,0:T(8,128)S(1)} collective-permute-done((f32[18,8,256]{2,1,0:T(8,128)S(1)}, f32[18,8,256]{2,1,0:T(8,128)S(1)}, u32[]{:S(2)}, u32[]{:S(2)}) %collective-permute-start) | collective-permute-done | bytes 147488 | tf_op jit(solution)/shard_map/ppermute | solution.py:59
  9.2 3.7 %collective-permute-done.1.got_b.refs_3_ = f32[18,8,256]{2,1,0:T(8,128)S(1)} collective-permute-done((f32[18,8,256]{2,1,0:T(8,128)S(1)}, f32[18,8,256]{2,1,0:T(8,128)S(1)}, u32[]{:S(2)}, u32[]{:S(2)}) %collective-permute-start.1) | collective-permute-done | bytes 147488 | tf_op jit(solution)/shard_map/ppermute | solution.py:62
  12.9 0.1 shard_map.112
  13.0 1.6 %collective-permute-start.2 = (f32[39,8,256]{2,1,0:T(8,128)S(1)}, f32[39,8,256]{2,1,0:T(8,128)S(1)}, u32[]{:S(2)}, u32[]{:S(2)}) collective-permute-start(f32[39,8,256]{2,1,0:T(8,128)S(1)} %get-tuple-element.38.sent_even), channel_id=1, source_target_pairs={{0,2},{2,0},{4,6},{6,4},{1,3},{3,1},{5,7},{7,5},{8,10},{10,8},{12,... | collective-permute-start | bytes 958472 | tf_op jit(solution)/shard_map/ppermute | solution.py:59
  14.7 0.8 %collective-permute-start.3 = (f32[39,8,256]{2,1,0:T(8,128)S(1)}, f32[39,8,256]{2,1,0:T(8,128)S(1)}, u32[]{:S(2)}, u32[]{:S(2)}) collective-permute-start(f32[39,8,256]{2,1,0:T(8,128)S(1)} %get-tuple-element.39.sent_odd), channel_id=1, source_target_pairs={{2,4},{4,2},{3,5},{5,3},{10,12},{12,10},{11,13},{13,11},{18,20},{2... | collective-permute-start | bytes 958472 | tf_op jit(solution)/shard_map/ppermute | solution.py:62
  15.5 0.2 shard_map.113
  15.7 0.1 collective-permute-start.4
  15.8 4.5 %collective-permute-start.5 = (f32[24,128]{1,0:T(8,128)S(1)}, f32[24,128]{1,0:T(8,128)S(1)}, u32[]{:S(2)}, u32[]{:S(2)}) collective-permute-start(f32[24,128]{1,0:T(8,128)S(1)} %get-tuple-element.41), channel_id=1, source_target_pairs={{0,3},{1,2},{2,1},{3,0},{4,7},{5,6},{6,5},{7,4},{8,11},{9,10},{10,... | collective-permute-start | bytes 36872 | tf_op jit(solution)/shard_map/ppermute | solution.py:77
  20.3 0.7 %collective-permute-start.6 = (f32[24,128]{1,0:T(8,128)S(1)}, f32[24,128]{1,0:T(8,128)S(1)}, u32[]{:S(2)}, u32[]{:S(2)}) collective-permute-start(f32[24,128]{1,0:T(8,128)S(1)} %get-tuple-element.42), channel_id=1, source_target_pairs={{2,5},{3,4},{4,3},{5,2},{10,13},{11,12},{12,11},{13,10},{18,21},{1... | collective-permute-start | bytes 36872 | tf_op jit(solution)/shard_map/ppermute | solution.py:77
  21.0 0.7 %collective-permute-done.5.refs_7_ = f32[24,128]{1,0:T(8,128)S(1)} collective-permute-done((f32[24,128]{1,0:T(8,128)S(1)}, f32[24,128]{1,0:T(8,128)S(1)}, u32[]{:S(2)}, u32[]{:S(2)}) %collective-permute-start.5) | collective-permute-done | bytes 12320 | tf_op jit(solution)/shard_map/ppermute | solution.py:77
  21.7 0.0 collective-permute-done.6.refs_8_
  21.7 0.0 collective-permute-done.4.refs_6_
  21.7 3.8 %shard_map.114 = (f32[3,16,16,384]{3,2,1,0:T(8,128)S(1)}, f32[3,16,16,384]{3,2,1,0:T(8,128)S(1)}, f32[3,20,16,384]{3,2,1,0:T(8,128)S(1)}, f32[16,16,384]{2,1,0:T...) custom-call(f32[3,8,8,256]{3,2,1,0:T(8,128)S(1)} %get-tuple-element., ...), custom_call_target="tpu_custom_call" | custom-call | tf_op jit(solution)/shard_map/pallas_call | solution.py:895
  25.6 0.1 collective-permute-start.7
  25.7 1.2 %collective-permute-done.7.refs_1_ = f32[104,128]{1,0:T(8,128)S(1)} collective-permute-done((f32[104,128]{1,0:T(8,128)S(1)}, f32[104,128]{1,0:T(8,128)S(1)}, u32[]{:S(2)}, u32[]{:S(2)}) %collective-permute-start.7) | collective-permute-done | bytes 53280 | tf_op jit(solution)/shard_map/ppermute | solution.py:59
  26.9 0.2 shard_map.115
  27.1 1.5 %collective-permute-start.8 = (f32[48,128]{1,0:T(8,128)S(1)}, f32[48,128]{1,0:T(8,128)S(1)}, u32[]{:S(2)}, u32[]{:S(2)}) collective-permute-start(f32[48,128]{1,0:T(8,128)S(1)} %get-tuple-element.46), channel_id=1, source_target_pairs={{0,8},{8,0},{16,24},{24,16},{1,9},{9,1},{17,25},{25,17},{2,10},{10... | collective-permute-start | bytes 73736 | tf_op jit(solution)/shard_map/ppermute | solution.py:59
  28.6 0.6 %collective-permute-start.9 = (f32[48,128]{1,0:T(8,128)S(1)}, f32[48,128]{1,0:T(8,128)S(1)}, u32[]{:S(2)}, u32[]{:S(2)}) collective-permute-start(f32[48,128]{1,0:T(8,128)S(1)} %get-tuple-element.47), channel_id=1, source_target_pairs={{0,24},{8,16},{16,8},{24,0},{1,25},{9,17},{17,9},{25,1},{2,26},{10... | collective-permute-start | bytes 73736 | tf_op jit(solution)/shard_map/ppermute | solution.py:62
  29.3 1.7 %collective-permute-done.8.got_a = f32[48,128]{1,0:T(8,128)S(1)} collective-permute-done((f32[48,128]{1,0:T(8,128)S(1)}, f32[48,128]{1,0:T(8,128)S(1)}, u32[]{:S(2)}, u32[]{:S(2)}) %collective-permute-start.8) | collective-permute-done | bytes 24608 | tf_op jit(solution)/shard_map/ppermute | solution.py:59
  31.0 2.4 %collective-permute-done.9.got_b = f32[48,128]{1,0:T(8,128)S(1)} collective-permute-done((f32[48,128]{1,0:T(8,128)S(1)}, f32[48,128]{1,0:T(8,128)S(1)}, u32[]{:S(2)}, u32[]{:S(2)}) %collective-permute-start.9) | collective-permute-done | bytes 24608 | tf_op jit(solution)/shard_map/ppermute | solution.py:62
  33.4 0.2 shard_map.116
  33.5 4.7 %collective-permute-start.10 = (f32[96,128]{1,0:T(8,128)S(1)}, f32[96,128]{1,0:T(8,128)S(1)}, u32[]{:S(2)}, u32[]{:S(2)}) collective-permute-start(f32[96,128]{1,0:T(8,128)S(1)} %get-tuple-element.50), channel_id=1, source_target_pairs={{0,2},{2,0},{4,6},{6,4},{1,3},{3,1},{5,7},{7,5},{8,10},{10,8},{12,... | collective-permute-start | bytes 147464 | tf_op jit(solution)/shard_map/ppermute | solution.py:59
  38.2 0.7 %collective-permute-start.11 = (f32[96,128]{1,0:T(8,128)S(1)}, f32[96,128]{1,0:T(8,128)S(1)}, u32[]{:S(2)}, u32[]{:S(2)}) collective-permute-start(f32[96,128]{1,0:T(8,128)S(1)} %get-tuple-element.51), channel_id=1, source_target_pairs={{2,4},{4,2},{3,5},{5,3},{10,12},{12,10},{11,13},{13,11},{18,20},{2... | collective-permute-start | bytes 147464 | tf_op jit(solution)/shard_map/ppermute | solution.py:62
  38.9 1.4 %collective-permute-done.10.got_a = f32[96,128]{1,0:T(8,128)S(1)} collective-permute-done((f32[96,128]{1,0:T(8,128)S(1)}, f32[96,128]{1,0:T(8,128)S(1)}, u32[]{:S(2)}, u32[]{:S(2)}) %collective-permute-start.10) | collective-permute-done | bytes 49184 | tf_op jit(solution)/shard_map/ppermute | solution.py:59
  40.3 0.0 copy-start.3
  40.3 3.8 %shard_map.117 = (f32[8,3,2,8,128]{4,3,2,1,0:T(8,128)S(1)}, f32[8,3,2,8,128]{4,3,2,1,0:T(8,128)S(1)}, f32[32,128]{1,0:T(8,128)}) custom-call(f32[24,8,256]{2,1,0:T(8,128)S(1)} %get-tuple-element.48.wide_planes, f32[40,256]{1,0:T(8,128)S(1)} %get-tuple-element.49.columns, f32[96,128]{1,0:T(8,128)S(1)} %collective-permute-done.10.got_a, ...), custom_call_target="tpu_custom_call" | custom-call | tf_op jit(solution)/shard_map/pallas_call | solution.py:927
  44.1 5.5 %all-to-all-start = ((f32[32,1,128]{2,1,0:T(1,128)}), f32[32,1,128]{2,1,0:T(1,128)S(1)}, u32[]{:S(2)}, u32[]{:S(2)}) async-start(f32[32,1,128]{2,1,0:T(1,128)} %bitcast.2), calls=%async_computation | async-start | bytes 32768 | tf_op jit(solution)/shard_map/all_to_all | solution.py:932
  50.3 6.4 %all-to-all-done = f32[32,1,128]{2,1,0:T(1,128)S(1)} async-done(((f32[32,1,128]{2,1,0:T(1,128)}), f32[32,1,128]{2,1,0:T(1,128)S(1)}, u32[]{:S(2)}, u32[]{:S(2)}) %all-to-all-start) | async-done | bytes 16416 | tf_op jit(solution)/shard_map/all_to_all | solution.py:932
  56.7 1.1 %shard_map.118 = (f32[3,8,8,256]{3,2,1,0:T(8,128)}, f32[3,8,8,256]{3,2,1,0:T(8,128)}, f32[3,8,8,256]{3,2,1,0:T(8,128)}, f32[3,8,8,256]{3,2,1,0:T(8,128)}) custom-call(f32[1]{0:T(128)} %bitcast.5.prev_rz, f32[32,128]{1,0:T(8,128)S(1)} %bitcast.6, f32[8,3,2,8,128]{4,3,2,1,0:T(8,128)S(1)} %get-tuple-element.62.precond, ...), custom_call_target="tpu_custom_call" | custom-call | tf_op jit(solution)/shard_map/pallas_call | solution.py:934
  (12 shorter events, 0.0 us)
Async XLA Ops:
  1.7 7.5 %collective-permute-start = (f32[18,8,256]{2,1,0:T(8,128)S(1)}, f32[18,8,256]{2,1,0:T(8,128)S(1)}, u32[]{:S(2)}, u32[]{:S(2)}) collective-permute-start(f32[18,8,256]{2,1,0:T(8,128)S(1)} %get-tuple-element.36), channel_id=1, source_target_pairs={{0,8},{8,0},{16,24},{24,16},{1,9},{9,1},{17,25},{25,17},{2,10},{10... | collective-permute-start | bytes 442376 | tf_op jit(solution)/shard_map/ppermute | solution.py:59
  4.7 8.2 %collective-permute-start.1 = (f32[18,8,256]{2,1,0:T(8,128)S(1)}, f32[18,8,256]{2,1,0:T(8,128)S(1)}, u32[]{:S(2)}, u32[]{:S(2)}) collective-permute-start(f32[18,8,256]{2,1,0:T(8,128)S(1)} %get-tuple-element.37), channel_id=1, source_target_pairs={{0,24},{8,16},{16,8},{24,0},{1,25},{9,17},{17,9},{25,1},{2,26},{10... | collective-permute-start | bytes 442376 | tf_op jit(solution)/shard_map/ppermute | solution.py:62
  13.0 8.7 %collective-permute-start.2 = (f32[39,8,256]{2,1,0:T(8,128)S(1)}, f32[39,8,256]{2,1,0:T(8,128)S(1)}, u32[]{:S(2)}, u32[]{:S(2)}) collective-permute-start(f32[39,8,256]{2,1,0:T(8,128)S(1)} %get-tuple-element.38.sent_even), channel_id=1, source_target_pairs={{0,2},{2,0},{4,6},{6,4},{1,3},{3,1},{5,7},{7,5},{8,10},{10,8},{12,... | collective-permute-start | bytes 958472 | tf_op jit(solution)/shard_map/ppermute | solution.py:59
  14.7 12.2 %copy-start.4 = (f32[1,1,48,48]{3,2,1,0:T(8,128)S(1)}, f32[1,1,48,48]{3,2,1,0:T(8,128)}, u32[]{:S(2)}) copy-start(f32[1,1,48,48]{3,2,1,0:T(8,128)} %refs_2_.1) | copy-start | bytes 27652
  14.7 25.6 %copy-start = (f32[3,8,8,256]{3,2,1,0:T(8,128)S(1)}, f32[3,8,8,256]{3,2,1,0:T(8,128)}, u32[]{:S(2)}) copy-start(f32[3,8,8,256]{3,2,1,0:T(8,128)} %res.3) | copy-start | bytes 589828
  14.7 25.6 %copy-start.1 = (f32[3,8,8,256]{3,2,1,0:T(8,128)S(1)}, f32[3,8,8,256]{3,2,1,0:T(8,128)}, u32[]{:S(2)}) copy-start(f32[3,8,8,256]{3,2,1,0:T(8,128)} %prev_d.3) | copy-start | bytes 589828
  14.7 25.6 %copy-start.2 = (f32[3,8,8,256]{3,2,1,0:T(8,128)S(1)}, f32[3,8,8,256]{3,2,1,0:T(8,128)}, u32[]{:S(2)}) copy-start(f32[3,8,8,256]{3,2,1,0:T(8,128)} %prev_i.3) | copy-start | bytes 589828
  14.7 7.1 %collective-permute-start.3 = (f32[39,8,256]{2,1,0:T(8,128)S(1)}, f32[39,8,256]{2,1,0:T(8,128)S(1)}, u32[]{:S(2)}, u32[]{:S(2)}) collective-permute-start(f32[39,8,256]{2,1,0:T(8,128)S(1)} %get-tuple-element.39.sent_odd), channel_id=1, source_target_pairs={{2,4},{4,2},{3,5},{5,3},{10,12},{12,10},{11,13},{13,11},{18,20},{2... | collective-permute-start | bytes 958472 | tf_op jit(solution)/shard_map/ppermute | solution.py:62
  15.7 6.0 %collective-permute-start.4 = (f32[40,128]{1,0:T(8,128)S(1)}, f32[40,128]{1,0:T(8,128)S(1)}, u32[]{:S(2)}, u32[]{:S(2)}) collective-permute-start(f32[40,128]{1,0:T(8,128)S(1)} %get-tuple-element.40), channel_id=1, source_target_pairs={{0,1},{1,0},{2,3},{3,2},{4,5},{5,4},{6,7},{7,6},{8,9},{9,8},{10,11... | collective-permute-start | bytes 61448 | tf_op jit(solution)/shard_map/ppermute | solution.py:59
  15.8 5.9 %collective-permute-start.5 = (f32[24,128]{1,0:T(8,128)S(1)}, f32[24,128]{1,0:T(8,128)S(1)}, u32[]{:S(2)}, u32[]{:S(2)}) collective-permute-start(f32[24,128]{1,0:T(8,128)S(1)} %get-tuple-element.41), channel_id=1, source_target_pairs={{0,3},{1,2},{2,1},{3,0},{4,7},{5,6},{6,5},{7,4},{8,11},{9,10},{10,... | collective-permute-start | bytes 36872 | tf_op jit(solution)/shard_map/ppermute | solution.py:77
  20.3 1.4 %collective-permute-start.6 = (f32[24,128]{1,0:T(8,128)S(1)}, f32[24,128]{1,0:T(8,128)S(1)}, u32[]{:S(2)}, u32[]{:S(2)}) collective-permute-start(f32[24,128]{1,0:T(8,128)S(1)} %get-tuple-element.42), channel_id=1, source_target_pairs={{2,5},{3,4},{4,3},{5,2},{10,13},{11,12},{12,11},{13,10},{18,21},{1... | collective-permute-start | bytes 36872 | tf_op jit(solution)/shard_map/ppermute | solution.py:77
  25.6 1.3 %collective-permute-start.7 = (f32[104,128]{1,0:T(8,128)S(1)}, f32[104,128]{1,0:T(8,128)S(1)}, u32[]{:S(2)}, u32[]{:S(2)}) collective-permute-start(f32[104,128]{1,0:T(8,128)S(1)} %get-tuple-element.43.refs_0_), channel_id=1, source_target_pairs={{0,1},{1,0},{2,3},{3,2},{4,5},{5,4},{6,7},{7,6},{8,9},{9,8},{10,11... | collective-permute-start | bytes 159752 | tf_op jit(solution)/shard_map/ppermute | solution.py:59
  27.1 3.8 %collective-permute-start.8 = (f32[48,128]{1,0:T(8,128)S(1)}, f32[48,128]{1,0:T(8,128)S(1)}, u32[]{:S(2)}, u32[]{:S(2)}) collective-permute-start(f32[48,128]{1,0:T(8,128)S(1)} %get-tuple-element.46), channel_id=1, source_target_pairs={{0,8},{8,0},{16,24},{24,16},{1,9},{9,1},{17,25},{25,17},{2,10},{10... | collective-permute-start | bytes 73736 | tf_op jit(solution)/shard_map/ppermute | solution.py:59
  28.6 4.7 %collective-permute-start.9 = (f32[48,128]{1,0:T(8,128)S(1)}, f32[48,128]{1,0:T(8,128)S(1)}, u32[]{:S(2)}, u32[]{:S(2)}) collective-permute-start(f32[48,128]{1,0:T(8,128)S(1)} %get-tuple-element.47), channel_id=1, source_target_pairs={{0,24},{8,16},{16,8},{24,0},{1,25},{9,17},{17,9},{25,1},{2,26},{10... | collective-permute-start | bytes 73736 | tf_op jit(solution)/shard_map/ppermute | solution.py:62
  33.5 6.7 %collective-permute-start.10 = (f32[96,128]{1,0:T(8,128)S(1)}, f32[96,128]{1,0:T(8,128)S(1)}, u32[]{:S(2)}, u32[]{:S(2)}) collective-permute-start(f32[96,128]{1,0:T(8,128)S(1)} %get-tuple-element.50), channel_id=1, source_target_pairs={{0,2},{2,0},{4,6},{6,4},{1,3},{3,1},{5,7},{7,5},{8,10},{10,8},{12,... | collective-permute-start | bytes 147464 | tf_op jit(solution)/shard_map/ppermute | solution.py:59
  38.2 2.1 %collective-permute-start.11 = (f32[96,128]{1,0:T(8,128)S(1)}, f32[96,128]{1,0:T(8,128)S(1)}, u32[]{:S(2)}, u32[]{:S(2)}) collective-permute-start(f32[96,128]{1,0:T(8,128)S(1)} %get-tuple-element.51), channel_id=1, source_target_pairs={{2,4},{4,2},{3,5},{5,3},{10,12},{12,10},{11,13},{13,11},{18,20},{2... | collective-permute-start | bytes 147464 | tf_op jit(solution)/shard_map/ppermute | solution.py:62
  40.3 16.4 %copy-start.3 = (f32[3,8,8,256]{3,2,1,0:T(8,128)S(1)}, f32[3,8,8,256]{3,2,1,0:T(8,128)}, u32[]{:S(2)}) copy-start(f32[3,8,8,256]{3,2,1,0:T(8,128)} %sol.1) | copy-start | bytes 589828
  44.1 12.6 %all-to-all-start = ((f32[32,1,128]{2,1,0:T(1,128)}), f32[32,1,128]{2,1,0:T(1,128)S(1)}, u32[]{:S(2)}, u32[]{:S(2)}) async-start(f32[32,1,128]{2,1,0:T(1,128)} %bitcast.2), calls=%async_computation | async-start | bytes 32768 | tf_op jit(solution)/shard_map/all_to_all | solution.py:932
